TPU v7x, 128 devices: a whole 4x4x4 slice. The times are simulated.
128 devices in a mesh: nodes: 32 (over y, x, core), hid: 4 (over z).
Axes of the slice: x: 4, y: 4, z: 4, core: 2. Of those that a mesh axis runs over, the one named last changes fastest.
Arguments:
- node_features: bfloat16 [32768, 512], P('nodes', 'hid'), may hold values from -6 to 6
- w_out: bfloat16 [512, 512], P(None, 'hid'), may hold values from -0.25 to 0.25
- w_in: bfloat16 [512, 512], P(None, 'hid'), may hold values from -0.25 to 0.25
- w_self: bfloat16 [512, 512], P(None, 'hid'), may hold values from -0.25 to 0.25
- cotangent: bfloat16 [32768, 512], P('nodes', 'hid'), may hold values from -6 to 6
- tile_src: int32 [8192], P('nodes'), may hold values from 0 to 255, as said below
- tile_dst: int32 [8192], P('nodes'), may hold values from 0 to 255, as said below
- tile_pattern: int32 [8192, 128, 128], P('nodes'), may hold values 0 or 1
- tile_count: int32 [32], P('nodes'), may hold values from 64 to 256, as said below
Outputs:
- hidden: bfloat16 [32768, 512], P('nodes', 'hid')
- grad_input: bfloat16 [32768, 512], P('nodes', 'hid')
- grad_w_out: float32 [512, 512], P('nodes', 'hid')
- grad_w_in: float32 [512, 512], P('nodes', 'hid')
- grad_w_self: float32 [512, 512], P('nodes', 'hid')
Inputs may be any that keep to these rules, and one draw needn't show every extreme that they name: `tile_src`: every slot of device d names a source row block of device d itself, that is d * 8 to d * 8 + 7. `tile_dst`: among the used slots of device d, at most 2 have a destination block held by any one other device, and exactly 2 for each of the devices just before and just after d along nodes, taken cyclically. `tile_count`: some device uses all 256 slots.
All inputs are finite; a program needn't handle non-finite values. No bound on the sum of `tile_pattern` on one device may be relied on, other than what follows from the above.
Results may differ from a plain program's by a relative error of at most 0.0055.
Values may be sent and summed in bfloat16 or wider, within the bound.
No kernel may reach another device: no remote copies, remote signals or barrier semaphores. Data moves between devices by JAX's collectives and lax.ppermute only.
A program may use at most 128 MiB of HBM per device.

v0:
```python
import jax
import jax.numpy as jnp
from jax import lax
from jax.sharding import PartitionSpec as P

CAP = 2


def shards(
    node_features, w_out, w_in, w_self, cotangent, tile_src, tile_dst, tile_pattern, tile_count
):
    nodes_size = lax.axis_size("nodes")
    myself = lax.axis_index("nodes")
    block_rows = tile_pattern.shape[1]
    slivers = node_features.shape[1]
    node_rows = node_features.shape[0]
    local_blocks = node_rows // block_rows
    tile_slots = tile_src.shape[0]
    tile_total = tile_count[0]
    slot_ids = jnp.arange(tile_slots, dtype=jnp.int32)
    is_valid = slot_ids < tile_total
    src_local = jnp.clip(tile_src - myself * local_blocks, 0, local_blocks - 1)
    owner_dev = tile_dst // local_blocks
    dst_local = jnp.clip(tile_dst - owner_dev * local_blocks, 0, local_blocks - 1)
    remote = is_valid & (owner_dev != myself)
    earlier = (
        (owner_dev[:, None] == owner_dev[None, :])
        & remote[None, :]
        & (slot_ids[None, :] < slot_ids[:, None])
    )
    slot_rank = jnp.sum(earlier.astype(jnp.int32), axis=1)
    slot_place = jnp.where(remote, owner_dev * CAP + slot_rank, -1)
    buffer_slots = nodes_size * CAP
    slot_grid = jnp.arange(buffer_slots, dtype=jnp.int32)
    wanted = (
        jnp.sum(
            jnp.where(slot_place[None, :] == slot_grid[:, None], dst_local[None, :] + 1, 0), axis=1
        )
        - 1
    )
    requested = lax.all_to_all(
        wanted.reshape(nodes_size, CAP), "nodes", split_axis=0, concat_axis=0, tiled=True
    ).reshape(-1)
    land_index = jnp.where(requested >= 0, requested, local_blocks)

    def fetch(feature):
        gathered = lax.all_gather(feature, "nodes", axis=0, tiled=True)
        source = gathered.reshape(-1, block_rows, slivers)
        row_index = jnp.clip(tile_dst, 0, nodes_size * local_blocks - 1)
        return (source, row_index)

    def aggregate(push_feat, source, row_index):
        push_blocks = push_feat.reshape(local_blocks, block_rows, slivers)
        tile_group = 32
        turns = (tile_total + tile_group - 1) // tile_group

        def advance(turn_index, running):
            out_acc, in_acc, outgoing = running
            first_tile = turn_index * tile_group

            def take_turn(values):
                return lax.dynamic_slice_in_dim(values, first_tile, tile_group, 0)

            usable = take_turn(is_valid)
            weights = jnp.where(usable[:, None, None], take_turn(tile_pattern), 0).astype(
                jnp.bfloat16
            )
            sources_here = take_turn(src_local)
            pulled = source[take_turn(row_index)]
            mine_rows = push_blocks[sources_here]
            out_part = jnp.einsum(
                "tij,tjk->tik", weights, pulled, preferred_element_type=jnp.float32
            )
            in_part = jnp.einsum(
                "tji,tjk->tik", weights, mine_rows, preferred_element_type=jnp.float32
            )
            out_index = jnp.where(usable, sources_here, local_blocks)
            home_mask = usable & jnp.logical_not(take_turn(remote))
            home_index = jnp.where(home_mask, take_turn(dst_local), local_blocks)
            away_index = jnp.where(usable & take_turn(remote), take_turn(slot_place), buffer_slots)
            out_acc = out_acc.at[out_index].add(out_part, mode="drop")
            in_acc = in_acc.at[home_index].add(in_part, mode="drop")
            outgoing = outgoing.at[away_index].add(in_part, mode="drop")
            return (out_acc, in_acc, outgoing)

        block_zeros = jnp.zeros((local_blocks, block_rows, slivers), jnp.float32)
        slot_zeros = jnp.zeros((buffer_slots, block_rows, slivers), jnp.float32)
        return lax.fori_loop(0, turns, advance, (block_zeros, block_zeros, slot_zeros))

    def deliver(outgoing):
        incoming = lax.all_to_all(
            outgoing.reshape(nodes_size, CAP, block_rows, slivers),
            "nodes",
            split_axis=0,
            concat_axis=0,
            tiled=True,
        )
        landed = jnp.zeros((local_blocks, block_rows, slivers), jnp.float32)
        return landed.at[land_index].add(incoming.reshape(-1, block_rows, slivers), mode="drop")

    source, row_index = fetch(node_features)
    out_acc, in_acc, outgoing = aggregate(node_features, source, row_index)
    in_acc = in_acc + deliver(outgoing)
    prop_out = out_acc.reshape(node_rows, slivers).astype(jnp.bfloat16)
    prop_in = in_acc.reshape(node_rows, slivers).astype(jnp.bfloat16)
    full_out, full_in, full_self = (
        lax.all_gather(prop_out, "hid", axis=1, tiled=True),
        lax.all_gather(prop_in, "hid", axis=1, tiled=True),
        lax.all_gather(node_features, "hid", axis=1, tiled=True),
    )
    pre_act = (
        jnp.dot(full_out, w_out, preferred_element_type=jnp.float32)
        + jnp.dot(full_in, w_in, preferred_element_type=jnp.float32)
    ) / 32.0
    pre_act = pre_act + jnp.dot(full_self, w_self, preferred_element_type=jnp.float32)
    hidden = jax.nn.silu(pre_act).astype(jnp.bfloat16)
    sigmoid_z = jax.nn.sigmoid(pre_act)
    grad_z = (
        cotangent.astype(jnp.float32) * sigmoid_z * (1.0 + pre_act * (1.0 - sigmoid_z))
    ).astype(jnp.bfloat16)
    term_out = jnp.einsum("nk,nj->kj", full_out, grad_z, preferred_element_type=jnp.float32) / 32.0
    term_in = jnp.einsum("nk,nj->kj", full_in, grad_z, preferred_element_type=jnp.float32) / 32.0
    term_self = jnp.einsum("nk,nj->kj", full_self, grad_z, preferred_element_type=jnp.float32)
    weight_grads = lax.psum_scatter(
        jnp.concatenate([term_out, term_in, term_self], axis=1),
        "nodes",
        scatter_dimension=0,
        tiled=True,
    )
    grad_w_out = weight_grads[:, :slivers]
    grad_w_in = weight_grads[:, slivers : 2 * slivers]
    grad_w_self = weight_grads[:, 2 * slivers :]
    sum_out = jnp.einsum("nj,dj->nd", grad_z, w_out, preferred_element_type=jnp.float32)
    sum_in = jnp.einsum("nj,dj->nd", grad_z, w_in, preferred_element_type=jnp.float32)
    sum_self = jnp.einsum("nj,dj->nd", grad_z, w_self, preferred_element_type=jnp.float32)
    part_out, part_in, grad_self = (
        lax.psum_scatter(sum_out, "hid", scatter_dimension=1, tiled=True),
        lax.psum_scatter(sum_in, "hid", scatter_dimension=1, tiled=True),
        lax.psum_scatter(sum_self, "hid", scatter_dimension=1, tiled=True),
    )
    back_out = (part_out / 32.0).astype(jnp.bfloat16)
    back_in = (part_in / 32.0).astype(jnp.bfloat16)
    source, row_index = fetch(back_in)
    from_in, from_out, outgoing = aggregate(back_out, source, row_index)
    from_out = from_out + deliver(outgoing)
    grad_input = (
        grad_self + from_in.reshape(node_rows, slivers) + from_out.reshape(node_rows, slivers)
    ).astype(jnp.bfloat16)
    return (hidden, grad_input, grad_w_out, grad_w_in, grad_w_self)


def solution(mesh):
    in_specs = (
        P("nodes", "hid"),
        P(None, "hid"),
        P(None, "hid"),
        P(None, "hid"),
        P("nodes", "hid"),
        P("nodes"),
        P("nodes"),
        P("nodes", None, None),
        P("nodes"),
    )
    out_specs = (
        P("nodes", "hid"),
        P("nodes", "hid"),
        P("nodes", "hid"),
        P("nodes", "hid"),
        P("nodes", "hid"),
    )
    return jax.shard_map(shards, mesh=mesh, in_specs=in_specs, out_specs=out_specs, check_vma=False)
```

profile of v0, /device:TPU:0, one launch (start us, length us, event | category | flops | bytes accessed | tf_op | source)
XLA Modules:
  0.0 810.5 jit_solution(947790978854955295)
XLA Ops:
  12.1 7.5 all-to-all-start
  19.7 17.5 %copy.38 = s32[256,128,128]{1,2,0:T(8,128)} copy(s32[256,128,128]{2,1,0:T(8,128)} %param.20) | data formatting | bytes 33554432 | tf_op jit(solution)/shard_map/while | solution.py:88
  37.8 27.8 %all-gather.6.cloned.1.call-done = bf16[32768,128]{1,0:T(8,128)(2,1)} async-done(((bf16[1024,128]{1,0:T(8,128)(2,1)}), bf16[32768,128]{1,0:T(8,128)(2,1)}) %all-gather.6.cloned.1.call-update) | async-done | bytes 8388624 | tf_op jit(solution)/shard_map/all_gather | solution.py:47
  65.5 2.5 broadcast.98.clone
  68.1 79.6 %while.28 = (s32[]{:T(128)}, f32[8,128,128]{2,1,0:T(8,128)S(1)}, f32[8,128,128]{2,1,0:T(8,128)S(1)}, f32[64,128,128]{2,1,0:T(8,128)}, s32[]{:T(128)}, /*index=5*...) while((s32[]{:T(128)}, f32[8,128,128]{2,1,0:T(8,128)S(1)}, ...), condition=%wide.region_5.6_spmd, body=%wide.region_1.5_spmd.sunk | while | flops 272108192 | bytes 33565088 | solution.py:88
  69.5 1.7 gather_fusion.1
  71.3 2.3 fusion.46
  73.6 6.9 scatter_fusion.2
  80.6 2.8 scatter_fusion.1
  84.0 5.1 gather_fusion
  89.1 2.6 fusion.45
  91.7 2.7 scatter_fusion
  95.8 1.7 gather_fusion.1
  97.6 2.3 fusion.46
  99.9 7.0 scatter_fusion.2
  107.0 2.8 scatter_fusion.1
  110.4 5.1 gather_fusion
  115.5 2.6 fusion.45
  118.1 2.7 scatter_fusion
  122.2 1.7 gather_fusion.1
  123.9 2.3 fusion.46
  126.3 7.6 scatter_fusion.2
  133.9 2.8 scatter_fusion.1
  137.3 5.1 gather_fusion
  142.4 2.6 fusion.45
  145.1 2.7 scatter_fusion
  147.7 142.2 %all-to-all-start.1 = ((f32[32,2,128,128]{3,2,1,0:T(8,128)}), f32[32,2,128,128]{3,2,1,0:T(8,128)}, u32[]{:S(2)}, u32[]{:S(2)}) async-start(f32[32,2,128,128]{3,2,1,0:T(8,128)} %bitcast.60), calls=%async_computation.1 | async-start | bytes 8388608 | tf_op jit(solution)/shard_map/all_to_all | solution.py:91
  292.8 50.6 %all-to-all-done.1 = f32[32,2,128,128]{3,2,1,0:T(8,128)} async-done(((f32[32,2,128,128]{3,2,1,0:T(8,128)}), f32[32,2,128,128]{3,2,1,0:T(8,128)}, u32[]{:S(2)}, u32[]{:S(2)}) %all-to-all-start.1) | async-done | bytes 4194336 | tf_op jit(solution)/shard_map/all_to_all | solution.py:91
  343.4 8.8 %scatter_fusion.6 = f32[8,128,128]{2,1,0:T(8,128)S(1)} fusion(f32[8,128,128]{2,1,0:T(8,128)S(1)} %get-tuple-element.156, s32[64]{0:T(128)S(1)} %fusion.7, f32[64,128,128]{2,1,0:T(8,128)} %bitcast.7), kind=kCustom, calls=%fused_computation.10 | custom fusion | flops 1048576 | bytes 12583168 | tf_op jit(solution)/shard_map/scatter-add | solution.py:99
  355.3 20.9 %all-gather.10.cloned.1.call-done = bf16[1024,512]{1,0:T(8,128)(2,1)} async-done(((bf16[1024,128]{1,0:T(8,128)(2,1)}), bf16[1024,512]{1,0:T(8,128)(2,1)}) %all-gather.10.cloned.1.call-update) | async-done | bytes 1048592 | tf_op jit(solution)/shard_map/all_gather | solution.py:108
  377.8 26.8 %all-gather.12.cloned.1.call-done = bf16[1024,512]{1,0:T(8,128)(2,1)} async-done(((bf16[1024,128]{1,0:T(8,128)(2,1)}), bf16[1024,512]{1,0:T(8,128)(2,1)}) %all-gather.12.cloned.1.call-update) | async-done | bytes 1048592 | tf_op jit(solution)/shard_map/all_gather | solution.py:109
  404.6 2.4 multiply_convert_fusion.2
  407.0 1.8 fusion.11
  408.9 1.8 fusion.12
  410.7 28.9 %reduce-scatter.9.cloned.1.call-done = f32[1024,128]{1,0:T(8,128)} async-done(((f32[1024,512]{1,0:T(8,128)}), f32[1024,128]{1,0:T(8,128)}) %reduce-scatter.9.cloned.1.call-update) | async-done | bytes 524304 | tf_op jit(solution)/shard_map/reduce_scatter | solution.py:138
  439.7 1.8 multiply_convert_fusion.1
  443.9 1.8 fusion.10
  445.7 25.9 %reduce-scatter.11.cloned.1.call-done = f32[1024,128]{1,0:T(8,128)} async-done(((f32[1024,512]{1,0:T(8,128)}), f32[1024,128]{1,0:T(8,128)}) %reduce-scatter.11.cloned.1.call-update) | async-done | bytes 524304 | tf_op jit(solution)/shard_map/reduce_scatter | solution.py:137
  472.7 54.1 %all-gather.14.cloned.1.call-done = bf16[32768,128]{1,0:T(8,128)(2,1)} async-done(((bf16[1024,128]{1,0:T(8,128)(2,1)}), bf16[32768,128]{1,0:T(8,128)(2,1)}) %all-gather.14.cloned.1.call-update) | async-done | bytes 8388624 | tf_op jit(solution)/shard_map/all_gather | solution.py:47
  526.8 2.5 broadcast.98
  529.3 75.6 %while.29 = (s32[]{:T(128)}, f32[8,128,128]{2,1,0:T(8,128)S(1)}, f32[8,128,128]{2,1,0:T(8,128)S(1)}, f32[64,128,128]{2,1,0:T(8,128)}, s32[]{:T(128)}, /*index=5*...) while((s32[]{:T(128)}, f32[8,128,128]{2,1,0:T(8,128)S(1)}, ...), condition=%wide.region_15.16_spmd, body=%wide.region_11.15_spmd.sunk | while | flops 272108192 | bytes 33565088 | solution.py:88
  530.4 1.7 gather_fusion.3
  532.1 2.3 fusion.50
  534.5 6.8 scatter_fusion.5
  541.3 2.7 scatter_fusion.4
  544.0 5.1 gather_fusion.2
  549.1 2.6 fusion.49
  551.7 2.7 scatter_fusion.3
  557.0 2.4 fusion.50
  559.4 6.9 scatter_fusion.5
  566.3 2.7 scatter_fusion.4
  569.0 5.1 gather_fusion.2
  574.0 2.7 fusion.49
  576.7 2.7 scatter_fusion.3
  582.0 2.3 fusion.50
  584.4 7.5 scatter_fusion.5
  591.8 2.7 scatter_fusion.4
  594.5 5.1 gather_fusion.2
  599.6 2.6 fusion.49
  602.2 2.7 scatter_fusion.3
  604.9 134.9 %all-to-all-start.2 = ((f32[32,2,128,128]{3,2,1,0:T(8,128)}), f32[32,2,128,128]{3,2,1,0:T(8,128)}, u32[]{:S(2)}, u32[]{:S(2)}) async-start(f32[32,2,128,128]{3,2,1,0:T(8,128)} %bitcast.59), calls=%async_computation.5 | async-start | bytes 8388608 | tf_op jit(solution)/shard_map/all_to_all | solution.py:91
  741.2 52.1 %all-to-all-done.2 = f32[32,2,128,128]{3,2,1,0:T(8,128)} async-done(((f32[32,2,128,128]{3,2,1,0:T(8,128)}), f32[32,2,128,128]{3,2,1,0:T(8,128)}, u32[]{:S(2)}, u32[]{:S(2)}) %all-to-all-start.2) | async-done | bytes 4194336 | tf_op jit(solution)/shard_map/all_to_all | solution.py:91
  793.3 8.8 %scatter_fusion.7 = f32[8,128,128]{2,1,0:T(8,128)S(1)} fusion(f32[8,128,128]{2,1,0:T(8,128)S(1)} %get-tuple-element.159, s32[64]{0:T(128)S(1)} %fusion.7, f32[64,128,128]{2,1,0:T(8,128)} %bitcast.13), kind=kCustom, calls=%fused_computation.11 | custom fusion | flops 1048576 | bytes 12583168 | tf_op jit(solution)/shard_map/scatter-add | solution.py:99
  802.1 1.9 fusion.5
  (95 shorter events, 29.8 us)
Async XLA Ops:
  7.2 397.4 %copy-start = (bf16[512,128]{1,0:T(8,128)(2,1)S(1)}, bf16[512,128]{1,0:T(8,128)(2,1)}, u32[]{:S(2)}) copy-start(bf16[512,128]{1,0:T(8,128)(2,1)} %param.16) | copy-start | bytes 393220
  7.2 58.4 %all-gather.6.cloned.1.call-start = ((), (), s32[]{:S(2)}) async-start(), calls=%async_computation.7 | async-start | bytes 8650752 | tf_op jit(solution)/shard_map/all_gather | solution.py:47
  12.1 135.6 %all-to-all-start = ((s32[32,1,2]{2,1,0:T(1,128)}), s32[32,1,2]{2,1,0:T(1,128)}, u32[]{:S(2)}, u32[]{:S(2)}) async-start(s32[32,1,2]{2,1,0:T(1,128)} %bitcast.4), calls=%async_computation | async-start | bytes 32768 | tf_op jit(solution)/shard_map/all_to_all | solution.py:41
  19.7 17.5 %copy-start.8 = (s32[256]{0:T(256)S(1)}, s32[256]{0:T(256)}, u32[]{:S(2)}) copy-start(s32[256]{0:T(256)} %param.18) | copy-start | bytes 3076
  65.5 2.6 copy-start.2
  147.7 195.6 %all-to-all-start.1 = ((f32[32,2,128,128]{3,2,1,0:T(8,128)}), f32[32,2,128,128]{3,2,1,0:T(8,128)}, u32[]{:S(2)}, u32[]{:S(2)}) async-start(f32[32,2,128,128]{3,2,1,0:T(8,128)} %bitcast.60), calls=%async_computation.1 | async-start | bytes 8388608 | tf_op jit(solution)/shard_map/all_to_all | solution.py:91
  289.9 63.7 %all-gather.8.cloned.1.call-start = ((), (), s32[]{:S(2)}) async-start(), calls=%async_computation.8 | async-start | bytes 1310720 | tf_op jit(solution)/shard_map/all_gather | solution.py:107
  290.7 85.4 %all-gather.10.cloned.1.call-start = ((), (), s32[]{:S(2)}) async-start(), calls=%async_computation.9 | async-start | bytes 1310720 | tf_op jit(solution)/shard_map/all_gather | solution.py:108
  343.4 10.2 %copy-start.7 = (bf16[512,128]{1,0:T(8,128)(2,1)S(1)}, bf16[512,128]{1,0:T(8,128)(2,1)}, u32[]{:S(2)}) copy-start(bf16[512,128]{1,0:T(8,128)(2,1)} %param.14) | copy-start | bytes 393220
  352.2 24.0 %copy-start.6 = (bf16[512,128]{1,0:T(8,128)(2,1)S(1)}, bf16[512,128]{1,0:T(8,128)(2,1)}, u32[]{:S(2)}) copy-start(bf16[512,128]{1,0:T(8,128)(2,1)} %param.15) | copy-start | bytes 393220
  353.0 51.6 %copy-start.9 = (bf16[1024,128]{1,0:T(8,128)(2,1)S(1)}, bf16[1024,128]{1,0:T(8,128)(2,1)}, u32[]{:S(2)}) copy-start(bf16[1024,128]{1,0:T(8,128)(2,1)} %param.17) | copy-start | bytes 786436
  353.0 51.6 %all-gather.12.cloned.1.call-start = ((), (), s32[]{:S(2)}) async-start(), calls=%async_computation.10 | async-start | bytes 1310720 | tf_op jit(solution)/shard_map/all_gather | solution.py:109
  353.6 86.1 %reduce-scatter.9.cloned.1.call-start = ((), (), s32[]{:S(2)}) async-start(), calls=%async_computation.12 | async-start | bytes 2621440 | tf_op jit(solution)/shard_map/reduce_scatter | solution.py:138
  408.8 62.8 %reduce-scatter.11.cloned.1.call-start = ((), (), s32[]{:S(2)}) async-start(), calls=%async_computation.14 | async-start | bytes 2621440 | tf_op jit(solution)/shard_map/reduce_scatter | solution.py:137
  410.6 30.9 %copy-start.3 = (bf16[1024,512]{1,0:T(8,128)(2,1)S(1)}, bf16[1024,512]{1,0:T(8,128)(2,1)}, u32[]{:S(2)}) copy-start(bf16[1024,512]{1,0:T(8,128)(2,1)} %all-gather.8.cloned.1.call-done) | copy-start | bytes 3145732
  410.6 31.2 %copy-start.4 = (bf16[1024,512]{1,0:T(8,128)(2,1)S(1)}, bf16[1024,512]{1,0:T(8,128)(2,1)}, u32[]{:S(2)}) copy-start(bf16[1024,512]{1,0:T(8,128)(2,1)} %all-gather.10.cloned.1.call-done) | copy-start | bytes 3145732
  410.7 31.6 %copy-start.5 = (bf16[1024,512]{1,0:T(8,128)(2,1)S(1)}, bf16[1024,512]{1,0:T(8,128)(2,1)}, u32[]{:S(2)}) copy-start(bf16[1024,512]{1,0:T(8,128)(2,1)} %all-gather.12.cloned.1.call-done) | copy-start | bytes 3145732
  410.7 116.1 %all-gather.14.cloned.1.call-start = ((), (), s32[]{:S(2)}) async-start(), calls=%async_computation.13 | async-start | bytes 8650752 | tf_op jit(solution)/shard_map/all_gather | solution.py:47
  441.5 298.4 %reduce-scatter.13.cloned.1.call-start = ((), (), s32[]{:S(2)}) async-start(), calls=%async_computation.15 | async-start | bytes 811008
  443.8 358.2 %reduce-scatter.7.cloned.1.call-start = ((), (), s32[]{:S(2)}) async-start(), calls=%async_computation.11 | async-start | bytes 2621440 | tf_op jit(solution)/shard_map/reduce_scatter | solution.py:139
  604.9 188.4 %all-to-all-start.2 = ((f32[32,2,128,128]{3,2,1,0:T(8,128)}), f32[32,2,128,128]{3,2,1,0:T(8,128)}, u32[]{:S(2)}, u32[]{:S(2)}) async-start(f32[32,2,128,128]{3,2,1,0:T(8,128)} %bitcast.59), calls=%async_computation.5 | async-start | bytes 8388608 | tf_op jit(solution)/shard_map/all_to_all | solution.py:91
  793.3 10.7 %copy-start.1 = (bf16[512,128]{1,0:T(8,128)(2,1)S(1)}, bf16[512,128]{1,0:T(8,128)(2,1)}, u32[]{:S(2)}) copy-start(bf16[512,128]{1,0:T(8,128)(2,1)} %param.16) | copy-start | bytes 393220
Sparse Core Ops, SparseCore 0:
  10.3 55.2 all-gather.5
  293.0 27.5 all-gather.7
  353.1 23.0 all-gather.9
  377.7 26.8 all-gather.11
  408.9 30.7 reduce-scatter.8
  442.1 29.4 reduce-scatter.10
  474.4 52.3 all-gather.13
  530.3 76.9 reduce-scatter.12
  609.6 29.2 reduce-scatter.6
where the time goes:
time: 816 us; the launch traced here: 810 us
  waiting for transfers between devices  288 us (35%)
  starting transfers between devices  285 us (35%)
  other arithmetic  112 us (14%)
  local copies, waits for them, and re-layouts  67.7 us (8%)
  matrix products  41.9 us (5%)
  between operations  14.8 us (2%)
    all_to_all x2, starting transfers between devices, deliver(): lax.all_to_all(outgoing.reshape(nodes_size, CAP, block_rows, slivers), 'n...  277 us
    all_to_all x2, waiting for transfers between devices, deliver(): lax.all_to_all(outgoing.reshape(nodes_size, CAP, block_rows, slivers), 'n...  103 us
    all_gather x2, waiting for transfers between devices, fetch(): gathered = lax.all_gather(feature, 'nodes', axis=0, tiled=True)  81.9 us
    scatter-add x6, other arithmetic, advance(): outgoing = outgoing.at[away_index].add(in_part, mode='drop')  42.8 us
    gather x6, local copies, waits for them, and re-layouts, advance(): pulled = source[take_turn(row_index)]  30.6 us
    reduce_scatter x1, waiting for transfers between devices, shards(): lax.psum_scatter(sum_in, 'hid', scatter_dimension=1, tiled=True)  28.9 us
    all_gather x1, waiting for transfers between devices, shards(): lax.all_gather(node_features, 'hid', axis=1, tiled=True)  26.8 us
    reduce_scatter x1, waiting for transfers between devices, shards(): lax.psum_scatter(sum_out, 'hid', scatter_dimension=1, tiled=True)  25.9 us
  transfers between devices with their start and end apart: 12, of which 8 were waited for; matrix products, arithmetic and copies ran while one was open for 27% of the time, Pallas kernels for 0%

commit v1 on v0

v1 whole, which is shorter than its diff:
```python
import jax
import jax.numpy as jnp
from jax import lax
from jax.experimental import pallas as pl
from jax.experimental.pallas import tpu as pltpu
from jax.sharding import PartitionSpec as P

CAP = 2
GROUP = 16
BATCH = 8
CODES = 16
PICKS = 4
MIB = 1024 * 1024
ROOM = 60 * MIB
F32 = jnp.float32
BF16 = jnp.bfloat16


def split(value, size):
    shift = size.bit_length() - 1
    return jnp.right_shift(value, shift), jnp.bitwise_and(value, size - 1)


def pick_kernel(blocks, src_ref, dst_ref, info_ref, pattern_ref, away_ref, send_ref, meta_ref, tiles, counts, listed, sems):
    side = tiles.shape[1]
    devices = counts.shape[0]
    part = (send_ref.shape[1] - CODES) // CAP
    total, myself, quarter = info_ref[0], info_ref[1], info_ref[2]

    def clear(owner, carry):
        counts[owner] = 0
        for rank in range(CAP):
            meta_ref[owner * CAP + rank] = 0
        return carry

    lax.fori_loop(0, devices, clear, 0, unroll=4)

    def copy(slot, entry):
        return pltpu.make_async_copy(pattern_ref.at[slot], tiles.at[entry], sems.at[entry])

    def scan(slot, found):
        owner, _ = split(dst_ref[slot], blocks)
        listed[found] = slot
        return found + ((owner != myself) & (slot < total)).astype(jnp.int32)

    found = lax.fori_loop(0, dst_ref.shape[0], scan, 0, unroll=8)
    found = jnp.minimum(found, devices * CAP)

    def keep(entry, carry):
        slot = listed[entry]
        copy(slot, entry).start()
        owner, landing = split(dst_ref[slot], blocks)
        source = jnp.clip(src_ref[slot] - myself * blocks, 0, blocks - 1)
        rank = jnp.minimum(counts[owner], CAP - 1)
        counts[owner] = rank + 1
        place = owner * CAP + rank
        meta_ref[place] = 1 + source + blocks * landing
        listed[entry] = place
        return carry

    lax.fori_loop(0, found, keep, 0)
    row = lax.broadcasted_iota(jnp.int32, (part, side), 0)
    column = lax.broadcasted_iota(jnp.int32, (part, side), 1)
    chosen = (column == row + quarter * part).astype(F32).astype(BF16)

    def turn(batch, carry):
        first = batch * PICKS
        for index in range(PICKS):

            @pl.when(first + index < found)
            def arrive():
                copy(0, first + index).wait()

        entries = [jnp.minimum(first + index, found - 1) for index in range(PICKS)]
        values = [tiles[entry].astype(F32).astype(BF16) for entry in entries]
        turned = [
            lax.dot_general(chosen, value, (((1,), (1,)), ((), ())), preferred_element_type=F32).astype(BF16) for value in values
        ]
        for index, entry in enumerate(entries):
            place = listed[entry]
            owner, rank = split(place, CAP)
            away_ref[place] = values[index]
            send_ref[owner, pl.ds(pl.multiple_of(rank * part, part), part), :] = turned[index]
        return carry

    lax.fori_loop(0, lax.div(found + PICKS - 1, PICKS), turn, 0)
    lane = lax.broadcasted_iota(jnp.int32, (CODES, side), 1)

    def code(owner, carry):
        values = jnp.zeros((CODES, side), jnp.int32)
        for rank in range(CAP):
            values = jnp.where(lane == rank, meta_ref[owner * CAP + rank], values)
        send_ref[owner, CAP * part :, :] = values.astype(F32).astype(BF16)
        return carry

    lax.fori_loop(0, devices, code, 0, unroll=4)


def pick(tile_src, tile_dst, info, tile_pattern, blocks, devices, quarters):
    side = tile_pattern.shape[1]
    places = devices * CAP
    vmem = pl.BlockSpec(memory_space=pltpu.VMEM)
    smem = pl.BlockSpec(memory_space=pltpu.SMEM)
    return pl.pallas_call(
        lambda *refs: pick_kernel(blocks, *refs),
        in_specs=[smem, smem, smem, pl.BlockSpec(memory_space=pltpu.HBM)],
        out_specs=[vmem, vmem, smem],
        out_shape=[
            jax.ShapeDtypeStruct((places, side, side), BF16),
            jax.ShapeDtypeStruct((devices, CAP * side // quarters + CODES, side), BF16),
            jax.ShapeDtypeStruct((places,), jnp.int32),
        ],
        scratch_shapes=[
            pltpu.VMEM((places, side, side), jnp.int32),
            pltpu.SMEM((devices,), jnp.int32),
            pltpu.SMEM((tile_src.shape[0] + 1,), jnp.int32),
            pltpu.SemaphoreType.DMA((places,)),
        ],
        compiler_params=pltpu.CompilerParams(vmem_limit_bytes=ROOM),
        cost_estimate=pl.CostEstimate(flops=places * side * side, bytes_accessed=8 * MIB, transcendentals=0),
        name="pick",
    )(tile_src, tile_dst, info, tile_pattern)


def pile_kernel(src_ref, dst_ref, info_ref, pattern_ref, local_ref, acc, groups, sems):
    depth, group, side = groups.shape[0], groups.shape[1], groups.shape[2]
    blocks = local_ref.shape[0] // side
    total, myself = info_ref[0], info_ref[1]
    turns = lax.div(total + group - 1, group)

    def copy(turn):
        return pltpu.make_async_copy(pattern_ref.at[pl.ds(turn * group, group)], groups.at[turn], sems.at[turn])

    for turn in range(depth):

        @pl.when(turn < turns)
        def begin():
            copy(turn).start()

    def clear(pair, carry):
        acc[pair] = jnp.zeros((side, side), jnp.int32)
        return carry

    lax.fori_loop(0, acc.shape[0], clear, 0)

    def take(turn, carry):
        copy(turn).wait()

        def add(index, carry):
            slot = turn * group + index
            source = jnp.clip(src_ref[slot] - myself * blocks, 0, blocks - 1)
            owner, landing = split(dst_ref[slot], blocks)
            pair = jnp.where((owner == myself) & (slot < total), source * blocks + landing, blocks * blocks)
            acc[pair] = acc[pair] + groups[turn, index]
            return carry

        lax.fori_loop(0, group, add, 0, unroll=4)
        return carry

    lax.fori_loop(0, turns, take, 0)

    def finish(source, carry):
        rows = pl.ds(pl.multiple_of(source * side, side), side)
        for landing in range(blocks):
            local_ref[rows, landing * side : (landing + 1) * side] = acc[source * blocks + landing].astype(F32).astype(BF16)
        return carry

    lax.fori_loop(0, blocks, finish, 0)


def pile(tile_src, tile_dst, info, tile_pattern, blocks):
    slots, side = tile_pattern.shape[0], tile_pattern.shape[1]
    smem = pl.BlockSpec(memory_space=pltpu.SMEM)
    return pl.pallas_call(
        pile_kernel,
        in_specs=[smem, smem, smem, pl.BlockSpec(memory_space=pltpu.HBM)],
        out_specs=pl.BlockSpec(memory_space=pltpu.VMEM),
        out_shape=jax.ShapeDtypeStruct((blocks * side, blocks * side), BF16),
        scratch_shapes=[
            pltpu.VMEM((blocks * blocks + 1, side, side), jnp.int32),
            pltpu.VMEM((slots // GROUP, GROUP, side, side), jnp.int32),
            pltpu.SemaphoreType.DMA((slots // GROUP,)),
        ],
        compiler_params=pltpu.CompilerParams(vmem_limit_bytes=ROOM),
        cost_estimate=pl.CostEstimate(flops=slots * side * side, bytes_accessed=slots * side * side * 4, transcendentals=0),
        name="pile",
    )(tile_src, tile_dst, info, tile_pattern)


def list_products(info_ref, sent_ref, got_ref, list_ref, blocks):
    x, y, core = info_ref[3], info_ref[4], info_ref[5]
    places = sent_ref.shape[0]
    half = blocks // 2
    last = list_ref.shape[0] - 2

    def entry(device, block, place, row):
        chip, their_core = split(device, 2)
        their_y, their_x = split(chip, 4)
        step_x, step_y = jnp.bitwise_and(x - their_x, 3), jnp.bitwise_and(y - their_y, 3)
        track, block = split(block, half)
        first = jnp.where(track == 0, step_x, step_y)
        second = jnp.where(track == 0, step_y, step_x)
        index = ((second * 4 + first) * 2 + jnp.bitwise_xor(their_core, track)) * half + block
        index = index + jnp.where(track == core, 0, 32 * half)
        return (index * 64 + place) * 32 + row

    def out(place, count):
        code = sent_ref[place] - 1
        landing, source = split(jnp.maximum(code, 0), blocks)
        list_ref[count] = entry(jnp.right_shift(place, 1), landing, place, source)
        return count + (code >= 0).astype(jnp.int32)

    def into(place, count):
        code = got_ref[jnp.right_shift(place, 1), jnp.bitwise_and(place, 1)] - 1
        landing, source = split(jnp.maximum(code, 0), blocks)
        list_ref[count] = entry(jnp.right_shift(place, 1), source, place, blocks + landing)
        return count + (code >= 0).astype(jnp.int32)

    def padded(count):
        ends = lax.div(count + BATCH - 1, BATCH) * BATCH

        def pad(index, carry):
            list_ref[index] = 2 * blocks
            return carry

        lax.fori_loop(count, ends, pad, 0)
        return ends

    count = padded(lax.fori_loop(0, places, out, 0, unroll=4))
    list_ref[last] = lax.div(count, BATCH)
    count = padded(lax.fori_loop(0, places, into, count, unroll=4))
    list_ref[last + 1] = lax.div(count, BATCH)


def spread_kernel(turned, n_pieces, *refs):
    if turned:
        info_ref, list_ref, base_out_ref, base_in_ref, own_ref, w_a_ref, w_b_ref, w_c_ref, away_ref = refs[:9]
        refs = refs[9:]
    else:
        info_ref, sent_ref, base_out_ref, base_in_ref, arrived_ref, away_ref = refs[:6]
        refs = refs[6:]
    landed_refs, piece_refs, refs = refs[:8], refs[8 : 8 + n_pieces], refs[8 + n_pieces :]
    if turned:
        total_ref, p1a_ref, p1b_ref, p2a_ref, p2b_ref, p3a_ref, p3b_ref = refs[:7]
        acc, every, tiles, landed, piece_sems, tile_sem, landed_sems, weights = refs[7:]
    else:
        out_ref, in_ref, list_ref = refs[:3]
        acc, every, tiles, landed, piece_sems, tile_sem, landed_sems, arrived, codes, got, code_sems = refs[3:]
    side = every.shape[1]
    blocks = base_out_ref.shape[0] // side
    plane = info_ref[2]
    planes, places = landed.shape[0], landed.shape[1]
    half, middle = blocks // 2, places // 2
    last = list_ref.shape[0] - 2
    starts = [pltpu.make_async_copy(away_ref, tiles, tile_sem.at[0])]
    for index, ref in enumerate(landed_refs):
        home = landed.at[jnp.bitwise_and(plane + (0, 0, -1, -1, 1, 1, 2, 2)[index], planes - 1), pl.ds((index % 2) * middle, middle)]
        starts.append(pltpu.make_async_copy(ref, home, landed_sems.at[index]))
    offset = 0
    for index, ref in enumerate(piece_refs):
        starts.append(pltpu.make_async_copy(ref, every.at[pl.ds(offset, ref.shape[0])], piece_sems.at[index]))
        offset += ref.shape[0]
    if not turned:
        rows = arrived_ref.shape[1] - CODES
        fetch = pltpu.make_async_copy(arrived_ref.at[:, pl.ds(rows, CODES), :], arrived, code_sems.at[0])
        fetch.start()
    for copy in starts:
        copy.start()
    if not turned:
        fetch.wait()
        codes[...] = arrived[:, 0, :].astype(F32).astype(jnp.int32)
        store = pltpu.make_async_copy(codes, got, code_sems.at[1])
        store.start()

    def clear(row, carry):
        acc[row] = jnp.zeros(acc.shape[1:], F32)
        return carry

    lax.fori_loop(0, acc.shape[0], clear, 0)
    if turned:
        for kind, ref in enumerate((w_a_ref, w_b_ref, w_c_ref)):
            for step in range(planes):
                at = pl.ds(pl.multiple_of(jnp.bitwise_and(plane + step, planes - 1) * side, side), side)
                weights[kind, step * side : (step + 1) * side, :] = ref[at, :]
    else:
        store.wait()
        list_products(info_ref, sent_ref, got, list_ref, blocks)
    for copy in starts:
        copy.wait()

    def batches(first_batch, end_batch, tile_of):
        def add_batch(batch, carry):
            codes = [list_ref[batch * BATCH + index] for index in range(BATCH)]
            products = [
                jnp.dot(
                    tile_of(jnp.bitwise_and(jnp.right_shift(code, 5), 63)),
                    every[jnp.right_shift(code, 11)],
                    preferred_element_type=F32,
                )
                for code in codes
            ]
            for code, product in zip(codes, products):
                row = jnp.bitwise_and(code, 31)
                acc[row] = acc[row] + product
            return carry

        lax.fori_loop(first_batch, end_batch, add_batch, 0)

    batches(0, list_ref[last], lambda place: tiles[place])
    batches(list_ref[last], list_ref[last + 1], lambda place: jnp.concatenate([landed[index, place] for index in range(planes)], axis=0))

    def sums(block):
        at = pl.ds(pl.multiple_of(block * side, side), side)
        return (acc[block] + base_out_ref[at, :]).astype(BF16), (acc[blocks + block] + base_in_ref[at, :]).astype(BF16), at

    def times(values, kind):
        return lax.dot_general(values, weights[kind], (((1,), (1,)), ((), ())), preferred_element_type=F32)

    def keep(block, carry):
        out, into, at = sums(block)
        out_ref[at, :] = out
        in_ref[at, :] = into
        return carry

    def multiply(low):
        def at_block(block, carry):
            out, into, at = sums(block)
            to = pl.ds(pl.multiple_of((block - low) * side, side), side)
            part = (times(out, 0) + times(into, 1)) * (1.0 / 32.0) + times(own_ref[at, :], 2)
            total_ref[at, :] = part[:, :side]
            for index, ref in enumerate((p1a_ref, p2a_ref, p3a_ref) if low == 0 else (p1b_ref, p2b_ref, p3b_ref)):
                ref[to, :] = part[:, (index + 1) * side : (index + 2) * side].astype(ref.dtype)
            return carry

        return at_block

    if turned:
        lax.fori_loop(0, half, multiply(0), 0)
        lax.fori_loop(half, blocks, multiply(half), 0)
    else:
        lax.fori_loop(0, blocks, keep, 0)


def spread(info, listing, base_out, base_in, others, away, landed, pieces, turned):
    side, places = away.shape[1], away.shape[0]
    rows, width = base_out.shape
    blocks = rows // side
    planes = side * CAP // landed[0].shape[1]
    every = sum(piece.shape[0] for piece in pieces) // side
    vmem = pl.BlockSpec(memory_space=pltpu.VMEM)
    smem = pl.BlockSpec(memory_space=pltpu.SMEM)
    far = pl.BlockSpec(memory_space=pltpu.HBM)
    landed = [piece.reshape(-1, side // planes, side) for piece in landed]
    pieces = [piece.reshape(-1, side, width) for piece in pieces]

    def shape(count, kind):
        return jax.ShapeDtypeStruct((count, width), kind)

    devices = places // CAP
    scratch = [
        pltpu.VMEM((2 * blocks + 1, side, width), F32),
        pltpu.VMEM((every, side, width), BF16),
        pltpu.VMEM((places, side, side), BF16),
        pltpu.VMEM((planes, places, side // planes, side), BF16),
        pltpu.SemaphoreType.DMA((len(pieces),)),
        pltpu.SemaphoreType.DMA((1,)),
        pltpu.SemaphoreType.DMA((len(landed),)),
    ]
    if turned:
        out_shape = [shape(rows, F32)] + [shape(rows // 2, kind) for kind in (F32, BF16, BF16, BF16, BF16, F32)]
        out_specs = [vmem] * len(out_shape)
        scratch += [pltpu.VMEM((3, planes * width, width), BF16)]
        other_specs = [vmem] * len(others)
    else:
        out_shape = [shape(rows, BF16), shape(rows, BF16), jax.ShapeDtypeStruct((2 * (places + BATCH) + 2,), jnp.int32)]
        out_specs = [vmem, vmem, smem]
        scratch += [
            pltpu.VMEM((devices, CODES, side), BF16),
            pltpu.VMEM((devices, side), jnp.int32),
            pltpu.SMEM((devices, side), jnp.int32),
            pltpu.SemaphoreType.DMA((2,)),
        ]
        other_specs = [far]
    return pl.pallas_call(
        lambda *refs: spread_kernel(turned, len(pieces), *refs),
        in_specs=[smem] * 2 + [vmem] * 2 + other_specs + [far] * (1 + len(landed) + len(pieces)),
        out_specs=out_specs,
        out_shape=out_shape,
        scratch_shapes=scratch,
        compiler_params=pltpu.CompilerParams(vmem_limit_bytes=ROOM),
        cost_estimate=pl.CostEstimate(flops=2 * rows * width * 3 * 512 + places * side**3 * 2, bytes_accessed=16 * MIB, transcendentals=0),
        name="spread",
    )(info, listing, base_out, base_in, *others, away, *landed, *pieces)


def activate_kernel(info_ref, *refs):
    planes = 4
    sides, weight_refs, refs = refs[: 3 * planes], refs[3 * planes : 3 * planes + 3], refs[3 * planes + 3 :]
    cotangent_ref, hidden_ref, grad_ref, weights = refs
    rows, width = cotangent_ref.shape
    plane = info_ref[2]
    for kind, ref in enumerate(weight_refs):
        for index, step in enumerate((0, -1, 1, 2)):
            at = pl.ds(pl.multiple_of(jnp.bitwise_and(plane + step, planes - 1) * width, width), width)
            weights[kind, index * width : (index + 1) * width, :] = ref[at, :]
    tall = 256

    def rows_at(turn, carry):
        at = pl.ds(pl.multiple_of(turn * tall, tall), tall)

        def times(kind):
            values = jnp.concatenate([ref[at, :] for ref in sides[kind * planes : (kind + 1) * planes]], axis=1)
            return jnp.dot(values, weights[kind], preferred_element_type=F32)

        value = (times(0) + times(1)) * (1.0 / 32.0) + times(2)
        gate = 1.0 / (1.0 + jnp.exp(-value))
        hidden_ref[at, :] = (value * gate).astype(BF16)
        grad_ref[at, :] = (cotangent_ref[at, :].astype(F32) * gate * (1.0 + value * (1.0 - gate))).astype(BF16)
        return carry

    lax.fori_loop(0, rows // tall, rows_at, 0)


def activate(info, outs, ins, selves, weights, cotangent):
    rows, width = cotangent.shape
    vmem = pl.BlockSpec(memory_space=pltpu.VMEM)
    return pl.pallas_call(
        activate_kernel,
        in_specs=[pl.BlockSpec(memory_space=pltpu.SMEM)] + [vmem] * 16,
        out_specs=[vmem] * 2,
        out_shape=[jax.ShapeDtypeStruct((rows, width), BF16)] * 2,
        scratch_shapes=[pltpu.VMEM((3, 4 * width, width), BF16)],
        compiler_params=pltpu.CompilerParams(vmem_limit_bytes=ROOM),
        cost_estimate=pl.CostEstimate(flops=2 * rows * 3 * 512 * width, bytes_accessed=4 * MIB, transcendentals=rows * width),
        name="activate",
    )(info, *outs, *ins, *selves, *weights, cotangent)


def slopes_kernel(info_ref, *refs):
    planes = 4
    grad_ref, out_ref, left = refs[3 * planes :]
    width = grad_ref.shape[1]
    slivers = out_ref.shape[1] // 3
    strips = width // slivers
    plane = info_ref[2]
    for kind in range(3):
        for index in range(planes):
            left[:, index * width : (index + 1) * width] = refs[kind * planes + index][...]
        terms = lax.dot_general(grad_ref[...], left[...], (((0,), (0,)), ((), ())), preferred_element_type=F32)
        for index, step in enumerate((0, -1, 1, 2)):
            first = jnp.bitwise_and(plane + step, planes - 1) * strips
            turned = terms[:, index * width : (index + 1) * width].T
            for strip in range(strips):
                out_ref[first + strip, kind * slivers : (kind + 1) * slivers, :] = turned[strip * slivers : (strip + 1) * slivers, :]


def slopes(info, outs, ins, selves, grad_z, devices):
    rows, width = grad_z.shape
    vmem = pl.BlockSpec(memory_space=pltpu.VMEM)
    return pl.pallas_call(
        slopes_kernel,
        in_specs=[pl.BlockSpec(memory_space=pltpu.SMEM)] + [vmem] * 13,
        out_specs=vmem,
        out_shape=jax.ShapeDtypeStruct((devices, 3 * width * 4 // devices, width), F32),
        scratch_shapes=[pltpu.VMEM((rows, 4 * width), BF16)],
        compiler_params=pltpu.CompilerParams(vmem_limit_bytes=ROOM),
        cost_estimate=pl.CostEstimate(flops=2 * rows * 3 * width * 4 * width, bytes_accessed=4 * MIB, transcendentals=0),
        name="slopes",
    )(info, *outs, *ins, *selves, grad_z)


def around(devices, stage, step):
    pairs = []
    for here in range(devices):
        core, x, y = here % 2, here // 2 % 4, here // 8
        if (core + stage) % 2 == 0:
            x = (x + step) % 4
        else:
            y = (y + step) % 4
        pairs.append((here, (y * 4 + x) * 2 + core))
    return pairs


def gather(values, devices, core, ahead):
    half = values.shape[0] // 2

    def forward(part, stage):
        return lax.ppermute(part, "nodes", around(devices, stage, 1))

    def backward(part, stage):
        return lax.ppermute(part, "nodes", around(devices, stage, -1))

    def sister(part):
        return lax.ppermute(part, "nodes", [(here, here ^ 1) for here in range(devices)])

    kept = lax.dynamic_slice_in_dim(values, core * half, half, 0)
    given = lax.dynamic_slice_in_dim(values, (1 - core) * half, half, 0)
    zero = jnp.concatenate([kept, sister(given)])
    if ahead is not None:
        zero, ahead = lax.optimization_barrier((zero, ahead))
    plus, minus = forward(zero, 0), backward(zero, 0)
    plus_far, minus_far = forward(plus[:half], 0), backward(minus[half:], 0)
    low = jnp.concatenate([zero, plus])
    high = jnp.concatenate([plus_far, minus_far, minus])
    plus_low, minus_low = forward(low, 1), backward(low, 1)
    plus_high, minus_high = forward(high, 1), backward(high, 1)
    plus_far, minus_far = forward(plus_low, 1), backward(minus_high, 1)
    own = [low, high, plus_low, plus_high, plus_far, minus_far, minus_low, minus_high]
    return own + [sister(piece) for piece in own], ahead, high


def shards(
    node_features, w_out, w_in, w_self, cotangent, tile_src, tile_dst, tile_pattern, tile_count
):
    devices = lax.axis_size("nodes")
    planes = lax.axis_size("hid")
    myself = lax.axis_index("nodes").astype(jnp.int32)
    plane = lax.axis_index("hid").astype(jnp.int32)
    core = lax.rem(myself, 2)
    side = tile_pattern.shape[1]
    rows, width = node_features.shape
    blocks = rows // side
    halves = rows // 2
    middle = devices // 2

    def shift(values, step):
        return lax.ppermute(values, "hid", [(here, (here + step) % planes) for here in range(planes)])

    def all_columns(part):
        left, right = shift(part, 1), shift(part, -1)
        return [part, left, right, shift(part, 2)]

    info = jnp.stack([tile_count[0], myself, plane, lax.rem(lax.div(myself, 2), 4), lax.div(myself, 8), core])
    away, send, sent = pick(tile_src, tile_dst, info, tile_pattern, blocks, devices, planes)
    pieces_x, (send, later_x), high = gather(node_features, devices, core, (send, node_features))
    arrived = lax.all_to_all(send, "nodes", 0, 0, tiled=True)
    part = send.shape[1] - CODES
    own_a, own_b = arrived[:middle, :part, :], arrived[middle:, :part, :]
    left_a, right_b = shift(own_a, 1), shift(own_b, -1)
    left_b, right_a = shift(own_b, 1), shift(own_a, -1)
    landed = [own_a, own_b, left_a, left_b, right_a, right_b, shift(left_a, 1), shift(right_b, -1)]
    pile_info, later_x, _ = lax.optimization_barrier((info, later_x, high))
    local = pile(tile_src, tile_dst, pile_info, tile_pattern, blocks)
    all_x = all_columns(later_x)

    def local_sums(values):
        return (
            jnp.dot(local, values, preferred_element_type=F32),
            jnp.einsum("ij,ik->jk", local, values, preferred_element_type=F32),
        )

    def collect(own, p1a, p1b, p2a, p2b, p3a, p3b):
        left, right = shift(p2a, 1), shift(p2b, -1)
        one_b, three_a = shift(p1b, 1), shift(p3a, -1)
        one_a = shift((p1a + left.astype(F32)).astype(BF16), 1)
        three_b = shift((p3b + right.astype(F32)).astype(BF16), -1)
        low = own[:halves] + one_a.astype(F32) + three_a.astype(F32)
        high = own[halves:] + one_b.astype(F32) + three_b.astype(F32)
        return jnp.concatenate([low, high])

    base_out, base_in = local_sums(node_features)
    prop_out, prop_in, listed = spread(info, sent, base_out, base_in, [arrived], away, landed, pieces_x, False)
    out_left, in_right = shift(prop_out, 1), shift(prop_in, -1)
    in_left, out_right = shift(prop_in, 1), shift(prop_out, -1)
    all_out = [prop_out, out_left, out_right, shift(out_left, 1)]
    all_in = [prop_in, in_left, in_right, shift(in_right, -1)]
    weights = [w_out, w_in, w_self]
    hidden, grad_z = activate(info, all_out, all_in, all_x, weights, cotangent)

    terms = slopes(info, all_out, all_in, all_x, grad_z, devices)
    pieces_z, terms, high = gather(grad_z, devices, core, terms)
    terms, _ = lax.optimization_barrier((terms, high))
    base_out, base_in = local_sums(grad_z)
    parts = spread(info, listed, base_out, base_in, [grad_z, w_in, w_out, w_self], away, landed, pieces_z, True)
    grad_input = collect(*parts).astype(BF16)

    slivers = width * planes // devices
    grads = jnp.sum(lax.all_to_all(terms, "nodes", 0, 0, tiled=True), axis=0).reshape(3, slivers, width)
    return (hidden, grad_input, grads[0] / 32.0, grads[1] / 32.0, grads[2])


def solution(mesh):
    in_specs = (
        P("nodes", "hid"),
        P(None, "hid"),
        P(None, "hid"),
        P(None, "hid"),
        P("nodes", "hid"),
        P("nodes"),
        P("nodes"),
        P("nodes", None, None),
        P("nodes"),
    )
    out_specs = (
        P("nodes", "hid"),
        P("nodes", "hid"),
        P("nodes", "hid"),
        P("nodes", "hid"),
        P("nodes", "hid"),
    )
    return jax.shard_map(shards, mesh=mesh, in_specs=in_specs, out_specs=out_specs, check_vma=False)
```

time: 816 us -> 210 us (0.26)
  waiting for transfers between devices: 288 us -> 62.4 us
  starting transfers between devices: 285 us -> 77.8 us
  other arithmetic: 112 us -> 3.49 us
  local copies, waits for them, and re-layouts: 67.7 us -> 9.67 us
  Pallas kernels: 0 us -> 44.4 us
  matrix products: 41.9 us -> 7.68 us
  between operations: 14.8 us -> 1.89 us
    all_to_all x3 -> x2, starting transfers between devices: 285 us -> 10.9 us  [the longest x1 7.03 us: shards(): arrived = lax.all_to_all(send, 'nodes', 0, 0, tiled=True)]
    all_gather x5 -> x0, waiting for transfers between devices: 130 us -> none  [the longest x2 81.9 us: fetch(): gathered = lax.all_gather(feature, 'nodes', axis=0, tiled=True)]
    all_to_all x3 -> x2, waiting for transfers between devices: 103 us -> 0.01 us  [the longest x1 0.01 us: shards(): arrived = lax.all_to_all(send, 'nodes', 0, 0, tiled=True)]
    scatter-add x20 -> x0, other arithmetic: 92.6 us -> none  [the longest x6 42.8 us: advance(): outgoing = outgoing.at[away_index].add(in_part, mode='drop')]
    ppermute x0 -> x59, starting transfers between devices: none -> 66.9 us  [the longest x21 32.1 us: shift(): lax.ppermute(values, 'hid', [(here, (here + step) % planes) for here in r...]
    ppermute x0 -> x59, waiting for transfers between devices: none -> 62.4 us  [the longest x21 32.8 us: shift(): lax.ppermute(values, 'hid', [(here, (here + step) % planes) for here in r...]
    reduce_scatter x3 -> x0, waiting for transfers between devices: 54.9 us -> none  [the longest x1 28.9 us: shards(): lax.psum_scatter(sum_in, 'hid', scatter_dimension=1, tiled=True)]
    pallas_call x0 -> x6, Pallas kernels: none -> 44.4 us  [the longest x2 21.4 us: spread(): pl.pallas_call(lambda *refs: spread_kernel(turned, len(pieces), *refs), i...]
  transfers between devices with their start and end apart: 12 -> 61, of which waited for: 8 -> 15; matrix products, arithmetic and copies ran while one was open for 27% -> 6% of each run, Pallas kernels for 0% -> 19%
where the time goes in v1:
time: 210 us; the launch traced here: 207 us
  starting transfers between devices  77.8 us (37%)
  waiting for transfers between devices  62.4 us (30%)
  Pallas kernels  44.4 us (21%)
  local copies, waits for them, and re-layouts  9.67 us (5%)
  matrix products  7.68 us (4%)
  other arithmetic  3.49 us (2%)
    ppermute x21, waiting for transfers between devices, shift(): lax.ppermute(values, 'hid', [(here, (here + step) % planes) for here in r...  32.8 us
    ppermute x21, starting transfers between devices, shift(): lax.ppermute(values, 'hid', [(here, (here + step) % planes) for here in r...  32.1 us
    ppermute x10, starting transfers between devices, backward(): return lax.ppermute(part, 'nodes', around(devices, stage, -1))  23.8 us
    pallas_call x2, Pallas kernels, spread(): pl.pallas_call(lambda *refs: spread_kernel(turned, len(pieces), *refs), i...  21.4 us
    ppermute x10, waiting for transfers between devices, backward(): return lax.ppermute(part, 'nodes', around(devices, stage, -1))  19.4 us
    ppermute x10, waiting for transfers between devices, forward(): return lax.ppermute(part, 'nodes', around(devices, stage, 1))  10.2 us
    pallas_call x1, Pallas kernels, pile(): pl.pallas_call(pile_kernel, in_specs=[smem, smem, smem, pl.BlockSpec(memo...  8.58 us
    ppermute x10, starting transfers between devices, forward(): return lax.ppermute(part, 'nodes', around(devices, stage, 1))  7.72 us
  transfers between devices with their start and end apart: 61, of which 15 were waited for; matrix products, arithmetic and copies ran while one was open for 6% of the time, Pallas kernels for 19%

profile of v1, /device:TPU:0, one launch (start us, length us, event | category | flops | bytes accessed | tf_op | source)
XLA Modules:
  0.0 207.4 jit_solution(3450073080240479729)
XLA Ops:
  0.6 1.0 constant_dynamic-slice_fusion.3
  2.4 0.7 stack.23.refs_2_.info_ref.refs_0_
  3.1 5.9 %pick.1 = (bf16[64,128,128]{2,1,0:T(8,128)(2,1)}, bf16[32,80,128]{2,1,0:T(8,128)(2,1)}, s32[64]{0:T(128)}) custom-call(s32[256]{0:T(256)} %src_ref.1, s32[256]{0:T(256)} %dst_ref.1, s32[6]{0:T(128)} %stack.23.refs_2_.info_ref.refs_0_, s32[256,128,128]{2,1,0:T(8,128)} %pattern_ref.1), custom_call_target="tpu_custom_call" | custom-call | flops 1048576 | bytes 8388608 | tf_op jit(solution)/shard_map/pick/pallas_call | solution.py:104
  9.0 2.0 collective-permute-start.1
  11.1 7.0 %all-to-all-start = ((bf16[32,80,128]{2,1,0:T(8,128)(2,1)}), bf16[32,80,128]{2,1,0:T(8,128)(2,1)S(1)}, u32[]{:S(2)}, u32[]{:S(2)}) async-start(bf16[32,80,128]{2,1,0:T(8,128)(2,1)} %get-tuple-element.33), calls=%async_computation | async-start | bytes 1310720 | tf_op jit(solution)/shard_map/all_to_all | solution.py:536
  18.1 3.1 %collective-permute-start.3 = (bf16[1024,128]{1,0:T(8,128)(2,1)S(1)}, bf16[1024,128]{1,0:T(8,128)(2,1)S(1)}, u32[]{:S(2)}, u32[]{:S(2)}) collective-permute-start(bf16[1024,128]{1,0:T(8,128)(2,1)S(1)} %pad_maximum_fusion), channel_id=1, source_target_pairs={{0,24},{4,100},{8,0},{12,108},{16,8},{20,116},{24,16},{28,124},{32... | collective-permute-start | bytes 786440 | tf_op jit(solution)/shard_map/ppermute | solution.py:491
  21.3 9.5 %collective-permute-done.3 = bf16[1024,128]{1,0:T(8,128)(2,1)S(1)} collective-permute-done((bf16[1024,128]{1,0:T(8,128)(2,1)S(1)}, bf16[1024,128]{1,0:T(8,128)(2,1)S(1)}, u32[]{:S(2)}, u32[]{:S(2)}) %collective-permute-start.3) | collective-permute-done | bytes 262176 | tf_op jit(solution)/shard_map/ppermute | solution.py:491
  30.8 1.6 collective-permute-start.4
  32.5 1.7 collective-permute-start.11
  34.3 1.6 collective-permute-start.16
  36.3 2.0 collective-permute-start.5
  38.2 2.2 %collective-permute-start.8 = (bf16[16,64,128]{2,1,0:T(8,128)(2,1)S(1)}, bf16[16,64,128]{2,1,0:T(8,128)(2,1)}, u32[]{:S(2)}, u32[]{:S(2)}) collective-permute-start(bf16[16,64,128]{2,1,0:T(8,128)(2,1)S(1)} %get-tuple-element.51), channel_id=1, source_target_pairs={{0,3},{1,0},{2,1},{3,2},{4,7},{5,4},{6,5},{7,6},{8,11},{9,8},{10,9... | collective-permute-start | bytes 786440 | tf_op jit(solution)/shard_map/ppermute | solution.py:527
  40.5 2.6 %collective-permute-done.11 = bf16[2048,128]{1,0:T(8,128)(2,1)} collective-permute-done((bf16[2048,128]{1,0:T(8,128)(2,1)S(1)}, bf16[2048,128]{1,0:T(8,128)(2,1)}, u32[]{:S(2)}, u32[]{:S(2)}) %collective-permute-start.11) | collective-permute-done | bytes 524320 | tf_op jit(solution)/shard_map/ppermute | solution.py:488
  43.1 1.7 collective-permute-start.14
  45.1 1.9 collective-permute-done.5
  47.1 3.2 %collective-permute-start.7 = (bf16[16,64,128]{2,1,0:T(8,128)(2,1)S(1)}, bf16[16,64,128]{2,1,0:T(8,128)(2,1)S(1)}, u32[]{:S(2)}, u32[]{:S(2)}) collective-permute-start(bf16[16,64,128]{2,1,0:T(8,128)(2,1)S(1)} %get-tuple-element.52), channel_id=1, source_target_pairs={{0,3},{1,0},{2,1},{3,2},{4,7},{5,4},{6,5},{7,6},{8,11},{9,8},{10,9... | collective-permute-start | bytes 786440 | tf_op jit(solution)/shard_map/ppermute | solution.py:527
  50.3 5.9 %collective-permute-done.6 = bf16[16,64,128]{2,1,0:T(8,128)(2,1)S(1)} collective-permute-done((bf16[16,64,128]{2,1,0:T(8,128)(2,1)S(1)}, bf16[16,64,128]{2,1,0:T(8,128)(2,1)S(1)}, u32[]{:S(2)}, u32[]{:S(2)}) %collective-permute-start.6) | collective-permute-done | bytes 262176 | tf_op jit(solution)/shard_map/ppermute | solution.py:527
  56.2 0.9 collective-permute-start.13
  57.2 2.4 %collective-permute-start.15 = (bf16[2048,128]{1,0:T(8,128)(2,1)}, bf16[2048,128]{1,0:T(8,128)(2,1)}, u32[]{:S(2)}, u32[]{:S(2)}) collective-permute-start(bf16[2048,128]{1,0:T(8,128)(2,1)} %collective-permute-done.14), channel_id=1, source_target_pairs={{0,96},{4,28},{8,104},{12,4},{16,112},{20,12},{24,120},{28,20},{32... | collective-permute-start | bytes 1572872 | tf_op jit(solution)/shard_map/ppermute | solution.py:491
  59.6 0.9 collective-permute-start.9
  60.4 0.8 copy-done.22
  61.3 2.6 %collective-permute-start.10 = (bf16[16,64,128]{2,1,0:T(8,128)(2,1)}, bf16[16,64,128]{2,1,0:T(8,128)(2,1)}, u32[]{:S(2)}, u32[]{:S(2)}) collective-permute-start(bf16[16,64,128]{2,1,0:T(8,128)(2,1)} %collective-permute-done.8), channel_id=1, source_target_pairs={{0,3},{1,0},{2,1},{3,2},{4,7},{5,4},{6,5},{7,6},{8,11},{9,8},{10,9... | collective-permute-start | bytes 786440 | tf_op jit(solution)/shard_map/ppermute | solution.py:527
  63.8 8.6 %pile.1 = bf16[1024,1024]{1,0:T(8,128)(2,1)} custom-call(s32[256]{0:T(256)} %src_ref.1, s32[256]{0:T(256)} %dst_ref.1, s32[6]{0:T(128)} %stack.23.refs_2_.info_ref.refs_0_, s32[256,128,128]{2,1,0:T(8,128)} %pattern_ref.1), custom_call_target="tpu_custom_call" | custom-call | flops 4194304 | bytes 16777216 | tf_op jit(solution)/shard_map/pile/pallas_call | solution.py:174
  73.7 3.1 %fusion.2.refs_2_ = f32[1024,128]{1,0:T(8,128)} fusion(bf16[1024,1024]{1,0:T(8,128)(2,1)} %pile.1, bf16[1024,128]{1,0:T(8,128)(2,1)S(1)} %copy-done.2), kind=kOutput, calls=%fused_computation.25 | convolution fusion | flops 268435456 | bytes 2883584 | tf_op jit(solution)/shard_map/dot_general | solution.py:548
  76.8 1.5 fusion.3.refs_3_
  78.4 3.2 %collective-permute-start.32 = (bf16[1024,128]{1,0:T(8,128)(2,1)S(1)}, bf16[1024,128]{1,0:T(8,128)(2,1)S(1)}, u32[]{:S(2)}, u32[]{:S(2)}) collective-permute-start(bf16[1024,128]{1,0:T(8,128)(2,1)S(1)} %copy-done.2), channel_id=1, source_target_pairs={{0,3},{1,0},{2,1},{3,2},{4,7},{5,4},{6,5},{7,6},{8,11},{9,8},{10,9... | collective-permute-start | bytes 786440 | tf_op jit(solution)/shard_map/ppermute | solution.py:527
  81.6 0.8 copy-done.26
  82.4 0.8 copy-done.27
  83.2 10.4 %spread.2 = (bf16[1024,128]{1,0:T(8,128)(2,1)}, bf16[1024,128]{1,0:T(8,128)(2,1)}, s32[146]{0:T(256)}) custom-call(s32[6]{0:T(128)} %stack.23.refs_2_.info_ref.refs_0_, s32[64]{0:T(128)} %get-tuple-element.28.refs_1_, f32[1024,128]{1,0:T(8,128)} %fusion.2.refs_2_, f32[1024,128]{1,0:T(8,128)} %fusion.3.refs_3_, bf16[32,80,128]{2,1,0:T(8,128)(2,1)} %copy-done.3, ...), custom_call_target="tpu_custom_call" | custom-call | flops 671088640 | bytes 16777216 | tf_op jit(solution)/shard_map/spread/pallas_call | solution.py:384
  93.8 3.2 %collective-permute-start.29 = (bf16[1024,128]{1,0:T(8,128)(2,1)}, bf16[1024,128]{1,0:T(8,128)(2,1)S(1)}, u32[]{:S(2)}, u32[]{:S(2)}) collective-permute-start(bf16[1024,128]{1,0:T(8,128)(2,1)} %get-tuple-element.36.refs_4_), channel_id=1, source_target_pairs={{0,3},{1,0},{2,1},{3,2},{4,7},{5,4},{6,5},{7,6},{8,11},{9,8},{10,9... | collective-permute-start | bytes 786440 | tf_op jit(solution)/shard_map/ppermute | solution.py:527
  97.0 1.5 collective-permute-start.26
  99.1 10.8 %collective-permute-done.25.refs_1_ = bf16[1024,128]{1,0:T(8,128)(2,1)S(1)} collective-permute-done((bf16[1024,128]{1,0:T(8,128)(2,1)}, bf16[1024,128]{1,0:T(8,128)(2,1)S(1)}, u32[]{:S(2)}, u32[]{:S(2)}) %collective-permute-start.25) | collective-permute-done | bytes 262176 | tf_op jit(solution)/shard_map/ppermute | solution.py:527
  109.9 3.3 %collective-permute-start.30 = (bf16[1024,128]{1,0:T(8,128)(2,1)S(1)}, bf16[1024,128]{1,0:T(8,128)(2,1)}, u32[]{:S(2)}, u32[]{:S(2)}) collective-permute-start(bf16[1024,128]{1,0:T(8,128)(2,1)S(1)} %collective-permute-done.29.refs_6_), channel_id=1, source_target_pairs={{0,3},{1,0},{2,1},{3,2},{4,7},{5,4},{6,5},{7,6},{8,11},{9,8},{10,9... | collective-permute-start | bytes 786440 | tf_op jit(solution)/shard_map/ppermute | solution.py:527
  113.2 2.0 collective-permute-done.26.refs_2_
  115.5 5.1 %collective-permute-done.27.refs_3_ = bf16[1024,128]{1,0:T(8,128)(2,1)S(1)} collective-permute-done((bf16[1024,128]{1,0:T(8,128)(2,1)S(1)}, bf16[1024,128]{1,0:T(8,128)(2,1)S(1)}, u32[]{:S(2)}, u32[]{:S(2)}) %collective-permute-start.27) | collective-permute-done | bytes 262176 | tf_op jit(solution)/shard_map/ppermute | solution.py:527
  120.6 0.7 copy-done.18
  121.4 4.4 %activate.1 = (bf16[1024,128]{1,0:T(8,128)(2,1)}, bf16[1024,128]{1,0:T(8,128)(2,1)}) custom-call(s32[6]{0:T(128)} %stack.23.refs_2_.info_ref.refs_0_, bf16[1024,128]{1,0:T(8,128)(2,1)} %get-tuple-element.35.refs_0_, bf16[1024,128]{1,0:T(8,128)(2,1)} %copy-done.13, bf16[1024,128]{1,0:T(8,128)(2,1)} %copy-done.16, bf16[1024,128]{1,0:T(8,128)(2,1)} %copy-done.18, ...), custom_call_target="tpu_custom_call" | custom-call | flops 402653184 | bytes 4194304 | tf_op jit(solution)/shard_map/activate/pallas_call | solution.py:427
  125.7 1.0 constant_dynamic-slice_fusion.1
  126.8 4.1 %slopes.1 = f32[32,48,128]{2,1,0:T(8,128)} custom-call(s32[6]{0:T(128)} %stack.23.refs_2_.info_ref.refs_0_, bf16[1024,128]{1,0:T(8,128)(2,1)} %get-tuple-element.35.refs_0_, bf16[1024,128]{1,0:T(8,128)(2,1)} %copy-done.13, bf16[1024,128]{1,0:T(8,128)(2,1)} %copy-done.16, bf16[1024,128]{1,0:T(8,128)(2,1)} %copy-done.18, ...), custom_call_target="tpu_custom_call" | custom-call | flops 402653184 | bytes 4194304 | tf_op jit(solution)/shard_map/slopes/pallas_call | solution.py:460
  131.1 3.2 %collective-permute-start.37 = (bf16[1024,128]{1,0:T(8,128)(2,1)S(1)}, bf16[1024,128]{1,0:T(8,128)(2,1)S(1)}, u32[]{:S(2)}, u32[]{:S(2)}) collective-permute-start(bf16[1024,128]{1,0:T(8,128)(2,1)S(1)} %pad_maximum_fusion.1), channel_id=1, source_target_pairs={{0,24},{4,100},{8,0},{12,108},{16,8},{20,116},{24,16},{28,124},{32... | collective-permute-start | bytes 786440 | tf_op jit(solution)/shard_map/ppermute | solution.py:491
  134.3 4.3 %collective-permute-done.35 = bf16[1024,128]{1,0:T(8,128)(2,1)S(1)} collective-permute-done((bf16[1024,128]{1,0:T(8,128)(2,1)S(1)}, bf16[1024,128]{1,0:T(8,128)(2,1)S(1)}, u32[]{:S(2)}, u32[]{:S(2)}) %collective-permute-start.35) | collective-permute-done | bytes 262176 | tf_op jit(solution)/shard_map/ppermute | solution.py:488
  138.8 3.3 %collective-permute-start.38 = (bf16[512,128]{1,0:T(8,128)(2,1)S(1)}, bf16[512,128]{1,0:T(8,128)(2,1)S(1)}, u32[]{:S(2)}, u32[]{:S(2)}) collective-permute-start(bf16[512,128]{1,0:T(8,128)(2,1)S(1)} %slice.52), channel_id=1, source_target_pairs={{0,24},{4,100},{8,0},{12,108},{16,8},{20,116},{24,16},{28,124},{32... | collective-permute-start | bytes 393224 | tf_op jit(solution)/shard_map/ppermute | solution.py:491
  142.2 3.2 %collective-permute-start.44 = (bf16[2048,128]{1,0:T(8,128)(2,1)S(1)}, bf16[2048,128]{1,0:T(8,128)(2,1)S(1)}, u32[]{:S(2)}, u32[]{:S(2)}) collective-permute-start(bf16[2048,128]{1,0:T(8,128)(2,1)S(1)} %constant_dynamic-update-slice_fusion.5), channel_id=1, source_target_pairs={{0,96},{4,28},{8,104},{12,4},{16,112},{20,12},{24,120},{28,20},{32... | collective-permute-start | bytes 1572872 | tf_op jit(solution)/shard_map/ppermute | solution.py:491
  146.1 0.6 constant_dynamic-update-slice_fusion.8
  146.8 0.7 constant_dynamic-update-slice_fusion.7
  147.5 2.0 collective-permute-start.40
  149.5 3.2 %collective-permute-done.39 = bf16[2048,128]{1,0:T(8,128)(2,1)} collective-permute-done((bf16[2048,128]{1,0:T(8,128)(2,1)S(1)}, bf16[2048,128]{1,0:T(8,128)(2,1)}, u32[]{:S(2)}, u32[]{:S(2)}) %collective-permute-start.39) | collective-permute-done | bytes 524320 | tf_op jit(solution)/shard_map/ppermute | solution.py:488
  154.3 3.5 %collective-permute-done.42 = bf16[2048,128]{1,0:T(8,128)(2,1)} collective-permute-done((bf16[2048,128]{1,0:T(8,128)(2,1)}, bf16[2048,128]{1,0:T(8,128)(2,1)}, u32[]{:S(2)}, u32[]{:S(2)}) %collective-permute-start.42) | collective-permute-done | bytes 524320 | tf_op jit(solution)/shard_map/ppermute | solution.py:491
  157.9 3.7 %collective-permute-start.43 = (bf16[2048,128]{1,0:T(8,128)(2,1)}, bf16[2048,128]{1,0:T(8,128)(2,1)}, u32[]{:S(2)}, u32[]{:S(2)}) collective-permute-start(bf16[2048,128]{1,0:T(8,128)(2,1)} %collective-permute-done.42), channel_id=1, source_target_pairs={{0,96},{4,28},{8,104},{12,4},{16,112},{20,12},{24,120},{28,20},{32... | collective-permute-start | bytes 1572872 | tf_op jit(solution)/shard_map/ppermute | solution.py:491
  161.6 3.9 %all-to-all-start.1 = ((f32[32,48,128]{2,1,0:T(8,128)}), f32[32,48,128]{2,1,0:T(8,128)S(1)}, u32[]{:S(2)}, u32[]{:S(2)}) async-start(f32[32,48,128]{2,1,0:T(8,128)} %slopes.1), calls=%async_computation.1 | async-start | bytes 1572864 | tf_op jit(solution)/shard_map/all_to_all | solution.py:578
  166.6 6.3 %collective-permute-done.43 = bf16[2048,128]{1,0:T(8,128)(2,1)} collective-permute-done((bf16[2048,128]{1,0:T(8,128)(2,1)}, bf16[2048,128]{1,0:T(8,128)(2,1)}, u32[]{:S(2)}, u32[]{:S(2)}) %collective-permute-start.43) | collective-permute-done | bytes 524320 | tf_op jit(solution)/shard_map/ppermute | solution.py:491
  172.9 1.5 fusion.5.refs_3_
  174.5 1.5 fusion.4.refs_2_
  176.0 0.8 copy-done.30
  176.8 11.0 %spread.3 = (f32[1024,128]{1,0:T(8,128)}, f32[512,128]{1,0:T(8,128)}, bf16[512,128]{1,0:T(8,128)(2,1)}, bf16[512,128]{1,0:T(8,128)(2,1)}, bf16[512,128]{1,0:T(8,...) custom-call(s32[6]{0:T(128)} %stack.23.refs_2_.info_ref.refs_0_, s32[146]{0:T(256)} %get-tuple-element.39.refs_1_, ...), custom_call_target="tpu_custom_call" | custom-call | flops 671088640 | bytes 16777216 | tf_op jit(solution)/shard_map/spread/pallas_call | solution.py:384
  187.8 2.4 %collective-permute-start.57 = (bf16[512,128]{1,0:T(8,128)(2,1)}, bf16[512,128]{1,0:T(8,128)(2,1)S(1)}, u32[]{:S(2)}, u32[]{:S(2)}) collective-permute-start(bf16[512,128]{1,0:T(8,128)(2,1)} %get-tuple-element.48), channel_id=1, source_target_pairs={{0,3},{1,0},{2,1},{3,2},{4,7},{5,4},{6,5},{7,6},{8,11},{9,8},{10,9... | collective-permute-start | bytes 393224 | tf_op jit(solution)/shard_map/ppermute | solution.py:527
  190.4 3.2 %collective-permute-start.55 = (bf16[512,128]{1,0:T(8,128)(2,1)}, bf16[512,128]{1,0:T(8,128)(2,1)S(1)}, u32[]{:S(2)}, u32[]{:S(2)}) collective-permute-start(bf16[512,128]{1,0:T(8,128)(2,1)} %get-tuple-element.45), channel_id=1, source_target_pairs={{0,3},{1,0},{2,1},{3,2},{4,7},{5,4},{6,5},{7,6},{8,11},{9,8},{10,9... | collective-permute-start | bytes 393224 | tf_op jit(solution)/shard_map/ppermute | solution.py:527
  193.6 0.9 collective-permute-done.57
  194.5 1.0 add_convert_fusion.1
  195.4 3.6 %collective-permute-start.58 = (bf16[512,128]{1,0:T(8,128)(2,1)S(1)}, bf16[512,128]{1,0:T(8,128)(2,1)S(1)}, u32[]{:S(2)}, u32[]{:S(2)}) collective-permute-start(bf16[512,128]{1,0:T(8,128)(2,1)S(1)} %add_convert_fusion.1), channel_id=1, source_target_pairs={{0,3},{1,0},{2,1},{3,2},{4,7},{5,4},{6,5},{7,6},{8,11},{9,8},{10,9... | collective-permute-start | bytes 393224 | tf_op jit(solution)/shard_map/ppermute | solution.py:527
  199.1 1.0 add_convert_fusion.3
  200.7 1.3 collective-permute-done.58
  202.1 4.5 %collective-permute-done.54 = bf16[512,128]{1,0:T(8,128)(2,1)S(1)} collective-permute-done((bf16[512,128]{1,0:T(8,128)(2,1)S(1)}, bf16[512,128]{1,0:T(8,128)(2,1)S(1)}, u32[]{:S(2)}, u32[]{:S(2)}) %collective-permute-start.54) | collective-permute-done | bytes 131104 | tf_op jit(solution)/shard_map/ppermute | solution.py:527
  206.7 0.7 pad_maximum_fusion.2
  (158 shorter events, 8.1 us)
Async XLA Ops:
  1.6 7.4 %collective-permute-start = (bf16[512,128]{1,0:T(8,128)(2,1)S(1)}, bf16[512,128]{1,0:T(8,128)(2,1)S(1)}, u32[]{:S(2)}, u32[]{:S(2)}) collective-permute-start(bf16[512,128]{1,0:T(8,128)(2,1)S(1)} %get-tuple-element.58), channel_id=1, source_target_pairs={{0,4},{4,0},{8,12},{12,8},{16,20},{20,16},{24,28},{28,24},{32,36},... | collective-permute-start | bytes 393224 | tf_op jit(solution)/shard_map/ppermute | solution.py:494
  9.0 12.1 %collective-permute-start.1 = (bf16[1024,128]{1,0:T(8,128)(2,1)S(1)}, bf16[1024,128]{1,0:T(8,128)(2,1)S(1)}, u32[]{:S(2)}, u32[]{:S(2)}) collective-permute-start(bf16[1024,128]{1,0:T(8,128)(2,1)S(1)} %pad_maximum_fusion), channel_id=1, source_target_pairs={{0,8},{4,36},{8,16},{12,44},{16,24},{20,52},{24,0},{28,60},{32,40}... | collective-permute-start | bytes 786440 | tf_op jit(solution)/shard_map/ppermute | solution.py:488
  11.1 25.1 %all-to-all-start = ((bf16[32,80,128]{2,1,0:T(8,128)(2,1)}), bf16[32,80,128]{2,1,0:T(8,128)(2,1)S(1)}, u32[]{:S(2)}, u32[]{:S(2)}) async-start(bf16[32,80,128]{2,1,0:T(8,128)(2,1)} %get-tuple-element.33), calls=%async_computation | async-start | bytes 1310720 | tf_op jit(solution)/shard_map/all_to_all | solution.py:536
  18.1 12.7 %collective-permute-start.3 = (bf16[1024,128]{1,0:T(8,128)(2,1)S(1)}, bf16[1024,128]{1,0:T(8,128)(2,1)S(1)}, u32[]{:S(2)}, u32[]{:S(2)}) collective-permute-start(bf16[1024,128]{1,0:T(8,128)(2,1)S(1)} %pad_maximum_fusion), channel_id=1, source_target_pairs={{0,24},{4,100},{8,0},{12,108},{16,8},{20,116},{24,16},{28,124},{32... | collective-permute-start | bytes 786440 | tf_op jit(solution)/shard_map/ppermute | solution.py:491
  21.2 14.9 %collective-permute-start.2 = (bf16[512,128]{1,0:T(8,128)(2,1)S(1)}, bf16[512,128]{1,0:T(8,128)(2,1)S(1)}, u32[]{:S(2)}, u32[]{:S(2)}) collective-permute-start(bf16[512,128]{1,0:T(8,128)(2,1)S(1)} %slice.47), channel_id=1, source_target_pairs={{0,8},{4,36},{8,16},{12,44},{16,24},{20,52},{24,0},{28,60},{32,40}... | collective-permute-start | bytes 393224 | tf_op jit(solution)/shard_map/ppermute | solution.py:488
  30.8 5.3 %collective-permute-start.4 = (bf16[512,128]{1,0:T(8,128)(2,1)S(1)}, bf16[512,128]{1,0:T(8,128)(2,1)S(1)}, u32[]{:S(2)}, u32[]{:S(2)}) collective-permute-start(bf16[512,128]{1,0:T(8,128)(2,1)S(1)} %slice.48), channel_id=1, source_target_pairs={{0,24},{4,100},{8,0},{12,108},{16,8},{20,116},{24,16},{28,124},{32... | collective-permute-start | bytes 393224 | tf_op jit(solution)/shard_map/ppermute | solution.py:491
  32.5 10.6 %collective-permute-start.11 = (bf16[2048,128]{1,0:T(8,128)(2,1)S(1)}, bf16[2048,128]{1,0:T(8,128)(2,1)}, u32[]{:S(2)}, u32[]{:S(2)}) collective-permute-start(bf16[2048,128]{1,0:T(8,128)(2,1)S(1)} %constant_dynamic-update-slice_fusion.3), channel_id=1, source_target_pairs={{0,32},{4,12},{8,40},{12,20},{16,48},{20,28},{24,56},{28,4},{32,64... | collective-permute-start | bytes 1572872 | tf_op jit(solution)/shard_map/ppermute | solution.py:488
  34.3 10.5 %collective-permute-start.16 = (bf16[2048,128]{1,0:T(8,128)(2,1)S(1)}, bf16[2048,128]{1,0:T(8,128)(2,1)S(1)}, u32[]{:S(2)}, u32[]{:S(2)}) collective-permute-start(bf16[2048,128]{1,0:T(8,128)(2,1)S(1)} %constant_dynamic-update-slice_fusion.3), channel_id=1, source_target_pairs={{0,96},{4,28},{8,104},{12,4},{16,112},{20,12},{24,120},{28,20},{32... | collective-permute-start | bytes 1572872 | tf_op jit(solution)/shard_map/ppermute | solution.py:491
  35.8 9.3 %collective-permute-start.17 = (bf16[2048,128]{1,0:T(8,128)(2,1)S(1)}, bf16[2048,128]{1,0:T(8,128)(2,1)}, u32[]{:S(2)}, u32[]{:S(2)}) collective-permute-start(bf16[2048,128]{1,0:T(8,128)(2,1)S(1)} %constant_dynamic-update-slice_fusion.3), channel_id=1, source_target_pairs={{0,4},{4,0},{8,12},{12,8},{16,20},{20,16},{24,28},{28,24},{32,36},... | collective-permute-start | bytes 1572872 | tf_op jit(solution)/shard_map/ppermute | solution.py:494
  36.2 36.3 %copy-start.3 = (bf16[32,80,128]{2,1,0:T(8,128)(2,1)}, bf16[32,80,128]{2,1,0:T(8,128)(2,1)S(1)}, u32[]{:S(2)}) copy-start(bf16[32,80,128]{2,1,0:T(8,128)(2,1)S(1)} %all-to-all-done.refs_4_) | copy-start | bytes 1966084
  36.2 36.2 %copy-start.4 = (bf16[16,64,128]{2,1,0:T(8,128)(2,1)}, bf16[16,64,128]{2,1,0:T(8,128)(2,1)S(1)}, u32[]{:S(2)}) copy-start(bf16[16,64,128]{2,1,0:T(8,128)(2,1)S(1)} %get-tuple-element.51) | copy-start | bytes 786436
  36.3 10.8 %collective-permute-start.5 = (bf16[16,64,128]{2,1,0:T(8,128)(2,1)S(1)}, bf16[16,64,128]{2,1,0:T(8,128)(2,1)S(1)}, u32[]{:S(2)}, u32[]{:S(2)}) collective-permute-start(bf16[16,64,128]{2,1,0:T(8,128)(2,1)S(1)} %get-tuple-element.52), channel_id=1, source_target_pairs={{0,1},{1,2},{2,3},{3,0},{4,5},{5,6},{6,7},{7,4},{8,9},{9,10},{10,1... | collective-permute-start | bytes 786440 | tf_op jit(solution)/shard_map/ppermute | solution.py:527
  38.2 8.9 %collective-permute-start.8 = (bf16[16,64,128]{2,1,0:T(8,128)(2,1)S(1)}, bf16[16,64,128]{2,1,0:T(8,128)(2,1)}, u32[]{:S(2)}, u32[]{:S(2)}) collective-permute-start(bf16[16,64,128]{2,1,0:T(8,128)(2,1)S(1)} %get-tuple-element.51), channel_id=1, source_target_pairs={{0,3},{1,0},{2,1},{3,2},{4,7},{5,4},{6,5},{7,6},{8,11},{9,8},{10,9... | collective-permute-start | bytes 786440 | tf_op jit(solution)/shard_map/ppermute | solution.py:527
  43.1 14.1 %collective-permute-start.14 = (bf16[2048,128]{1,0:T(8,128)(2,1)S(1)}, bf16[2048,128]{1,0:T(8,128)(2,1)}, u32[]{:S(2)}, u32[]{:S(2)}) collective-permute-start(bf16[2048,128]{1,0:T(8,128)(2,1)S(1)} %constant_dynamic-update-slice_fusion), channel_id=1, source_target_pairs={{0,96},{4,28},{8,104},{12,4},{16,112},{20,12},{24,120},{28,20},{32... | collective-permute-start | bytes 1572872 | tf_op jit(solution)/shard_map/ppermute | solution.py:491
  44.8 14.8 %collective-permute-start.12 = (bf16[2048,128]{1,0:T(8,128)(2,1)S(1)}, bf16[2048,128]{1,0:T(8,128)(2,1)S(1)}, u32[]{:S(2)}, u32[]{:S(2)}) collective-permute-start(bf16[2048,128]{1,0:T(8,128)(2,1)S(1)} %constant_dynamic-update-slice_fusion), channel_id=1, source_target_pairs={{0,32},{4,12},{8,40},{12,20},{16,48},{20,28},{24,56},{28,4},{32,64... | collective-permute-start | bytes 1572872 | tf_op jit(solution)/shard_map/ppermute | solution.py:488
  45.1 15.3 %collective-permute-start.18 = (bf16[2048,128]{1,0:T(8,128)(2,1)S(1)}, bf16[2048,128]{1,0:T(8,128)(2,1)S(1)}, u32[]{:S(2)}, u32[]{:S(2)}) collective-permute-start(bf16[2048,128]{1,0:T(8,128)(2,1)S(1)} %constant_dynamic-update-slice_fusion), channel_id=1, source_target_pairs={{0,4},{4,0},{8,12},{12,8},{16,20},{20,16},{24,28},{28,24},{32,36},... | collective-permute-start | bytes 1572872 | tf_op jit(solution)/shard_map/ppermute | solution.py:494
  47.1 9.2 %collective-permute-start.6 = (bf16[16,64,128]{2,1,0:T(8,128)(2,1)S(1)}, bf16[16,64,128]{2,1,0:T(8,128)(2,1)S(1)}, u32[]{:S(2)}, u32[]{:S(2)}) collective-permute-start(bf16[16,64,128]{2,1,0:T(8,128)(2,1)S(1)} %get-tuple-element.51), channel_id=1, source_target_pairs={{0,1},{1,2},{2,3},{3,0},{4,5},{5,6},{6,7},{7,4},{8,9},{9,10},{10,1... | collective-permute-start | bytes 786440 | tf_op jit(solution)/shard_map/ppermute | solution.py:527
  47.1 10.0 %collective-permute-start.7 = (bf16[16,64,128]{2,1,0:T(8,128)(2,1)S(1)}, bf16[16,64,128]{2,1,0:T(8,128)(2,1)S(1)}, u32[]{:S(2)}, u32[]{:S(2)}) collective-permute-start(bf16[16,64,128]{2,1,0:T(8,128)(2,1)S(1)} %get-tuple-element.52), channel_id=1, source_target_pairs={{0,3},{1,0},{2,1},{3,2},{4,7},{5,4},{6,5},{7,6},{8,11},{9,8},{10,9... | collective-permute-start | bytes 786440 | tf_op jit(solution)/shard_map/ppermute | solution.py:527
  56.2 16.8 %collective-permute-start.13 = (bf16[2048,128]{1,0:T(8,128)(2,1)}, bf16[2048,128]{1,0:T(8,128)(2,1)}, u32[]{:S(2)}, u32[]{:S(2)}) collective-permute-start(bf16[2048,128]{1,0:T(8,128)(2,1)} %collective-permute-done.11), channel_id=1, source_target_pairs={{0,32},{4,12},{8,40},{12,20},{16,48},{20,28},{24,56},{28,4},{32,64... | collective-permute-start | bytes 1572872 | tf_op jit(solution)/shard_map/ppermute | solution.py:488
  57.1 16.0 %collective-permute-start.19 = (bf16[2048,128]{1,0:T(8,128)(2,1)}, bf16[2048,128]{1,0:T(8,128)(2,1)}, u32[]{:S(2)}, u32[]{:S(2)}) collective-permute-start(bf16[2048,128]{1,0:T(8,128)(2,1)} %collective-permute-done.11), channel_id=1, source_target_pairs={{0,4},{4,0},{8,12},{12,8},{16,20},{20,16},{24,28},{28,24},{32,36},... | collective-permute-start | bytes 1572872 | tf_op jit(solution)/shard_map/ppermute | solution.py:494
  57.2 16.4 %collective-permute-start.15 = (bf16[2048,128]{1,0:T(8,128)(2,1)}, bf16[2048,128]{1,0:T(8,128)(2,1)}, u32[]{:S(2)}, u32[]{:S(2)}) collective-permute-start(bf16[2048,128]{1,0:T(8,128)(2,1)} %collective-permute-done.14), channel_id=1, source_target_pairs={{0,96},{4,28},{8,104},{12,4},{16,112},{20,12},{24,120},{28,20},{32... | collective-permute-start | bytes 1572872 | tf_op jit(solution)/shard_map/ppermute | solution.py:491
  59.6 12.9 %collective-permute-start.9 = (bf16[16,64,128]{2,1,0:T(8,128)(2,1)S(1)}, bf16[16,64,128]{2,1,0:T(8,128)(2,1)}, u32[]{:S(2)}, u32[]{:S(2)}) collective-permute-start(bf16[16,64,128]{2,1,0:T(8,128)(2,1)S(1)} %collective-permute-done.5), channel_id=1, source_target_pairs={{0,1},{1,2},{2,3},{3,0},{4,5},{5,6},{6,7},{7,4},{8,9},{9,10},{10,1... | collective-permute-start | bytes 786440 | tf_op jit(solution)/shard_map/ppermute | solution.py:527
  61.3 11.3 %collective-permute-start.10 = (bf16[16,64,128]{2,1,0:T(8,128)(2,1)}, bf16[16,64,128]{2,1,0:T(8,128)(2,1)}, u32[]{:S(2)}, u32[]{:S(2)}) collective-permute-start(bf16[16,64,128]{2,1,0:T(8,128)(2,1)} %collective-permute-done.8), channel_id=1, source_target_pairs={{0,3},{1,0},{2,1},{3,2},{4,7},{5,4},{6,5},{7,6},{8,11},{9,8},{10,9... | collective-permute-start | bytes 786440 | tf_op jit(solution)/shard_map/ppermute | solution.py:527
  72.5 5.9 %collective-permute-start.23 = (bf16[2048,128]{1,0:T(8,128)(2,1)}, bf16[2048,128]{1,0:T(8,128)(2,1)S(1)}, u32[]{:S(2)}, u32[]{:S(2)}) collective-permute-start(bf16[2048,128]{1,0:T(8,128)(2,1)} %copy-done.20), channel_id=1, source_target_pairs={{0,4},{4,0},{8,12},{12,8},{16,20},{20,16},{24,28},{28,24},{32,36},... | collective-permute-start | bytes 1572872 | tf_op jit(solution)/shard_map/ppermute | solution.py:494
  72.6 9.0 %collective-permute-start.24 = (bf16[2048,128]{1,0:T(8,128)(2,1)}, bf16[2048,128]{1,0:T(8,128)(2,1)S(1)}, u32[]{:S(2)}, u32[]{:S(2)}) collective-permute-start(bf16[2048,128]{1,0:T(8,128)(2,1)} %collective-permute-done.14), channel_id=1, source_target_pairs={{0,4},{4,0},{8,12},{12,8},{16,20},{20,16},{24,28},{28,24},{32,36},... | collective-permute-start | bytes 1572872 | tf_op jit(solution)/shard_map/ppermute | solution.py:494
  73.1 5.3 %collective-permute-start.20 = (bf16[2048,128]{1,0:T(8,128)(2,1)}, bf16[2048,128]{1,0:T(8,128)(2,1)S(1)}, u32[]{:S(2)}, u32[]{:S(2)}) collective-permute-start(bf16[2048,128]{1,0:T(8,128)(2,1)} %copy-done.21), channel_id=1, source_target_pairs={{0,4},{4,0},{8,12},{12,8},{16,20},{20,16},{24,28},{28,24},{32,36},... | collective-permute-start | bytes 1572872 | tf_op jit(solution)/shard_map/ppermute | solution.py:494
  73.2 8.4 %collective-permute-start.21 = (bf16[2048,128]{1,0:T(8,128)(2,1)}, bf16[2048,128]{1,0:T(8,128)(2,1)S(1)}, u32[]{:S(2)}, u32[]{:S(2)}) collective-permute-start(bf16[2048,128]{1,0:T(8,128)(2,1)} %collective-permute-done.13), channel_id=1, source_target_pairs={{0,4},{4,0},{8,12},{12,8},{16,20},{20,16},{24,28},{28,24},{32,36},... | collective-permute-start | bytes 1572872 | tf_op jit(solution)/shard_map/ppermute | solution.py:494
  73.6 8.8 %collective-permute-start.22 = (bf16[2048,128]{1,0:T(8,128)(2,1)}, bf16[2048,128]{1,0:T(8,128)(2,1)S(1)}, u32[]{:S(2)}, u32[]{:S(2)}) collective-permute-start(bf16[2048,128]{1,0:T(8,128)(2,1)} %collective-permute-done.15), channel_id=1, source_target_pairs={{0,4},{4,0},{8,12},{12,8},{16,20},{20,16},{24,28},{28,24},{32,36},... | collective-permute-start | bytes 1572872 | tf_op jit(solution)/shard_map/ppermute | solution.py:494
  78.3 18.7 %collective-permute-start.31 = (bf16[1024,128]{1,0:T(8,128)(2,1)S(1)}, bf16[1024,128]{1,0:T(8,128)(2,1)S(1)}, u32[]{:S(2)}, u32[]{:S(2)}) collective-permute-start(bf16[1024,128]{1,0:T(8,128)(2,1)S(1)} %copy-done.2), channel_id=1, source_target_pairs={{0,1},{1,2},{2,3},{3,0},{4,5},{5,6},{6,7},{7,4},{8,9},{9,10},{10,1... | collective-permute-start | bytes 786440 | tf_op jit(solution)/shard_map/ppermute | solution.py:527
  78.4 20.2 %collective-permute-start.32 = (bf16[1024,128]{1,0:T(8,128)(2,1)S(1)}, bf16[1024,128]{1,0:T(8,128)(2,1)S(1)}, u32[]{:S(2)}, u32[]{:S(2)}) collective-permute-start(bf16[1024,128]{1,0:T(8,128)(2,1)S(1)} %copy-done.2), channel_id=1, source_target_pairs={{0,3},{1,0},{2,1},{3,2},{4,7},{5,4},{6,5},{7,6},{8,11},{9,8},{10,9... | collective-permute-start | bytes 786440 | tf_op jit(solution)/shard_map/ppermute | solution.py:527
  93.7 16.2 %collective-permute-start.25 = (bf16[1024,128]{1,0:T(8,128)(2,1)}, bf16[1024,128]{1,0:T(8,128)(2,1)S(1)}, u32[]{:S(2)}, u32[]{:S(2)}) collective-permute-start(bf16[1024,128]{1,0:T(8,128)(2,1)} %get-tuple-element.35.refs_0_), channel_id=1, source_target_pairs={{0,1},{1,2},{2,3},{3,0},{4,5},{5,6},{6,7},{7,4},{8,9},{9,10},{10,1... | collective-permute-start | bytes 786440 | tf_op jit(solution)/shard_map/ppermute | solution.py:527
  93.8 16.2 %collective-permute-start.29 = (bf16[1024,128]{1,0:T(8,128)(2,1)}, bf16[1024,128]{1,0:T(8,128)(2,1)S(1)}, u32[]{:S(2)}, u32[]{:S(2)}) collective-permute-start(bf16[1024,128]{1,0:T(8,128)(2,1)} %get-tuple-element.36.refs_4_), channel_id=1, source_target_pairs={{0,3},{1,0},{2,1},{3,2},{4,7},{5,4},{6,5},{7,6},{8,11},{9,8},{10,9... | collective-permute-start | bytes 786440 | tf_op jit(solution)/shard_map/ppermute | solution.py:527
  97.0 16.2 %collective-permute-start.33 = (bf16[1024,128]{1,0:T(8,128)(2,1)S(1)}, bf16[1024,128]{1,0:T(8,128)(2,1)S(1)}, u32[]{:S(2)}, u32[]{:S(2)}) collective-permute-start(bf16[1024,128]{1,0:T(8,128)(2,1)S(1)} %copy-done.2), channel_id=1, source_target_pairs={{0,2},{1,3},{2,0},{3,1},{4,6},{5,7},{6,4},{7,5},{8,10},{9,11},{10,... | collective-permute-start | bytes 786440 | tf_op jit(solution)/shard_map/ppermute | solution.py:527
  97.0 18.2 %collective-permute-start.26 = (bf16[1024,128]{1,0:T(8,128)(2,1)}, bf16[1024,128]{1,0:T(8,128)(2,1)S(1)}, u32[]{:S(2)}, u32[]{:S(2)}) collective-permute-start(bf16[1024,128]{1,0:T(8,128)(2,1)} %get-tuple-element.35.refs_0_), channel_id=1, source_target_pairs={{0,3},{1,0},{2,1},{3,2},{4,7},{5,4},{6,5},{7,6},{8,11},{9,8},{10,9... | collective-permute-start | bytes 786440 | tf_op jit(solution)/shard_map/ppermute | solution.py:527
  98.5 17.0 %collective-permute-start.28 = (bf16[1024,128]{1,0:T(8,128)(2,1)}, bf16[1024,128]{1,0:T(8,128)(2,1)S(1)}, u32[]{:S(2)}, u32[]{:S(2)}) collective-permute-start(bf16[1024,128]{1,0:T(8,128)(2,1)} %get-tuple-element.36.refs_4_), channel_id=1, source_target_pairs={{0,1},{1,2},{2,3},{3,0},{4,5},{5,6},{6,7},{7,4},{8,9},{9,10},{10,1... | collective-permute-start | bytes 786440 | tf_op jit(solution)/shard_map/ppermute | solution.py:527
  109.9 10.7 %collective-permute-start.27 = (bf16[1024,128]{1,0:T(8,128)(2,1)S(1)}, bf16[1024,128]{1,0:T(8,128)(2,1)S(1)}, u32[]{:S(2)}, u32[]{:S(2)}) collective-permute-start(bf16[1024,128]{1,0:T(8,128)(2,1)S(1)} %collective-permute-done.25.refs_1_), channel_id=1, source_target_pairs={{0,1},{1,2},{2,3},{3,0},{4,5},{5,6},{6,7},{7,4},{8,9},{9,10},{10,1... | collective-permute-start | bytes 786440 | tf_op jit(solution)/shard_map/ppermute | solution.py:527
  109.9 11.4 %collective-permute-start.30 = (bf16[1024,128]{1,0:T(8,128)(2,1)S(1)}, bf16[1024,128]{1,0:T(8,128)(2,1)}, u32[]{:S(2)}, u32[]{:S(2)}) collective-permute-start(bf16[1024,128]{1,0:T(8,128)(2,1)S(1)} %collective-permute-done.29.refs_6_), channel_id=1, source_target_pairs={{0,3},{1,0},{2,1},{3,2},{4,7},{5,4},{6,5},{7,6},{8,11},{9,8},{10,9... | collective-permute-start | bytes 786440 | tf_op jit(solution)/shard_map/ppermute | solution.py:527
  126.7 4.2 %collective-permute-start.34 = (bf16[512,128]{1,0:T(8,128)(2,1)S(1)}, bf16[512,128]{1,0:T(8,128)(2,1)S(1)}, u32[]{:S(2)}, u32[]{:S(2)}) collective-permute-start(bf16[512,128]{1,0:T(8,128)(2,1)S(1)} %get-tuple-element.56), channel_id=1, source_target_pairs={{0,4},{4,0},{8,12},{12,8},{16,20},{20,16},{24,28},{28,24},{32,36},... | collective-permute-start | bytes 393224 | tf_op jit(solution)/shard_map/ppermute | solution.py:494
  131.0 41.9 %copy-start.1 = (bf16[1024,128]{1,0:T(8,128)(2,1)S(1)}, bf16[1024,128]{1,0:T(8,128)(2,1)}, u32[]{:S(2)}) copy-start(bf16[1024,128]{1,0:T(8,128)(2,1)} %get-tuple-element.40.refs_12_.refs_4_) | copy-start | bytes 786436
  131.0 7.7 %collective-permute-start.35 = (bf16[1024,128]{1,0:T(8,128)(2,1)S(1)}, bf16[1024,128]{1,0:T(8,128)(2,1)S(1)}, u32[]{:S(2)}, u32[]{:S(2)}) collective-permute-start(bf16[1024,128]{1,0:T(8,128)(2,1)S(1)} %pad_maximum_fusion.1), channel_id=1, source_target_pairs={{0,8},{4,36},{8,16},{12,44},{16,24},{20,52},{24,0},{28,60},{32,40}... | collective-permute-start | bytes 786440 | tf_op jit(solution)/shard_map/ppermute | solution.py:488
  131.1 7.7 %collective-permute-start.37 = (bf16[1024,128]{1,0:T(8,128)(2,1)S(1)}, bf16[1024,128]{1,0:T(8,128)(2,1)S(1)}, u32[]{:S(2)}, u32[]{:S(2)}) collective-permute-start(bf16[1024,128]{1,0:T(8,128)(2,1)S(1)} %pad_maximum_fusion.1), channel_id=1, source_target_pairs={{0,24},{4,100},{8,0},{12,108},{16,8},{20,116},{24,16},{28,124},{32... | collective-permute-start | bytes 786440 | tf_op jit(solution)/shard_map/ppermute | solution.py:491
  138.7 6.8 %collective-permute-start.36 = (bf16[512,128]{1,0:T(8,128)(2,1)S(1)}, bf16[512,128]{1,0:T(8,128)(2,1)S(1)}, u32[]{:S(2)}, u32[]{:S(2)}) collective-permute-start(bf16[512,128]{1,0:T(8,128)(2,1)S(1)} %slice.51), channel_id=1, source_target_pairs={{0,8},{4,36},{8,16},{12,44},{16,24},{20,52},{24,0},{28,60},{32,40}... | collective-permute-start | bytes 393224 | tf_op jit(solution)/shard_map/ppermute | solution.py:488
  138.8 7.3 %collective-permute-start.38 = (bf16[512,128]{1,0:T(8,128)(2,1)S(1)}, bf16[512,128]{1,0:T(8,128)(2,1)S(1)}, u32[]{:S(2)}, u32[]{:S(2)}) collective-permute-start(bf16[512,128]{1,0:T(8,128)(2,1)S(1)} %slice.52), channel_id=1, source_target_pairs={{0,24},{4,100},{8,0},{12,108},{16,8},{20,116},{24,16},{28,124},{32... | collective-permute-start | bytes 393224 | tf_op jit(solution)/shard_map/ppermute | solution.py:491
  142.1 10.6 %collective-permute-start.39 = (bf16[2048,128]{1,0:T(8,128)(2,1)S(1)}, bf16[2048,128]{1,0:T(8,128)(2,1)}, u32[]{:S(2)}, u32[]{:S(2)}) collective-permute-start(bf16[2048,128]{1,0:T(8,128)(2,1)S(1)} %constant_dynamic-update-slice_fusion.5), channel_id=1, source_target_pairs={{0,32},{4,12},{8,40},{12,20},{16,48},{20,28},{24,56},{28,4},{32,64... | collective-permute-start | bytes 1572872 | tf_op jit(solution)/shard_map/ppermute | solution.py:488
  142.2 10.5 %collective-permute-start.44 = (bf16[2048,128]{1,0:T(8,128)(2,1)S(1)}, bf16[2048,128]{1,0:T(8,128)(2,1)S(1)}, u32[]{:S(2)}, u32[]{:S(2)}) collective-permute-start(bf16[2048,128]{1,0:T(8,128)(2,1)S(1)} %constant_dynamic-update-slice_fusion.5), channel_id=1, source_target_pairs={{0,96},{4,28},{8,104},{12,4},{16,112},{20,12},{24,120},{28,20},{32... | collective-permute-start | bytes 1572872 | tf_op jit(solution)/shard_map/ppermute | solution.py:491
  145.4 7.7 %collective-permute-start.45 = (bf16[2048,128]{1,0:T(8,128)(2,1)S(1)}, bf16[2048,128]{1,0:T(8,128)(2,1)S(1)}, u32[]{:S(2)}, u32[]{:S(2)}) collective-permute-start(bf16[2048,128]{1,0:T(8,128)(2,1)S(1)} %constant_dynamic-update-slice_fusion.5), channel_id=1, source_target_pairs={{0,4},{4,0},{8,12},{12,8},{16,20},{20,16},{24,28},{28,24},{32,36},... | collective-permute-start | bytes 1572872 | tf_op jit(solution)/shard_map/ppermute | solution.py:494
  147.5 10.4 %collective-permute-start.42 = (bf16[2048,128]{1,0:T(8,128)(2,1)}, bf16[2048,128]{1,0:T(8,128)(2,1)}, u32[]{:S(2)}, u32[]{:S(2)}) collective-permute-start(bf16[2048,128]{1,0:T(8,128)(2,1)} %constant_dynamic-update-slice_fusion.7), channel_id=1, source_target_pairs={{0,96},{4,28},{8,104},{12,4},{16,112},{20,12},{24,120},{28,20},{32... | collective-permute-start | bytes 1572872 | tf_op jit(solution)/shard_map/ppermute | solution.py:491
  147.5 18.0 %collective-permute-start.40 = (bf16[2048,128]{1,0:T(8,128)(2,1)}, bf16[2048,128]{1,0:T(8,128)(2,1)}, u32[]{:S(2)}, u32[]{:S(2)}) collective-permute-start(bf16[2048,128]{1,0:T(8,128)(2,1)} %constant_dynamic-update-slice_fusion.7), channel_id=1, source_target_pairs={{0,32},{4,12},{8,40},{12,20},{16,48},{20,28},{24,56},{28,4},{32,64... | collective-permute-start | bytes 1572872 | tf_op jit(solution)/shard_map/ppermute | solution.py:488
  152.7 13.0 %collective-permute-start.46 = (bf16[2048,128]{1,0:T(8,128)(2,1)}, bf16[2048,128]{1,0:T(8,128)(2,1)}, u32[]{:S(2)}, u32[]{:S(2)}) collective-permute-start(bf16[2048,128]{1,0:T(8,128)(2,1)} %constant_dynamic-update-slice_fusion.7), channel_id=1, source_target_pairs={{0,4},{4,0},{8,12},{12,8},{16,20},{20,16},{24,28},{28,24},{32,36},... | collective-permute-start | bytes 1572872 | tf_op jit(solution)/shard_map/ppermute | solution.py:494
  152.7 13.4 %collective-permute-start.41 = (bf16[2048,128]{1,0:T(8,128)(2,1)}, bf16[2048,128]{1,0:T(8,128)(2,1)}, u32[]{:S(2)}, u32[]{:S(2)}) collective-permute-start(bf16[2048,128]{1,0:T(8,128)(2,1)} %collective-permute-done.39), channel_id=1, source_target_pairs={{0,32},{4,12},{8,40},{12,20},{16,48},{20,28},{24,56},{28,4},{32,64... | collective-permute-start | bytes 1572872 | tf_op jit(solution)/shard_map/ppermute | solution.py:488
  153.5 12.7 %collective-permute-start.47 = (bf16[2048,128]{1,0:T(8,128)(2,1)}, bf16[2048,128]{1,0:T(8,128)(2,1)}, u32[]{:S(2)}, u32[]{:S(2)}) collective-permute-start(bf16[2048,128]{1,0:T(8,128)(2,1)} %collective-permute-done.39), channel_id=1, source_target_pairs={{0,4},{4,0},{8,12},{12,8},{16,20},{20,16},{24,28},{28,24},{32,36},... | collective-permute-start | bytes 1572872 | tf_op jit(solution)/shard_map/ppermute | solution.py:494
  157.9 15.1 %collective-permute-start.43 = (bf16[2048,128]{1,0:T(8,128)(2,1)}, bf16[2048,128]{1,0:T(8,128)(2,1)}, u32[]{:S(2)}, u32[]{:S(2)}) collective-permute-start(bf16[2048,128]{1,0:T(8,128)(2,1)} %collective-permute-done.42), channel_id=1, source_target_pairs={{0,96},{4,28},{8,104},{12,4},{16,112},{20,12},{24,120},{28,20},{32... | collective-permute-start | bytes 1572872 | tf_op jit(solution)/shard_map/ppermute | solution.py:491
  161.6 28.7 %all-to-all-start.1 = ((f32[32,48,128]{2,1,0:T(8,128)}), f32[32,48,128]{2,1,0:T(8,128)S(1)}, u32[]{:S(2)}, u32[]{:S(2)}) async-start(f32[32,48,128]{2,1,0:T(8,128)} %slopes.1), calls=%async_computation.1 | async-start | bytes 1572864 | tf_op jit(solution)/shard_map/all_to_all | solution.py:578
  165.5 10.5 %collective-permute-start.51 = (bf16[2048,128]{1,0:T(8,128)(2,1)}, bf16[2048,128]{1,0:T(8,128)(2,1)S(1)}, u32[]{:S(2)}, u32[]{:S(2)}) collective-permute-start(bf16[2048,128]{1,0:T(8,128)(2,1)} %copy-done.28), channel_id=1, source_target_pairs={{0,4},{4,0},{8,12},{12,8},{16,20},{20,16},{24,28},{28,24},{32,36},... | collective-permute-start | bytes 1572872 | tf_op jit(solution)/shard_map/ppermute | solution.py:494
  165.7 10.3 %collective-permute-start.52 = (bf16[2048,128]{1,0:T(8,128)(2,1)}, bf16[2048,128]{1,0:T(8,128)(2,1)}, u32[]{:S(2)}, u32[]{:S(2)}) collective-permute-start(bf16[2048,128]{1,0:T(8,128)(2,1)} %collective-permute-done.42), channel_id=1, source_target_pairs={{0,4},{4,0},{8,12},{12,8},{16,20},{20,16},{24,28},{28,24},{32,36},... | collective-permute-start | bytes 1572872 | tf_op jit(solution)/shard_map/ppermute | solution.py:494
  166.1 9.9 %collective-permute-start.48 = (bf16[2048,128]{1,0:T(8,128)(2,1)}, bf16[2048,128]{1,0:T(8,128)(2,1)}, u32[]{:S(2)}, u32[]{:S(2)}) collective-permute-start(bf16[2048,128]{1,0:T(8,128)(2,1)} %collective-permute-done.40), channel_id=1, source_target_pairs={{0,4},{4,0},{8,12},{12,8},{16,20},{20,16},{24,28},{28,24},{32,36},... | collective-permute-start | bytes 1572872 | tf_op jit(solution)/shard_map/ppermute | solution.py:494
  166.2 9.8 %collective-permute-start.49 = (bf16[2048,128]{1,0:T(8,128)(2,1)}, bf16[2048,128]{1,0:T(8,128)(2,1)}, u32[]{:S(2)}, u32[]{:S(2)}) collective-permute-start(bf16[2048,128]{1,0:T(8,128)(2,1)} %collective-permute-done.41), channel_id=1, source_target_pairs={{0,4},{4,0},{8,12},{12,8},{16,20},{20,16},{24,28},{28,24},{32,36},... | collective-permute-start | bytes 1572872 | tf_op jit(solution)/shard_map/ppermute | solution.py:494
  172.9 3.1 %collective-permute-start.50 = (bf16[2048,128]{1,0:T(8,128)(2,1)}, bf16[2048,128]{1,0:T(8,128)(2,1)}, u32[]{:S(2)}, u32[]{:S(2)}) collective-permute-start(bf16[2048,128]{1,0:T(8,128)(2,1)} %collective-permute-done.43), channel_id=1, source_target_pairs={{0,4},{4,0},{8,12},{12,8},{16,20},{20,16},{24,28},{28,24},{32,36},... | collective-permute-start | bytes 1572872 | tf_op jit(solution)/shard_map/ppermute | solution.py:494
  187.8 6.6 %collective-permute-start.57 = (bf16[512,128]{1,0:T(8,128)(2,1)}, bf16[512,128]{1,0:T(8,128)(2,1)S(1)}, u32[]{:S(2)}, u32[]{:S(2)}) collective-permute-start(bf16[512,128]{1,0:T(8,128)(2,1)} %get-tuple-element.48), channel_id=1, source_target_pairs={{0,3},{1,0},{2,1},{3,2},{4,7},{5,4},{6,5},{7,6},{8,11},{9,8},{10,9... | collective-permute-start | bytes 393224 | tf_op jit(solution)/shard_map/ppermute | solution.py:527
  190.3 8.8 %collective-permute-start.53 = (bf16[512,128]{1,0:T(8,128)(2,1)}, bf16[512,128]{1,0:T(8,128)(2,1)S(1)}, u32[]{:S(2)}, u32[]{:S(2)}) collective-permute-start(bf16[512,128]{1,0:T(8,128)(2,1)} %get-tuple-element.44), channel_id=1, source_target_pairs={{0,1},{1,2},{2,3},{3,0},{4,5},{5,6},{6,7},{7,4},{8,9},{9,10},{10,1... | collective-permute-start | bytes 393224 | tf_op jit(solution)/shard_map/ppermute | solution.py:527
  190.4 10.4 %collective-permute-start.55 = (bf16[512,128]{1,0:T(8,128)(2,1)}, bf16[512,128]{1,0:T(8,128)(2,1)S(1)}, u32[]{:S(2)}, u32[]{:S(2)}) collective-permute-start(bf16[512,128]{1,0:T(8,128)(2,1)} %get-tuple-element.45), channel_id=1, source_target_pairs={{0,3},{1,0},{2,1},{3,2},{4,7},{5,4},{6,5},{7,6},{8,11},{9,8},{10,9... | collective-permute-start | bytes 393224 | tf_op jit(solution)/shard_map/ppermute | solution.py:527
  193.6 7.1 %collective-permute-start.56 = (bf16[512,128]{1,0:T(8,128)(2,1)}, bf16[512,128]{1,0:T(8,128)(2,1)S(1)}, u32[]{:S(2)}, u32[]{:S(2)}) collective-permute-start(bf16[512,128]{1,0:T(8,128)(2,1)} %get-tuple-element.46), channel_id=1, source_target_pairs={{0,1},{1,2},{2,3},{3,0},{4,5},{5,6},{6,7},{7,4},{8,9},{9,10},{10,1... | collective-permute-start | bytes 393224 | tf_op jit(solution)/shard_map/ppermute | solution.py:527
  195.4 6.6 %collective-permute-start.58 = (bf16[512,128]{1,0:T(8,128)(2,1)S(1)}, bf16[512,128]{1,0:T(8,128)(2,1)S(1)}, u32[]{:S(2)}, u32[]{:S(2)}) collective-permute-start(bf16[512,128]{1,0:T(8,128)(2,1)S(1)} %add_convert_fusion.1), channel_id=1, source_target_pairs={{0,3},{1,0},{2,1},{3,2},{4,7},{5,4},{6,5},{7,6},{8,11},{9,8},{10,9... | collective-permute-start | bytes 393224 | tf_op jit(solution)/shard_map/ppermute | solution.py:527
  200.0 6.5 %collective-permute-start.54 = (bf16[512,128]{1,0:T(8,128)(2,1)S(1)}, bf16[512,128]{1,0:T(8,128)(2,1)S(1)}, u32[]{:S(2)}, u32[]{:S(2)}) collective-permute-start(bf16[512,128]{1,0:T(8,128)(2,1)S(1)} %add_convert_fusion.3), channel_id=1, source_target_pairs={{0,1},{1,2},{2,3},{3,0},{4,5},{5,6},{6,7},{7,4},{8,9},{9,10},{10,1... | collective-permute-start | bytes 393224 | tf_op jit(solution)/shard_map/ppermute | solution.py:527
  (29 other events, 297.9 us)

commit v2 on v1

v2 whole, which is shorter than its diff:
```python
import jax
import jax.numpy as jnp
from jax import lax
from jax.experimental import pallas as pl
from jax.experimental.pallas import tpu as pltpu
from jax.sharding import PartitionSpec as P

CAP = 2
GROUP = 16
BATCH = 8
CODES = 16
PICKS = 4
MIB = 1024 * 1024
ROOM = 63 * MIB
LESS = 16 * MIB
F32 = jnp.float32
BF16 = jnp.bfloat16


def split(value, size):
    shift = size.bit_length() - 1
    return jnp.right_shift(value, shift), jnp.bitwise_and(value, size - 1)


def pick_kernel(blocks, src_ref, dst_ref, info_ref, pattern_ref, away_ref, send_ref, meta_ref, tiles, counts, listed, sems):
    side = tiles.shape[1]
    devices = counts.shape[0]
    part = (send_ref.shape[1] - CODES) // CAP
    total, myself, first_row = info_ref[0], info_ref[1], jnp.bitwise_and(info_ref[2], 1) * part

    def clear(owner, carry):
        counts[owner] = 0
        for rank in range(CAP):
            meta_ref[owner * CAP + rank] = 0
        return carry

    lax.fori_loop(0, devices, clear, 0, unroll=4)

    def copy(slot, entry):
        return pltpu.make_async_copy(pattern_ref.at[slot], tiles.at[entry], sems.at[entry])

    def scan(slot, found):
        owner, _ = split(dst_ref[slot], blocks)
        listed[found] = slot
        return found + ((owner != myself) & (slot < total)).astype(jnp.int32)

    found = lax.fori_loop(0, dst_ref.shape[0], scan, 0, unroll=8)
    found = jnp.minimum(found, devices * CAP)

    def keep(entry, carry):
        slot = listed[entry]
        copy(slot, entry).start()
        owner, landing = split(dst_ref[slot], blocks)
        source = jnp.clip(src_ref[slot] - myself * blocks, 0, blocks - 1)
        rank = jnp.minimum(counts[owner], CAP - 1)
        counts[owner] = rank + 1
        place = owner * CAP + rank
        meta_ref[place] = 1 + source + blocks * landing
        listed[entry] = place
        return carry

    lax.fori_loop(0, found, keep, 0)
    row = lax.broadcasted_iota(jnp.int32, (part, side), 0)
    column = lax.broadcasted_iota(jnp.int32, (part, side), 1)
    chosen = (column == row + first_row).astype(F32).astype(BF16)

    def turn(batch, carry):
        first = batch * PICKS
        for index in range(PICKS):

            @pl.when(first + index < found)
            def arrive():
                copy(0, first + index).wait()

        entries = [jnp.minimum(first + index, found - 1) for index in range(PICKS)]
        values = [tiles[entry].astype(F32).astype(BF16) for entry in entries]
        turned = [
            lax.dot_general(chosen, value, (((1,), (1,)), ((), ())), preferred_element_type=F32).astype(BF16) for value in values
        ]
        for index, entry in enumerate(entries):
            place = listed[entry]
            owner, rank = split(place, CAP)
            away_ref[place] = values[index]
            send_ref[owner, pl.ds(pl.multiple_of(rank * part, part), part), :] = turned[index]
        return carry

    lax.fori_loop(0, lax.div(found + PICKS - 1, PICKS), turn, 0)
    lane = lax.broadcasted_iota(jnp.int32, (CODES, side), 1)

    def code(owner, carry):
        values = jnp.zeros((CODES, side), jnp.int32)
        for rank in range(CAP):
            values = jnp.where(lane == rank, meta_ref[owner * CAP + rank], values)
        send_ref[owner, CAP * part :, :] = values.astype(F32).astype(BF16)
        return carry

    lax.fori_loop(0, devices, code, 0, unroll=4)


def pick(tile_src, tile_dst, info, tile_pattern, blocks, devices):
    side = tile_pattern.shape[1]
    places = devices * CAP
    vmem = pl.BlockSpec(memory_space=pltpu.VMEM)
    smem = pl.BlockSpec(memory_space=pltpu.SMEM)
    return pl.pallas_call(
        lambda *refs: pick_kernel(blocks, *refs),
        in_specs=[smem, smem, smem, pl.BlockSpec(memory_space=pltpu.HBM)],
        out_specs=[vmem, vmem, smem],
        out_shape=[
            jax.ShapeDtypeStruct((places, side, side), BF16),
            jax.ShapeDtypeStruct((devices, CAP * side // 2 + CODES, side), BF16),
            jax.ShapeDtypeStruct((places,), jnp.int32),
        ],
        scratch_shapes=[
            pltpu.VMEM((places, side, side), jnp.int32),
            pltpu.SMEM((devices,), jnp.int32),
            pltpu.SMEM((tile_src.shape[0] + 1,), jnp.int32),
            pltpu.SemaphoreType.DMA((places,)),
        ],
        compiler_params=pltpu.CompilerParams(vmem_limit_bytes=ROOM),
        cost_estimate=pl.CostEstimate(flops=places * side * side, bytes_accessed=8 * MIB, transcendentals=0),
        name="pick",
    )(tile_src, tile_dst, info, tile_pattern)


def own_products(local_ref, values_ref, out_ref, in_ref):
    side = values_ref.shape[1]

    def block(index, carry):
        at = pl.ds(pl.multiple_of(index * side, side), side)
        out_ref[at, :] = jnp.dot(local_ref[at, :], values_ref[...], preferred_element_type=F32)
        return carry

    lax.fori_loop(0, values_ref.shape[0] // side, block, 0)
    for index in range(values_ref.shape[0] // side):
        span = slice(index * side, (index + 1) * side)
        in_ref[span, :] = lax.dot_general(local_ref[:, span], values_ref[...], (((0,), (0,)), ((), ())), preferred_element_type=F32)


def pile_kernel(src_ref, dst_ref, info_ref, pattern_ref, values_ref, local_ref, out_ref, in_ref, acc, groups, sems):
    depth, group, side = groups.shape[0], groups.shape[1], groups.shape[2]
    blocks = local_ref.shape[0] // side
    total, myself = info_ref[0], info_ref[1]
    turns = lax.div(total + group - 1, group)

    def copy(turn):
        return pltpu.make_async_copy(pattern_ref.at[pl.ds(turn * group, group)], groups.at[turn], sems.at[turn])

    for turn in range(depth):

        @pl.when(turn < turns)
        def begin():
            copy(turn).start()

    def clear(pair, carry):
        acc[pair] = jnp.zeros((side, side), jnp.int32)
        return carry

    lax.fori_loop(0, acc.shape[0], clear, 0)

    def take(turn, carry):
        copy(turn).wait()

        def add(index, carry):
            slot = turn * group + index
            source = jnp.clip(src_ref[slot] - myself * blocks, 0, blocks - 1)
            owner, landing = split(dst_ref[slot], blocks)
            pair = jnp.where((owner == myself) & (slot < total), source * blocks + landing, blocks * blocks)
            acc[pair] = acc[pair] + groups[turn, index]
            return carry

        lax.fori_loop(0, group, add, 0, unroll=4)
        return carry

    lax.fori_loop(0, turns, take, 0)

    def finish(source, carry):
        rows = pl.ds(pl.multiple_of(source * side, side), side)
        for landing in range(blocks):
            local_ref[rows, landing * side : (landing + 1) * side] = acc[source * blocks + landing].astype(F32).astype(BF16)
        return carry

    lax.fori_loop(0, blocks, finish, 0)
    own_products(local_ref, values_ref, out_ref, in_ref)


def pile(tile_src, tile_dst, info, tile_pattern, values):
    slots, side = tile_pattern.shape[0], tile_pattern.shape[1]
    blocks = values.shape[0] // side
    smem = pl.BlockSpec(memory_space=pltpu.SMEM)
    vmem = pl.BlockSpec(memory_space=pltpu.VMEM)
    return pl.pallas_call(
        pile_kernel,
        in_specs=[smem, smem, smem, pl.BlockSpec(memory_space=pltpu.HBM), vmem],
        out_specs=[vmem] * 3,
        out_shape=[jax.ShapeDtypeStruct((blocks * side, blocks * side), BF16)] + [jax.ShapeDtypeStruct(values.shape, F32)] * 2,
        scratch_shapes=[
            pltpu.VMEM((blocks * blocks + 1, side, side), jnp.int32),
            pltpu.VMEM((slots // GROUP, GROUP, side, side), jnp.int32),
            pltpu.SemaphoreType.DMA((slots // GROUP,)),
        ],
        compiler_params=pltpu.CompilerParams(vmem_limit_bytes=ROOM),
        cost_estimate=pl.CostEstimate(flops=slots * side * side, bytes_accessed=slots * side * side * 4, transcendentals=0),
        name="pile",
    )(tile_src, tile_dst, info, tile_pattern, values)


def list_products(info_ref, sent_ref, got_ref, list_ref, blocks):
    x, y, core = info_ref[3], info_ref[4], info_ref[5]
    places = sent_ref.shape[0]
    last = list_ref.shape[0] - 2

    def entry(device, block, place, row):
        chip, their_core = split(device, 2)
        their_y, their_x = split(chip, 4)
        step_x, step_y = jnp.bitwise_and(x - their_x, 3), jnp.bitwise_and(y - their_y, 3)
        first = jnp.where(their_core == 0, step_x, step_y)
        second = jnp.where(their_core == 0, step_y, step_x)
        index = (second * 4 + first) * blocks + block + jnp.where(their_core == core, 0, 16 * blocks)
        return (index * 64 + place) * 32 + row

    def out(place, count):
        code = sent_ref[place] - 1
        landing, source = split(jnp.maximum(code, 0), blocks)
        list_ref[count] = entry(jnp.right_shift(place, 1), landing, place, source)
        return count + (code >= 0).astype(jnp.int32)

    def into(place, count):
        code = got_ref[jnp.right_shift(place, 1), jnp.bitwise_and(place, 1)] - 1
        landing, source = split(jnp.maximum(code, 0), blocks)
        list_ref[count] = entry(jnp.right_shift(place, 1), source, place, blocks + landing)
        return count + (code >= 0).astype(jnp.int32)

    def padded(count):
        ends = lax.div(count + BATCH - 1, BATCH) * BATCH

        def pad(index, carry):
            list_ref[index] = 2 * blocks
            return carry

        lax.fori_loop(count, ends, pad, 0)
        return ends

    count = padded(lax.fori_loop(0, places, out, 0, unroll=4))
    list_ref[last] = lax.div(count, BATCH)
    count = padded(lax.fori_loop(0, places, into, count, unroll=4))
    list_ref[last + 1] = lax.div(count, BATCH)


def spread_kernel(turned, n_pieces, *refs):
    info_ref, listing_ref, refs = refs[0], refs[1], refs[2:]
    n_loads, n_stores = (6, 7) if turned else (7, 9)
    load_refs, refs = refs[:n_loads], refs[n_loads:]
    (arrived_ref, other_a_ref, other_b_ref, away_ref), refs = refs[:4], refs[4:]
    piece_refs, store_refs, refs = refs[:n_pieces], refs[n_pieces : n_pieces + n_stores], refs[n_pieces + n_stores :]
    if turned:
        list_ref = listing_ref
    else:
        list_ref, refs = refs[0], refs[1:]
    loads, refs = refs[:n_loads], refs[n_loads:]
    stores, refs = refs[:n_stores], refs[n_stores:]
    acc, every, tiles, weights, piece_sems, tile_sems, load_sems, store_sems = refs[:8]
    refs = refs[8:]
    base_out, base_in = loads[:2]
    side = every.shape[1]
    blocks = base_out.shape[0] // side
    plane = info_ref[2]
    planes = 4
    half, part, devices = blocks // 2, side // 2, other_a_ref.shape[0]
    last = list_ref.shape[0] - 2
    if not turned:
        arrived, codes, got, code_sems = refs
        fetch = pltpu.make_async_copy(arrived_ref.at[:, pl.ds(CAP * part, CODES), :], arrived, code_sems.at[0])
        fetch.start()
    starts = []
    offset = 0
    for index, ref in enumerate(piece_refs):
        starts.append(pltpu.make_async_copy(ref, every.at[pl.ds(offset, ref.shape[0])], piece_sems.at[index]))
        offset += ref.shape[0]
    for copy in starts:
        copy.start(priority=1)
    fetched = [pltpu.make_async_copy(ref, to, load_sems.at[index]) for index, (ref, to) in enumerate(zip(load_refs, loads))]
    for copy in fetched:
        copy.start()
    if not turned:
        fetch.wait()
        codes[...] = arrived[:, 0, :].astype(F32).astype(jnp.int32)
        store = pltpu.make_async_copy(codes, got, code_sems.at[1])
        store.start()

    def clear(row, carry):
        acc[row] = jnp.zeros(acc.shape[1:], F32)
        return carry

    if not turned:
        lax.fori_loop(0, acc.shape[0], clear, 0)
        store.wait()
        list_products(info_ref, listing_ref, got, list_ref, blocks)

    def begin_away(index, carry):
        place = jnp.bitwise_and(jnp.right_shift(list_ref[index], 5), 63)
        pltpu.make_async_copy(away_ref.at[place], tiles.at[index], tile_sems.at[index]).start()
        return carry

    def begin_arrived(index, carry):
        device, rank = split(jnp.bitwise_and(jnp.right_shift(list_ref[index], 5), 63), CAP)
        rows = pl.ds(pl.multiple_of(rank * part, part), part)
        parity = jnp.bitwise_and(plane, 1)

        def bring(ref, at, step):
            to = tiles.at[index, pl.ds(pl.multiple_of(step * part, part), part), :]
            pltpu.make_async_copy(ref.at[at, rows, :], to, tile_sems.at[index]).start()

        bring(arrived_ref, device, parity)

        @pl.when(device < devices)
        def first():
            bring(other_a_ref, device, 1 - parity)

        @pl.when(device >= devices)
        def second():
            bring(other_b_ref, device - devices, 1 - parity)

        return carry

    middle, end = list_ref[last], list_ref[last + 1]
    lax.fori_loop(0, middle * BATCH, begin_away, 0)
    lax.fori_loop(middle * BATCH, end * BATCH, begin_arrived, 0)
    if turned:
        lax.fori_loop(0, acc.shape[0], clear, 0)
    for copy in fetched:
        copy.wait()
    for kind in range(3):
        for step in range(planes):
            span = slice(step * side, (step + 1) * side)
            if turned:
                at = pl.ds(pl.multiple_of(jnp.bitwise_and(plane + step, planes - 1) * side, side), side)
                weights[kind, span, :] = loads[3 + kind][at, :]
            else:
                weights[kind, :, span] = loads[3 + step][kind * side : (kind + 1) * side, :]
    for copy in starts:
        copy.wait()

    def add_batch(batch, carry):
        indices = [batch * BATCH + index for index in range(BATCH)]
        codes = [list_ref[index] for index in indices]
        for index in indices:
            pltpu.make_async_copy(away_ref.at[0], tiles.at[index], tile_sems.at[index]).wait()
        products = [
            jnp.dot(tiles[index], every[jnp.right_shift(code, 11)], preferred_element_type=F32) for index, code in zip(indices, codes)
        ]
        for code, product in zip(codes, products):
            row = jnp.bitwise_and(code, 31)
            acc[row] = acc[row] + product
        return carry

    lax.fori_loop(0, end, add_batch, 0)

    def sums(block):
        at = pl.ds(pl.multiple_of(block * side, side), side)
        return (acc[block] + base_out[at, :]).astype(BF16), (acc[blocks + block] + base_in[at, :]).astype(BF16), at

    def times(values, kind):
        return lax.dot_general(values, weights[kind], (((1,), (1 if turned else 0,)), ((), ())), preferred_element_type=F32)

    def multiply(low):
        def at_block(block, carry):
            out, into, at = sums(block)
            to = pl.ds(pl.multiple_of((block - low) * side, side), side)
            if not turned:
                stores[7][at, :] = out
                stores[8][at, :] = into
            part = (times(out, 0) + times(into, 1)) * (1.0 / 32.0) + times(loads[2][at, :], 2)
            stores[0][at, :] = part[:, :side]
            for index in range(3):
                ref = stores[1 + 2 * index + (low > 0)]
                ref[to, :] = part[:, (index + 1) * side : (index + 2) * side].astype(ref.dtype)
            return carry

        return at_block

    written = [pltpu.make_async_copy(ref, to, store_sems.at[index]) for index, (ref, to) in enumerate(zip(stores, store_refs))]
    lax.fori_loop(0, half, multiply(0), 0)
    for index in (3, 1, 5):
        written[index].start()
    lax.fori_loop(half, blocks, multiply(half), 0)
    for index in (4, 2, 6, 0) if turned else (4, 2, 6, 0, 7, 8):
        written[index].start()
    for copy in written:
        copy.wait()


def spread(info, listing, base_out, base_in, others, arrived, others_a_b, away, pieces, turned):
    side, places = away.shape[1], away.shape[0]
    rows, width = base_out.shape
    blocks = rows // side
    planes = 4
    entries = 2 * (places + BATCH)
    every = sum(piece.shape[0] for piece in pieces) // side
    smem = pl.BlockSpec(memory_space=pltpu.SMEM)
    far = pl.BlockSpec(memory_space=pltpu.HBM)
    pieces = [piece.reshape(-1, side, width) for piece in pieces]
    loads = [base_out, base_in, *others]

    def shape(count, kind):
        return jax.ShapeDtypeStruct((count, width), kind)

    devices = places // CAP
    out_shape = [shape(rows, F32)] + [shape(rows // 2, kind) for kind in (F32, BF16, BF16, BF16, BF16, F32)]
    if not turned:
        out_shape += [shape(rows, BF16), shape(rows, BF16)]
    scratch = [pltpu.VMEM(part.shape, part.dtype) for part in loads + out_shape]
    scratch += [
        pltpu.VMEM((2 * blocks + 1, side, width), F32),
        pltpu.VMEM((every, side, width), BF16),
        pltpu.VMEM((entries, side, side), BF16),
        pltpu.VMEM((3, planes * width, width) if turned else (3, width, planes * width), BF16),
        pltpu.SemaphoreType.DMA((len(pieces),)),
        pltpu.SemaphoreType.DMA((entries,)),
        pltpu.SemaphoreType.DMA((len(loads),)),
        pltpu.SemaphoreType.DMA((len(out_shape),)),
    ]
    out_specs = [far] * len(out_shape)
    if not turned:
        out_shape += [jax.ShapeDtypeStruct((entries + 2,), jnp.int32)]
        out_specs += [smem]
        scratch += [
            pltpu.VMEM((devices, CODES, side), BF16),
            pltpu.VMEM((devices, side), jnp.int32),
            pltpu.SMEM((devices, side), jnp.int32),
            pltpu.SemaphoreType.DMA((2,)),
        ]
    return pl.pallas_call(
        lambda *refs: spread_kernel(turned, len(pieces), *refs),
        in_specs=[smem] * 2 + [far] * (len(loads) + 4 + len(pieces)),
        out_specs=out_specs,
        out_shape=out_shape,
        scratch_shapes=scratch,
        compiler_params=pltpu.CompilerParams(vmem_limit_bytes=ROOM),
        cost_estimate=pl.CostEstimate(flops=2 * rows * width * 3 * 512 + places * side**3 * 2, bytes_accessed=16 * MIB, transcendentals=0),
        name="spread",
    )(info, listing, *loads, arrived, *others_a_b, away, *pieces)


def slopes_kernel(left_1_ref, left_2_ref, left_3_ref, z0_ref, z1_ref, z2_ref, z3_ref, out_ref, right):
    width = z0_ref.shape[1]
    planes = right.shape[1] // width
    strips = out_ref.shape[0] // planes
    slivers = out_ref.shape[1] // 3
    for step, ref in enumerate((z0_ref, z1_ref, z2_ref, z3_ref)):
        right[:, step * width : (step + 1) * width] = ref[...]
    for kind, ref in enumerate((left_1_ref, left_2_ref, left_3_ref)):
        terms = lax.dot_general(ref[...], right[...], (((0,), (0,)), ((), ())), preferred_element_type=F32)
        for step in range(planes):
            for strip in range(strips):
                out_ref[step * strips + strip, kind * slivers : (kind + 1) * slivers, :] = terms[
                    strip * slivers : (strip + 1) * slivers, step * width : (step + 1) * width
                ]


def slopes(lefts, rights, devices):
    rows, width = rights[0].shape
    vmem = pl.BlockSpec(memory_space=pltpu.VMEM)
    planes = len(rights)
    return pl.pallas_call(
        slopes_kernel,
        in_specs=[vmem] * 7,
        out_specs=vmem,
        out_shape=jax.ShapeDtypeStruct((devices, 3 * width * planes // devices, width), F32),
        scratch_shapes=[pltpu.VMEM((rows, planes * width), BF16)],
        compiler_params=pltpu.CompilerParams(vmem_limit_bytes=LESS),
        cost_estimate=pl.CostEstimate(flops=2 * rows * 3 * width * planes * width, bytes_accessed=3 * MIB, transcendentals=0),
        name="slopes",
    )(*lefts, *rights)


def around(devices, stage, step):
    pairs = []
    for here in range(devices):
        core, x, y = here % 2, here // 2 % 4, here // 8
        if (core + stage) % 2 == 0:
            x = (x + step) % 4
        else:
            y = (y + step) % 4
        pairs.append((here, (y * 4 + x) * 2 + core))
    return pairs


def sister(part, devices):
    return lax.ppermute(part, "nodes", [(here, here ^ 1) for here in range(devices)])


def gather(values, devices, before, between):
    def move(part, stage, step):
        return lax.ppermute(part, "nodes", around(devices, stage, step))

    plus, minus, far = move(values, 0, 1), move(values, 0, -1), move(values, 0, 2)
    row = jnp.concatenate([values, plus, far, minus])
    row, before = lax.optimization_barrier((row, before))
    plus, minus = move(row, 1, 1), move(row, 1, -1)
    plus, minus, between = lax.optimization_barrier((plus, minus, between(before)))
    half = row.shape[0] // 2
    plus_far, minus_far = move(plus[:half], 1, 1), move(minus[half:], 1, -1)
    own = [row, plus, plus_far, minus_far, minus]
    return own + [sister(piece, devices) for piece in own], before, between


def shards(
    node_features, w_out, w_in, w_self, cotangent, tile_src, tile_dst, tile_pattern, tile_count
):
    devices = lax.axis_size("nodes")
    planes = lax.axis_size("hid")
    myself = lax.axis_index("nodes").astype(jnp.int32)
    plane = lax.axis_index("hid").astype(jnp.int32)
    core = lax.rem(myself, 2)
    side = tile_pattern.shape[1]
    rows, width = node_features.shape
    blocks = rows // side
    halves = rows // 2

    def shift(values, step):
        return lax.ppermute(values, "hid", [(here, (here + step) % planes) for here in range(planes)])

    info = jnp.stack([tile_count[0], myself, plane, lax.rem(lax.div(myself, 2), 4), lax.div(myself, 8), core])
    away, send, sent = pick(tile_src, tile_dst, info, tile_pattern, blocks, devices)
    stacked = jnp.stack([w_out, w_in, w_self]).reshape(3, planes, width, width)

    def rows_of(step):
        return lax.dynamic_index_in_dim(stacked, (plane + step) % planes, 1, keepdims=False).reshape(3 * width, width)

    pieces_x, _, (local, base_out, base_in) = gather(
        node_features,
        devices,
        (info, node_features, send),
        lambda held: pile(tile_src, tile_dst, held[0], tile_pattern, held[1]),
    )
    forward = [rows_of(0)] + [shift(rows_of(-step), -step) for step in range(1, planes)]
    arrived = lax.all_to_all(send, "nodes", 0, 0, tiled=True)
    arrived, _ = lax.optimization_barrier((arrived, base_out))
    middle = devices // 2
    others = [
        lax.ppermute(arrived[:middle], "hid", [(here, here ^ 1) for here in range(planes)]),
        lax.ppermute(arrived[middle:], "hid", [(here, (here + 1 if here % 2 else here - 1) % planes) for here in range(planes)]),
    ]
    base_out, forward = lax.optimization_barrier((base_out, forward))

    def collect(own, p1a, p1b, p2a, p2b, p3a, p3b, give=False):
        left, right = shift(p2a, 1), shift(p2b, -1)
        one_b, three_a = shift(p1b, 1), shift(p3a, -1)
        one_a = shift((p1a + left.astype(F32)).astype(BF16), 1)
        three_b = shift((p3b + right.astype(F32)).astype(BF16), -1)
        low = own[:halves] + one_a.astype(F32) + three_a.astype(F32)
        high = own[halves:] + one_b.astype(F32) + three_b.astype(F32)
        return (jnp.concatenate([low, high]), (one_b, three_a)) if give else jnp.concatenate([low, high])

    *parts, prop_out, prop_in, listed = spread(
        info, sent, base_out, base_in, [node_features, *forward], arrived, others, away, pieces_x, False
    )
    pre_act = collect(*parts)
    hidden = jax.nn.silu(pre_act).astype(BF16)
    gate = jax.nn.sigmoid(pre_act)
    grad_z = (cotangent.astype(F32) * gate * (1.0 + pre_act * (1.0 - gate))).astype(BF16)

    rights = [grad_z] + [shift(grad_z, step) for step in range(1, planes)]
    base_out = jnp.dot(local, grad_z, preferred_element_type=F32)
    base_in = jnp.einsum("ij,ik->jk", local, grad_z, preferred_element_type=F32)
    slivers = width * planes // devices
    pieces_z, (base_out, base_in), terms = gather(
        grad_z, devices, (base_out, base_in), lambda held: slopes([prop_out, prop_in, node_features], rights, devices)
    )
    terms = lax.all_to_all(terms, "nodes", 0, 0, tiled=True)
    parts = spread(info, listed, base_out, base_in, [grad_z, w_in, w_out, w_self], arrived, others, away, pieces_z, True)
    grad_sum, middle_sum = collect(*parts, True)
    grad_input = grad_sum.astype(BF16)

    strips = width // slivers
    moves = [
        ((step * strips + strip) * planes + here, (here * strips + strip) * planes + (here - step) % planes)
        for step in range(planes)
        for strip in range(strips)
        for here in range(planes)
    ]
    summed, _ = lax.optimization_barrier((jnp.sum(terms, axis=0), middle_sum))
    grads = lax.ppermute(summed, ("nodes", "hid"), moves).reshape(3, slivers, width)
    return (hidden, grad_input, grads[0] / 32.0, grads[1] / 32.0, grads[2])


def solution(mesh):
    in_specs = (
        P("nodes", "hid"),
        P(None, "hid"),
        P(None, "hid"),
        P(None, "hid"),
        P("nodes", "hid"),
        P("nodes"),
        P("nodes"),
        P("nodes", None, None),
        P("nodes"),
    )
    out_specs = (
        P("nodes", "hid"),
        P("nodes", "hid"),
        P("nodes", "hid"),
        P("nodes", "hid"),
        P("nodes", "hid"),
    )
    return jax.shard_map(shards, mesh=mesh, in_specs=in_specs, out_specs=out_specs, check_vma=False)
```

time: 210 us -> 196 us (0.933)
  waiting for transfers between devices: 62.4 us -> 54.8 us
  other arithmetic: 3.49 us -> 8.75 us
  matrix products: 7.68 us -> 3.05 us
  starting transfers between devices: 77.8 us -> 74.7 us
  Pallas kernels: 44.4 us -> 41.7 us
    ppermute x21 -> x18, waiting for transfers between devices: 32.8 us -> 18.2 us  [shift(): lax.ppermute(values, 'hid', [(here, (here + step) % planes) for here in r...]
    ppermute x20 -> x17, starting transfers between devices: 31.5 us -> 24.1 us  [the longest x14 22.9 us: move(): return lax.ppermute(part, 'nodes', around(devices, stage, step))]
    pallas_call x2 -> x1, Pallas kernels: 8.52 us -> 1.73 us  [slopes(): pl.pallas_call(slopes_kernel, in_specs=[vmem] * 7, out_specs=vmem, out_sh...]
    slice x5, local copies, waits for them, and re-layouts: 0.09 us -> 6.3 us  [the longest x4 4.98 us: gather(): plus_far, minus_far = (move(plus[:half], 1, 1), move(minus[half:], 1, -1))]
    ppermute x20 -> x17, waiting for transfers between devices: 29.6 us -> 34.5 us  [the longest x14 26.8 us: move(): return lax.ppermute(part, 'nodes', around(devices, stage, step))]
    dot_general x4 -> x2, matrix products: 7.68 us -> 3.05 us  [the longest x1 1.55 us: shards(): base_in = jnp.einsum('ij,ik->jk', local, grad_z, preferred_element_type=F32)]
    pallas_call x2, Pallas kernels: 21.4 us -> 25.1 us  [spread(): pl.pallas_call(lambda *refs: spread_kernel(turned, len(pieces), *refs), i...]
    all_to_all x1, starting transfers between devices: 3.91 us -> 7.59 us  [shards(): terms = lax.all_to_all(terms, 'nodes', 0, 0, tiled=True)]
  transfers between devices with their start and end apart: 61 -> 47, of which waited for: 15 -> 21; matrix products, arithmetic and copies ran while one was open for 6% -> 8% of each run, Pallas kernels for 19% -> 15%
where the time goes in v2:
time: 196 us; the launch traced here: 195 us
  starting transfers between devices  74.7 us (38%)
  waiting for transfers between devices  54.8 us (28%)
  Pallas kernels  41.7 us (21%)
  local copies, waits for them, and re-layouts  10.1 us (5%)
  other arithmetic  8.75 us (4%)
  matrix products  3.05 us (2%)
    ppermute x18, starting transfers between devices, shift(): lax.ppermute(values, 'hid', [(here, (here + step) % planes) for here in r...  34.5 us
    ppermute x14, waiting for transfers between devices, move(): return lax.ppermute(part, 'nodes', around(devices, stage, step))  26.8 us
    pallas_call x2, Pallas kernels, spread(): pl.pallas_call(lambda *refs: spread_kernel(turned, len(pieces), *refs), i...  25.1 us
    ppermute x14, starting transfers between devices, move(): return lax.ppermute(part, 'nodes', around(devices, stage, step))  22.9 us
    ppermute x18, waiting for transfers between devices, shift(): lax.ppermute(values, 'hid', [(here, (here + step) % planes) for here in r...  18.2 us
    pallas_call x1, Pallas kernels, pile(): pl.pallas_call(pile_kernel, in_specs=[smem, smem, smem, pl.BlockSpec(memo...  7.83 us
    all_to_all x1, starting transfers between devices, shards(): terms = lax.all_to_all(terms, 'nodes', 0, 0, tiled=True)  7.59 us
    pallas_call x1, Pallas kernels, pick(): pl.pallas_call(lambda *refs: pick_kernel(blocks, *refs), in_specs=[smem,...  6.98 us
  transfers between devices with their start and end apart: 47, of which 21 were waited for; matrix products, arithmetic and copies ran while one was open for 8% of the time, Pallas kernels for 15%

profile of v2, /device:TPU:0, one launch (start us, length us, event | category | flops | bytes accessed | tf_op | source)
XLA Modules:
  0.0 194.9 jit_solution(9736463295592216222)
XLA Ops:
  0.6 2.9 %collective-permute-start.2 = (bf16[1024,128]{1,0:T(8,128)(2,1)}, bf16[1024,128]{1,0:T(8,128)(2,1)S(1)}, u32[]{:S(2)}, u32[]{:S(2)}) collective-permute-start(bf16[1024,128]{1,0:T(8,128)(2,1)} %left_3_ref.1), channel_id=1, source_target_pairs={{0,24},{4,100},{8,0},{12,108},{16,8},{20,116},{24,16},{28,124},{32... | collective-permute-start | bytes 786440 | tf_op jit(solution)/shard_map/ppermute | solution.py:495
  3.5 0.8 collective-permute-start.1
  4.3 0.9 collective-permute-start
  6.6 7.0 %pick.1 = (bf16[64,128,128]{2,1,0:T(8,128)(2,1)}, bf16[32,144,128]{2,1,0:T(8,128)(2,1)}, s32[64]{0:T(128)}) custom-call(s32[256]{0:T(256)} %src_ref.1, s32[256]{0:T(256)} %dst_ref.1, s32[6]{0:T(128)} %stack.35.refs_2_.info_ref.refs_0_, s32[256,128,128]{2,1,0:T(8,128)} %pattern_ref.1), custom_call_target="tpu_custom_call" | custom-call | flops 1048576 | bytes 8388608 | tf_op jit(solution)/shard_map/pick/pallas_call | solution.py:105
  13.6 6.9 %all-to-all-start = ((bf16[32,144,128]{2,1,0:T(8,128)(2,1)}), bf16[32,144,128]{2,1,0:T(8,128)(2,1)}, u32[]{:S(2)}, u32[]{:S(2)}) async-start(bf16[32,144,128]{2,1,0:T(8,128)(2,1)} %get-tuple-element.50), calls=%async_computation | async-start | bytes 2359296 | tf_op jit(solution)/shard_map/all_to_all | solution.py:538
  20.6 1.1 pad_maximum_fusion
  21.7 3.0 %collective-permute-start.4 = (bf16[4096,128]{1,0:T(8,128)(2,1)}, bf16[4096,128]{1,0:T(8,128)(2,1)}, u32[]{:S(2)}, u32[]{:S(2)}) collective-permute-start(bf16[4096,128]{1,0:T(8,128)(2,1)} %pad_maximum_fusion), channel_id=1, source_target_pairs={{0,96},{4,28},{8,104},{12,4},{16,112},{20,12},{24,120},{28,20},{32... | collective-permute-start | bytes 3145736 | tf_op jit(solution)/shard_map/ppermute | solution.py:495
  25.5 3.9 %collective-permute-start.6 = (bf16[384,128]{1,0:T(8,128)(2,1)S(1)}, bf16[384,128]{1,0:T(8,128)(2,1)S(1)}, u32[]{:S(2)}, u32[]{:S(2)}) collective-permute-start(bf16[384,128]{1,0:T(8,128)(2,1)S(1)} %bitcast.55), channel_id=1, source_target_pairs={{0,2},{1,3},{2,0},{3,1},{4,6},{5,7},{6,4},{7,5},{8,10},{9,11},{10,... | collective-permute-start | bytes 294920 | tf_op jit(solution)/shard_map/ppermute | solution.py:522
  29.3 1.0 collective-permute-start.7
  30.4 7.8 %pile.1 = (bf16[1024,1024]{1,0:T(8,128)(2,1)}, f32[1024,128]{1,0:T(8,128)}, f32[1024,128]{1,0:T(8,128)}) custom-call(s32[256]{0:T(256)} %src_ref.1, s32[256]{0:T(256)} %dst_ref.1, s32[6]{0:T(128)} %stack.35.refs_2_.info_ref.refs_0_, s32[256,128,128]{2,1,0:T(8,128)} %pattern_ref.1, bf16[1024,128]{1,0:T(8,128)(2,1)} %left_3_ref.1), custom_call_target="tpu_custom_call" | custom-call | flops 4194304 | bytes 16777216 | tf_op jit(solution)/shard_map/pile/pallas_call | solution.py:192
  38.2 9.1 %collective-permute-done.4 = bf16[4096,128]{1,0:T(8,128)(2,1)} collective-permute-done((bf16[4096,128]{1,0:T(8,128)(2,1)}, bf16[4096,128]{1,0:T(8,128)(2,1)}, u32[]{:S(2)}, u32[]{:S(2)}) %collective-permute-start.4) | collective-permute-done | bytes 1048608 | tf_op jit(solution)/shard_map/ppermute | solution.py:495
  47.3 4.0 %collective-permute-start.5 = (bf16[384,128]{1,0:T(8,128)(2,1)S(1)}, bf16[384,128]{1,0:T(8,128)(2,1)S(1)}, u32[]{:S(2)}, u32[]{:S(2)}) collective-permute-start(bf16[384,128]{1,0:T(8,128)(2,1)S(1)} %bitcast.54), channel_id=1, source_target_pairs={{0,3},{1,0},{2,1},{3,2},{4,7},{5,4},{6,5},{7,6},{8,11},{9,8},{10,9... | collective-permute-start | bytes 294920 | tf_op jit(solution)/shard_map/ppermute | solution.py:522
  51.3 1.1 slice.45
  52.4 2.3 %collective-permute-start.11 = (bf16[2048,128]{1,0:T(8,128)(2,1)S(1)}, bf16[2048,128]{1,0:T(8,128)(2,1)S(1)}, u32[]{:S(2)}, u32[]{:S(2)}) collective-permute-start(bf16[2048,128]{1,0:T(8,128)(2,1)S(1)} %slice.45), channel_id=1, source_target_pairs={{0,96},{4,28},{8,104},{12,4},{16,112},{20,12},{24,120},{28,20},{32... | collective-permute-start | bytes 1572872 | tf_op jit(solution)/shard_map/ppermute | solution.py:495
  54.7 1.3 fusion
  56.6 1.1 slice.44
  58.5 0.8 collective-permute-start.16
  59.3 2.4 %collective-permute-done.11 = bf16[2048,128]{1,0:T(8,128)(2,1)S(1)} collective-permute-done((bf16[2048,128]{1,0:T(8,128)(2,1)S(1)}, bf16[2048,128]{1,0:T(8,128)(2,1)S(1)}, u32[]{:S(2)}, u32[]{:S(2)}) %collective-permute-start.11) | collective-permute-done | bytes 524320 | tf_op jit(solution)/shard_map/ppermute | solution.py:495
  61.6 6.6 %collective-permute-done.10 = bf16[2048,128]{1,0:T(8,128)(2,1)S(1)} collective-permute-done((bf16[2048,128]{1,0:T(8,128)(2,1)S(1)}, bf16[2048,128]{1,0:T(8,128)(2,1)S(1)}, u32[]{:S(2)}, u32[]{:S(2)}) %collective-permute-start.10) | collective-permute-done | bytes 524320 | tf_op jit(solution)/shard_map/ppermute | solution.py:495
  68.2 3.2 %collective-permute-done.9.refs_11_.refs_10_ = bf16[16,144,128]{2,1,0:T(8,128)(2,1)S(1)} collective-permute-done((bf16[16,144,128]{2,1,0:T(8,128)(2,1)S(1)}, bf16[16,144,128]{2,1,0:T(8,128)(2,1)S(1)}, u32[]{:S(2)}, u32[]{:S(2)}) %collective-permute-start.9) | collective-permute-done | bytes 589856 | tf_op jit(solution)/shard_map/ppermute | solution.py:543
  71.5 4.5 %collective-permute-done.8.refs_10_.refs_9_ = bf16[16,144,128]{2,1,0:T(8,128)(2,1)} collective-permute-done((bf16[16,144,128]{2,1,0:T(8,128)(2,1)S(1)}, bf16[16,144,128]{2,1,0:T(8,128)(2,1)}, u32[]{:S(2)}, u32[]{:S(2)}) %collective-permute-start.8) | collective-permute-done | bytes 589856 | tf_op jit(solution)/shard_map/ppermute | solution.py:542
  76.0 0.8 copy-done.11
  76.8 0.8 copy-done.12
  77.6 13.0 %spread.2 = (f32[1024,128]{1,0:T(8,128)}, f32[512,128]{1,0:T(8,128)}, bf16[512,128]{1,0:T(8,128)(2,1)}, bf16[512,128]{1,0:T(8,128)(2,1)}, bf16[512,128]{1,0:T(8,...) custom-call(s32[6]{0:T(128)} %stack.35.refs_2_.info_ref.refs_0_, ...), custom_call_target="tpu_custom_call" | custom-call | flops 671088640 | bytes 16777216 | tf_op jit(solution)/shard_map/spread/pallas_call | solution.py:433
  91.0 2.9 %collective-permute-start.19 = (bf16[512,128]{1,0:T(8,128)(2,1)}, bf16[512,128]{1,0:T(8,128)(2,1)S(1)}, u32[]{:S(2)}, u32[]{:S(2)}) collective-permute-start(bf16[512,128]{1,0:T(8,128)(2,1)} %get-tuple-element.71), channel_id=1, source_target_pairs={{0,3},{1,0},{2,1},{3,2},{4,7},{5,4},{6,5},{7,6},{8,11},{9,8},{10,9... | collective-permute-start | bytes 393224 | tf_op jit(solution)/shard_map/ppermute | solution.py:522
  94.0 3.2 %collective-permute-start.21 = (bf16[512,128]{1,0:T(8,128)(2,1)}, bf16[512,128]{1,0:T(8,128)(2,1)S(1)}, u32[]{:S(2)}, u32[]{:S(2)}) collective-permute-start(bf16[512,128]{1,0:T(8,128)(2,1)} %get-tuple-element.74), channel_id=1, source_target_pairs={{0,3},{1,0},{2,1},{3,2},{4,7},{5,4},{6,5},{7,6},{8,11},{9,8},{10,9... | collective-permute-start | bytes 393224 | tf_op jit(solution)/shard_map/ppermute | solution.py:522
  97.2 1.1 collective-permute-done.17
  98.3 1.0 add_convert_fusion.5
  100.0 1.0 add_convert_fusion.4
  101.0 3.6 %collective-permute-start.22 = (bf16[512,128]{1,0:T(8,128)(2,1)S(1)}, bf16[512,128]{1,0:T(8,128)(2,1)S(1)}, u32[]{:S(2)}, u32[]{:S(2)}) collective-permute-start(bf16[512,128]{1,0:T(8,128)(2,1)S(1)} %add_convert_fusion.4), channel_id=1, source_target_pairs={{0,3},{1,0},{2,1},{3,2},{4,7},{5,4},{6,5},{7,6},{8,11},{9,8},{10,9... | collective-permute-start | bytes 393224 | tf_op jit(solution)/shard_map/ppermute | solution.py:522
  104.6 0.9 collective-permute-done.18
  105.6 1.6 collective-permute-done.22
  107.2 1.1 convert_add_fusion.1
  108.3 1.0 multiply_convert_fusion
  109.2 2.8 %collective-permute-start.25 = (bf16[1024,128]{1,0:T(8,128)(2,1)S(1)}, bf16[1024,128]{1,0:T(8,128)(2,1)S(1)}, u32[]{:S(2)}, u32[]{:S(2)}) collective-permute-start(bf16[1024,128]{1,0:T(8,128)(2,1)S(1)} %get-tuple-element.97.z0_ref.refs_4_), channel_id=1, source_target_pairs={{0,24},{4,100},{8,0},{12,108},{16,8},{20,116},{24,16},{28,124},{32... | collective-permute-start | bytes 786440 | tf_op jit(solution)/shard_map/ppermute | solution.py:495
  112.1 1.4 collective-permute-start.24
  113.5 1.6 fusion.3.refs_3_
  115.0 1.5 fusion.2.refs_2_
  116.5 2.3 %collective-permute-done.25 = bf16[1024,128]{1,0:T(8,128)(2,1)S(1)} collective-permute-done((bf16[1024,128]{1,0:T(8,128)(2,1)S(1)}, bf16[1024,128]{1,0:T(8,128)(2,1)S(1)}, u32[]{:S(2)}, u32[]{:S(2)}) %collective-permute-start.25) | collective-permute-done | bytes 262176 | tf_op jit(solution)/shard_map/ppermute | solution.py:495
  118.8 1.2 collective-permute-done.24
  120.1 2.7 %collective-permute-done.23 = bf16[1024,128]{1,0:T(8,128)(2,1)S(1)} collective-permute-done((bf16[1024,128]{1,0:T(8,128)(2,1)S(1)}, bf16[1024,128]{1,0:T(8,128)(2,1)S(1)}, u32[]{:S(2)}, u32[]{:S(2)}) %collective-permute-start.23) | collective-permute-done | bytes 262176 | tf_op jit(solution)/shard_map/ppermute | solution.py:495
  122.8 5.2 %collective-permute-start.27 = (bf16[4096,128]{1,0:T(8,128)(2,1)S(1)}, bf16[4096,128]{1,0:T(8,128)(2,1)S(1)}, u32[]{:S(2)}, u32[]{:S(2)}) collective-permute-start(bf16[4096,128]{1,0:T(8,128)(2,1)S(1)} %pad_maximum_fusion.1), channel_id=1, source_target_pairs={{0,96},{4,28},{8,104},{12,4},{16,112},{20,12},{24,120},{28,20},{32... | collective-permute-start | bytes 3145736 | tf_op jit(solution)/shard_map/ppermute | solution.py:495
  128.0 3.7 %collective-permute-start.30 = (bf16[1024,128]{1,0:T(8,128)(2,1)S(1)}, bf16[1024,128]{1,0:T(8,128)(2,1)S(1)}, u32[]{:S(2)}, u32[]{:S(2)}) collective-permute-start(bf16[1024,128]{1,0:T(8,128)(2,1)S(1)} %get-tuple-element.97.z0_ref.refs_4_), channel_id=1, source_target_pairs={{0,3},{1,0},{2,1},{3,2},{4,7},{5,4},{6,5},{7,6},{8,11},{9,8},{10,9... | collective-permute-start | bytes 786440 | tf_op jit(solution)/shard_map/ppermute | solution.py:522
  131.7 0.9 collective-permute-start.28
  132.5 5.8 %collective-permute-done.30.z3_ref = bf16[1024,128]{1,0:T(8,128)(2,1)S(1)} collective-permute-done((bf16[1024,128]{1,0:T(8,128)(2,1)S(1)}, bf16[1024,128]{1,0:T(8,128)(2,1)S(1)}, u32[]{:S(2)}, u32[]{:S(2)}) %collective-permute-start.30) | collective-permute-done | bytes 262176 | tf_op jit(solution)/shard_map/ppermute | solution.py:522
  138.4 1.3 collective-permute-done.29.z2_ref
  139.7 2.4 %collective-permute-done.28.z1_ref = bf16[1024,128]{1,0:T(8,128)(2,1)S(1)} collective-permute-done((bf16[1024,128]{1,0:T(8,128)(2,1)S(1)}, bf16[1024,128]{1,0:T(8,128)(2,1)S(1)}, u32[]{:S(2)}, u32[]{:S(2)}) %collective-permute-start.28) | collective-permute-done | bytes 262176 | tf_op jit(solution)/shard_map/ppermute | solution.py:522
  142.1 1.7 slopes.1
  144.1 1.0 slice.49
  145.1 2.9 %collective-permute-start.32 = (bf16[2048,128]{1,0:T(8,128)(2,1)}, bf16[2048,128]{1,0:T(8,128)(2,1)}, u32[]{:S(2)}, u32[]{:S(2)}) collective-permute-start(bf16[2048,128]{1,0:T(8,128)(2,1)} %slice.49), channel_id=1, source_target_pairs={{0,96},{4,28},{8,104},{12,4},{16,112},{20,12},{24,120},{28,20},{32... | collective-permute-start | bytes 1572872 | tf_op jit(solution)/shard_map/ppermute | solution.py:495
  148.0 1.9 slice.48
  150.3 7.6 %all-to-all-start.1 = ((f32[32,48,128]{2,1,0:T(8,128)}), f32[32,48,128]{2,1,0:T(8,128)S(1)}, u32[]{:S(2)}, u32[]{:S(2)}) async-start(f32[32,48,128]{2,1,0:T(8,128)} %slopes.1), calls=%async_computation.1 | async-start | bytes 1572864 | tf_op jit(solution)/shard_map/all_to_all | solution.py:571
  158.3 2.2 %collective-permute-done.31 = bf16[2048,128]{1,0:T(8,128)(2,1)} collective-permute-done((bf16[2048,128]{1,0:T(8,128)(2,1)}, bf16[2048,128]{1,0:T(8,128)(2,1)}, u32[]{:S(2)}, u32[]{:S(2)}) %collective-permute-start.31) | collective-permute-done | bytes 524320 | tf_op jit(solution)/shard_map/ppermute | solution.py:495
  160.6 2.1 %collective-permute-done.35 = bf16[2048,128]{1,0:T(8,128)(2,1)S(1)} collective-permute-done((bf16[2048,128]{1,0:T(8,128)(2,1)}, bf16[2048,128]{1,0:T(8,128)(2,1)S(1)}, u32[]{:S(2)}, u32[]{:S(2)}) %collective-permute-start.35) | collective-permute-done | bytes 524320 | tf_op jit(solution)/shard_map/ppermute | solution.py:490
  162.7 0.8 copy-done.17
  163.4 12.1 %spread.3 = (f32[1024,128]{1,0:T(8,128)}, f32[512,128]{1,0:T(8,128)}, bf16[512,128]{1,0:T(8,128)(2,1)}, bf16[512,128]{1,0:T(8,128)(2,1)}, bf16[512,128]{1,0:T(8,...) custom-call(s32[6]{0:T(128)} %stack.35.refs_2_.info_ref.refs_0_, s32[146]{0:T(256)} %get-tuple-element.75.refs_1_, ...), custom_call_target="tpu_custom_call" | custom-call | flops 671088640 | bytes 16777216 | tf_op jit(solution)/shard_map/spread/pallas_call | solution.py:433
  175.8 3.3 %collective-permute-start.40 = (bf16[512,128]{1,0:T(8,128)(2,1)}, bf16[512,128]{1,0:T(8,128)(2,1)S(1)}, u32[]{:S(2)}, u32[]{:S(2)}) collective-permute-start(bf16[512,128]{1,0:T(8,128)(2,1)} %get-tuple-element.87), channel_id=1, source_target_pairs={{0,3},{1,0},{2,1},{3,2},{4,7},{5,4},{6,5},{7,6},{8,11},{9,8},{10,9... | collective-permute-start | bytes 393224 | tf_op jit(solution)/shard_map/ppermute | solution.py:522
  179.0 3.2 %collective-permute-start.42 = (bf16[512,128]{1,0:T(8,128)(2,1)}, bf16[512,128]{1,0:T(8,128)(2,1)S(1)}, u32[]{:S(2)}, u32[]{:S(2)}) collective-permute-start(bf16[512,128]{1,0:T(8,128)(2,1)} %get-tuple-element.90), channel_id=1, source_target_pairs={{0,3},{1,0},{2,1},{3,2},{4,7},{5,4},{6,5},{7,6},{8,11},{9,8},{10,9... | collective-permute-start | bytes 393224 | tf_op jit(solution)/shard_map/ppermute | solution.py:522
  183.0 1.0 add_convert_fusion.3
  184.0 1.7 collective-permute-done.41
  186.4 1.0 add_convert_fusion.1
  187.4 4.1 %collective-permute-start.43 = (bf16[512,128]{1,0:T(8,128)(2,1)S(1)}, bf16[512,128]{1,0:T(8,128)(2,1)S(1)}, u32[]{:S(2)}, u32[]{:S(2)}) collective-permute-start(bf16[512,128]{1,0:T(8,128)(2,1)S(1)} %add_convert_fusion.1), channel_id=1, source_target_pairs={{0,3},{1,0},{2,1},{3,2},{4,7},{5,4},{6,5},{7,6},{8,11},{9,8},{10,9... | collective-permute-start | bytes 393224 | tf_op jit(solution)/shard_map/ppermute | solution.py:522
  192.1 1.9 collective-permute-done.43
  194.2 0.7 pad_maximum_fusion.4
  (103 shorter events, 7.5 us)
Async XLA Ops:
  0.6 19.9 %collective-permute-start.2 = (bf16[1024,128]{1,0:T(8,128)(2,1)}, bf16[1024,128]{1,0:T(8,128)(2,1)S(1)}, u32[]{:S(2)}, u32[]{:S(2)}) collective-permute-start(bf16[1024,128]{1,0:T(8,128)(2,1)} %left_3_ref.1), channel_id=1, source_target_pairs={{0,24},{4,100},{8,0},{12,108},{16,8},{20,116},{24,16},{28,124},{32... | collective-permute-start | bytes 786440 | tf_op jit(solution)/shard_map/ppermute | solution.py:495
  3.5 17.0 %collective-permute-start.1 = (bf16[1024,128]{1,0:T(8,128)(2,1)}, bf16[1024,128]{1,0:T(8,128)(2,1)S(1)}, u32[]{:S(2)}, u32[]{:S(2)}) collective-permute-start(bf16[1024,128]{1,0:T(8,128)(2,1)} %left_3_ref.1), channel_id=1, source_target_pairs={{0,16},{4,68},{8,24},{12,76},{16,0},{20,84},{24,8},{28,92},{32,48}... | collective-permute-start | bytes 786440 | tf_op jit(solution)/shard_map/ppermute | solution.py:495
  4.3 16.2 %collective-permute-start = (bf16[1024,128]{1,0:T(8,128)(2,1)}, bf16[1024,128]{1,0:T(8,128)(2,1)S(1)}, u32[]{:S(2)}, u32[]{:S(2)}) collective-permute-start(bf16[1024,128]{1,0:T(8,128)(2,1)} %left_3_ref.1), channel_id=1, source_target_pairs={{0,8},{4,36},{8,16},{12,44},{16,24},{20,52},{24,0},{28,60},{32,40}... | collective-permute-start | bytes 786440 | tf_op jit(solution)/shard_map/ppermute | solution.py:495
  13.6 11.1 %copy-start.13 = (bf16[512,128]{1,0:T(8,128)(2,1)S(1)}, bf16[512,128]{1,0:T(8,128)(2,1)}, u32[]{:S(2)}) copy-start(bf16[512,128]{1,0:T(8,128)(2,1)} %refs_7_.1) | copy-start | bytes 393220
  13.6 11.1 %copy-start.14 = (bf16[512,128]{1,0:T(8,128)(2,1)S(1)}, bf16[512,128]{1,0:T(8,128)(2,1)}, u32[]{:S(2)}) copy-start(bf16[512,128]{1,0:T(8,128)(2,1)} %refs_5_.1) | copy-start | bytes 393220
  13.6 11.1 %copy-start.15 = (bf16[512,128]{1,0:T(8,128)(2,1)S(1)}, bf16[512,128]{1,0:T(8,128)(2,1)}, u32[]{:S(2)}) copy-start(bf16[512,128]{1,0:T(8,128)(2,1)} %refs_6_.1) | copy-start | bytes 393220
  13.6 37.7 %all-to-all-start = ((bf16[32,144,128]{2,1,0:T(8,128)(2,1)}), bf16[32,144,128]{2,1,0:T(8,128)(2,1)}, u32[]{:S(2)}, u32[]{:S(2)}) async-start(bf16[32,144,128]{2,1,0:T(8,128)(2,1)} %get-tuple-element.50), calls=%async_computation | async-start | bytes 2359296 | tf_op jit(solution)/shard_map/all_to_all | solution.py:538
  21.7 25.6 %collective-permute-start.4 = (bf16[4096,128]{1,0:T(8,128)(2,1)}, bf16[4096,128]{1,0:T(8,128)(2,1)}, u32[]{:S(2)}, u32[]{:S(2)}) collective-permute-start(bf16[4096,128]{1,0:T(8,128)(2,1)} %pad_maximum_fusion), channel_id=1, source_target_pairs={{0,96},{4,28},{8,104},{12,4},{16,112},{20,12},{24,120},{28,20},{32... | collective-permute-start | bytes 3145736 | tf_op jit(solution)/shard_map/ppermute | solution.py:495
  24.7 26.6 %collective-permute-start.3 = (bf16[4096,128]{1,0:T(8,128)(2,1)}, bf16[4096,128]{1,0:T(8,128)(2,1)}, u32[]{:S(2)}, u32[]{:S(2)}) collective-permute-start(bf16[4096,128]{1,0:T(8,128)(2,1)} %pad_maximum_fusion), channel_id=1, source_target_pairs={{0,32},{4,12},{8,40},{12,20},{16,48},{20,28},{24,56},{28,4},{32,64... | collective-permute-start | bytes 3145736 | tf_op jit(solution)/shard_map/ppermute | solution.py:495
  24.7 33.8 %collective-permute-start.12 = (bf16[4096,128]{1,0:T(8,128)(2,1)}, bf16[4096,128]{1,0:T(8,128)(2,1)}, u32[]{:S(2)}, u32[]{:S(2)}) collective-permute-start(bf16[4096,128]{1,0:T(8,128)(2,1)} %pad_maximum_fusion), channel_id=1, source_target_pairs={{0,4},{4,0},{8,12},{12,8},{16,20},{20,16},{24,28},{28,24},{32,36},... | collective-permute-start | bytes 3145736 | tf_op jit(solution)/shard_map/ppermute | solution.py:490
  25.5 30.6 %collective-permute-start.6 = (bf16[384,128]{1,0:T(8,128)(2,1)S(1)}, bf16[384,128]{1,0:T(8,128)(2,1)S(1)}, u32[]{:S(2)}, u32[]{:S(2)}) collective-permute-start(bf16[384,128]{1,0:T(8,128)(2,1)S(1)} %bitcast.55), channel_id=1, source_target_pairs={{0,2},{1,3},{2,0},{3,1},{4,6},{5,7},{6,4},{7,5},{8,10},{9,11},{10,... | collective-permute-start | bytes 294920 | tf_op jit(solution)/shard_map/ppermute | solution.py:522
  29.3 28.3 %collective-permute-start.7 = (bf16[384,128]{1,0:T(8,128)(2,1)}, bf16[384,128]{1,0:T(8,128)(2,1)S(1)}, u32[]{:S(2)}, u32[]{:S(2)}) collective-permute-start(bf16[384,128]{1,0:T(8,128)(2,1)} %bitcast.14), channel_id=1, source_target_pairs={{0,1},{1,2},{2,3},{3,0},{4,5},{5,6},{6,7},{7,4},{8,9},{9,10},{10,1... | collective-permute-start | bytes 294920 | tf_op jit(solution)/shard_map/ppermute | solution.py:522
  47.3 10.5 %collective-permute-start.5 = (bf16[384,128]{1,0:T(8,128)(2,1)S(1)}, bf16[384,128]{1,0:T(8,128)(2,1)S(1)}, u32[]{:S(2)}, u32[]{:S(2)}) collective-permute-start(bf16[384,128]{1,0:T(8,128)(2,1)S(1)} %bitcast.54), channel_id=1, source_target_pairs={{0,3},{1,0},{2,1},{3,2},{4,7},{5,4},{6,5},{7,6},{8,11},{9,8},{10,9... | collective-permute-start | bytes 294920 | tf_op jit(solution)/shard_map/ppermute | solution.py:522
  52.4 9.2 %collective-permute-start.11 = (bf16[2048,128]{1,0:T(8,128)(2,1)S(1)}, bf16[2048,128]{1,0:T(8,128)(2,1)S(1)}, u32[]{:S(2)}, u32[]{:S(2)}) collective-permute-start(bf16[2048,128]{1,0:T(8,128)(2,1)S(1)} %slice.45), channel_id=1, source_target_pairs={{0,96},{4,28},{8,104},{12,4},{16,112},{20,12},{24,120},{28,20},{32... | collective-permute-start | bytes 1572872 | tf_op jit(solution)/shard_map/ppermute | solution.py:495
  56.1 21.5 %copy-start.20 = (bf16[384,128]{1,0:T(8,128)(2,1)}, bf16[384,128]{1,0:T(8,128)(2,1)S(1)}, u32[]{:S(2)}) copy-start(bf16[384,128]{1,0:T(8,128)(2,1)S(1)} %collective-permute-done.6.refs_7_) | copy-start | bytes 294916
  56.1 15.4 %collective-permute-start.9 = (bf16[16,144,128]{2,1,0:T(8,128)(2,1)S(1)}, bf16[16,144,128]{2,1,0:T(8,128)(2,1)S(1)}, u32[]{:S(2)}, u32[]{:S(2)}) collective-permute-start(bf16[16,144,128]{2,1,0:T(8,128)(2,1)S(1)} %get-tuple-element.93), channel_id=1, source_target_pairs={{0,3},{1,2},{2,1},{3,0},{4,7},{5,6},{6,5},{7,4},{8,11},{9,10},{10,... | collective-permute-start | bytes 1769480 | tf_op jit(solution)/shard_map/ppermute | solution.py:543
  57.7 20.0 %copy-start.21 = (bf16[384,128]{1,0:T(8,128)(2,1)}, bf16[384,128]{1,0:T(8,128)(2,1)S(1)}, u32[]{:S(2)}) copy-start(bf16[384,128]{1,0:T(8,128)(2,1)S(1)} %collective-permute-done.7.refs_8_) | copy-start | bytes 294916
  57.7 18.3 %collective-permute-start.13 = (bf16[4096,128]{1,0:T(8,128)(2,1)}, bf16[4096,128]{1,0:T(8,128)(2,1)}, u32[]{:S(2)}, u32[]{:S(2)}) collective-permute-start(bf16[4096,128]{1,0:T(8,128)(2,1)} %collective-permute-done.3), channel_id=1, source_target_pairs={{0,4},{4,0},{8,12},{12,8},{16,20},{20,16},{24,28},{28,24},{32,36},... | collective-permute-start | bytes 3145736 | tf_op jit(solution)/shard_map/ppermute | solution.py:490
  57.8 19.8 %copy-start.22 = (bf16[384,128]{1,0:T(8,128)(2,1)}, bf16[384,128]{1,0:T(8,128)(2,1)S(1)}, u32[]{:S(2)}) copy-start(bf16[384,128]{1,0:T(8,128)(2,1)S(1)} %collective-permute-done.5.refs_6_) | copy-start | bytes 294916
  57.8 10.5 %collective-permute-start.10 = (bf16[2048,128]{1,0:T(8,128)(2,1)S(1)}, bf16[2048,128]{1,0:T(8,128)(2,1)S(1)}, u32[]{:S(2)}, u32[]{:S(2)}) collective-permute-start(bf16[2048,128]{1,0:T(8,128)(2,1)S(1)} %slice.44), channel_id=1, source_target_pairs={{0,32},{4,12},{8,40},{12,20},{16,48},{20,28},{24,56},{28,4},{32,64... | collective-permute-start | bytes 1572872 | tf_op jit(solution)/shard_map/ppermute | solution.py:495
  58.5 17.5 %collective-permute-start.16 = (bf16[4096,128]{1,0:T(8,128)(2,1)}, bf16[4096,128]{1,0:T(8,128)(2,1)}, u32[]{:S(2)}, u32[]{:S(2)}) collective-permute-start(bf16[4096,128]{1,0:T(8,128)(2,1)} %collective-permute-done.4), channel_id=1, source_target_pairs={{0,4},{4,0},{8,12},{12,8},{16,20},{20,16},{24,28},{28,24},{32,36},... | collective-permute-start | bytes 3145736 | tf_op jit(solution)/shard_map/ppermute | solution.py:490
  61.6 14.3 %copy-start.9 = (bf16[2048,128]{1,0:T(8,128)(2,1)}, bf16[2048,128]{1,0:T(8,128)(2,1)S(1)}, u32[]{:S(2)}) copy-start(bf16[2048,128]{1,0:T(8,128)(2,1)S(1)} %collective-permute-done.11) | copy-start | bytes 1572868
  61.6 14.3 %collective-permute-start.8 = (bf16[16,144,128]{2,1,0:T(8,128)(2,1)S(1)}, bf16[16,144,128]{2,1,0:T(8,128)(2,1)}, u32[]{:S(2)}, u32[]{:S(2)}) collective-permute-start(bf16[16,144,128]{2,1,0:T(8,128)(2,1)S(1)} %get-tuple-element.94), channel_id=1, source_target_pairs={{0,1},{1,0},{2,3},{3,2},{4,5},{5,4},{6,7},{7,6},{8,9},{9,8},{10,11... | collective-permute-start | bytes 1769480 | tf_op jit(solution)/shard_map/ppermute | solution.py:542
  68.2 7.7 %copy-start.10 = (bf16[2048,128]{1,0:T(8,128)(2,1)}, bf16[2048,128]{1,0:T(8,128)(2,1)S(1)}, u32[]{:S(2)}) copy-start(bf16[2048,128]{1,0:T(8,128)(2,1)S(1)} %collective-permute-done.10) | copy-start | bytes 1572868
  68.2 7.7 %collective-permute-start.15 = (bf16[2048,128]{1,0:T(8,128)(2,1)S(1)}, bf16[2048,128]{1,0:T(8,128)(2,1)S(1)}, u32[]{:S(2)}, u32[]{:S(2)}) collective-permute-start(bf16[2048,128]{1,0:T(8,128)(2,1)S(1)} %collective-permute-done.11), channel_id=1, source_target_pairs={{0,4},{4,0},{8,12},{12,8},{16,20},{20,16},{24,28},{28,24},{32,36},... | collective-permute-start | bytes 1572872 | tf_op jit(solution)/shard_map/ppermute | solution.py:490
  71.5 4.6 %collective-permute-start.14 = (bf16[2048,128]{1,0:T(8,128)(2,1)S(1)}, bf16[2048,128]{1,0:T(8,128)(2,1)S(1)}, u32[]{:S(2)}, u32[]{:S(2)}) collective-permute-start(bf16[2048,128]{1,0:T(8,128)(2,1)S(1)} %collective-permute-done.10), channel_id=1, source_target_pairs={{0,4},{4,0},{8,12},{12,8},{16,20},{20,16},{24,28},{28,24},{32,36},... | collective-permute-start | bytes 1572872 | tf_op jit(solution)/shard_map/ppermute | solution.py:490
  90.6 17.7 %copy-start.19 = (bf16[1024,128]{1,0:T(8,128)(2,1)S(1)}, bf16[1024,128]{1,0:T(8,128)(2,1)}, u32[]{:S(2)}) copy-start(bf16[1024,128]{1,0:T(8,128)(2,1)} %param.13) | copy-start | bytes 786436
  90.6 22.8 %copy-start.5 = (bf16[1024,1024]{1,0:T(8,128)(2,1)S(1)}, bf16[1024,1024]{1,0:T(8,128)(2,1)}, u32[]{:S(2)}) copy-start(bf16[1024,1024]{1,0:T(8,128)(2,1)} %get-tuple-element.76) | copy-start | bytes 6291460
  90.6 7.7 %collective-permute-start.17 = (bf16[512,128]{1,0:T(8,128)(2,1)}, bf16[512,128]{1,0:T(8,128)(2,1)S(1)}, u32[]{:S(2)}, u32[]{:S(2)}) collective-permute-start(bf16[512,128]{1,0:T(8,128)(2,1)} %get-tuple-element.70), channel_id=1, source_target_pairs={{0,1},{1,2},{2,3},{3,0},{4,5},{5,6},{6,7},{7,4},{8,9},{9,10},{10,1... | collective-permute-start | bytes 393224 | tf_op jit(solution)/shard_map/ppermute | solution.py:522
  91.0 13.6 %collective-permute-start.19 = (bf16[512,128]{1,0:T(8,128)(2,1)}, bf16[512,128]{1,0:T(8,128)(2,1)S(1)}, u32[]{:S(2)}, u32[]{:S(2)}) collective-permute-start(bf16[512,128]{1,0:T(8,128)(2,1)} %get-tuple-element.71), channel_id=1, source_target_pairs={{0,3},{1,0},{2,1},{3,2},{4,7},{5,4},{6,5},{7,6},{8,11},{9,8},{10,9... | collective-permute-start | bytes 393224 | tf_op jit(solution)/shard_map/ppermute | solution.py:522
  93.9 10.7 %collective-permute-start.20 = (bf16[512,128]{1,0:T(8,128)(2,1)}, bf16[512,128]{1,0:T(8,128)(2,1)S(1)}, u32[]{:S(2)}, u32[]{:S(2)}) collective-permute-start(bf16[512,128]{1,0:T(8,128)(2,1)} %get-tuple-element.72), channel_id=1, source_target_pairs={{0,1},{1,2},{2,3},{3,0},{4,5},{5,6},{6,7},{7,4},{8,9},{9,10},{10,1... | collective-permute-start | bytes 393224 | tf_op jit(solution)/shard_map/ppermute | solution.py:522
  94.0 6.1 %collective-permute-start.21 = (bf16[512,128]{1,0:T(8,128)(2,1)}, bf16[512,128]{1,0:T(8,128)(2,1)S(1)}, u32[]{:S(2)}, u32[]{:S(2)}) collective-permute-start(bf16[512,128]{1,0:T(8,128)(2,1)} %get-tuple-element.74), channel_id=1, source_target_pairs={{0,3},{1,0},{2,1},{3,2},{4,7},{5,4},{6,5},{7,6},{8,11},{9,8},{10,9... | collective-permute-start | bytes 393224 | tf_op jit(solution)/shard_map/ppermute | solution.py:522
  99.3 6.2 %collective-permute-start.18 = (bf16[512,128]{1,0:T(8,128)(2,1)S(1)}, bf16[512,128]{1,0:T(8,128)(2,1)S(1)}, u32[]{:S(2)}, u32[]{:S(2)}) collective-permute-start(bf16[512,128]{1,0:T(8,128)(2,1)S(1)} %add_convert_fusion.5), channel_id=1, source_target_pairs={{0,1},{1,2},{2,3},{3,0},{4,5},{5,6},{6,7},{7,4},{8,9},{9,10},{10,1... | collective-permute-start | bytes 393224 | tf_op jit(solution)/shard_map/ppermute | solution.py:522
  101.0 6.1 %collective-permute-start.22 = (bf16[512,128]{1,0:T(8,128)(2,1)S(1)}, bf16[512,128]{1,0:T(8,128)(2,1)S(1)}, u32[]{:S(2)}, u32[]{:S(2)}) collective-permute-start(bf16[512,128]{1,0:T(8,128)(2,1)S(1)} %add_convert_fusion.4), channel_id=1, source_target_pairs={{0,3},{1,0},{2,1},{3,2},{4,7},{5,4},{6,5},{7,6},{8,11},{9,8},{10,9... | collective-permute-start | bytes 393224 | tf_op jit(solution)/shard_map/ppermute | solution.py:522
  109.2 32.8 %copy-start = (bf16[1024,128]{1,0:T(8,128)(2,1)}, bf16[1024,128]{1,0:T(8,128)(2,1)S(1)}, u32[]{:S(2)}) copy-start(bf16[1024,128]{1,0:T(8,128)(2,1)S(1)} %get-tuple-element.97.z0_ref.refs_4_) | copy-start | bytes 786436
  109.2 9.6 %collective-permute-start.25 = (bf16[1024,128]{1,0:T(8,128)(2,1)S(1)}, bf16[1024,128]{1,0:T(8,128)(2,1)S(1)}, u32[]{:S(2)}, u32[]{:S(2)}) collective-permute-start(bf16[1024,128]{1,0:T(8,128)(2,1)S(1)} %get-tuple-element.97.z0_ref.refs_4_), channel_id=1, source_target_pairs={{0,24},{4,100},{8,0},{12,108},{16,8},{20,116},{24,16},{28,124},{32... | collective-permute-start | bytes 786440 | tf_op jit(solution)/shard_map/ppermute | solution.py:495
  112.1 8.0 %collective-permute-start.24 = (bf16[1024,128]{1,0:T(8,128)(2,1)S(1)}, bf16[1024,128]{1,0:T(8,128)(2,1)S(1)}, u32[]{:S(2)}, u32[]{:S(2)}) collective-permute-start(bf16[1024,128]{1,0:T(8,128)(2,1)S(1)} %get-tuple-element.97.z0_ref.refs_4_), channel_id=1, source_target_pairs={{0,16},{4,68},{8,24},{12,76},{16,0},{20,84},{24,8},{28,92},{32,48}... | collective-permute-start | bytes 786440 | tf_op jit(solution)/shard_map/ppermute | solution.py:495
  113.5 9.3 %collective-permute-start.23 = (bf16[1024,128]{1,0:T(8,128)(2,1)S(1)}, bf16[1024,128]{1,0:T(8,128)(2,1)S(1)}, u32[]{:S(2)}, u32[]{:S(2)}) collective-permute-start(bf16[1024,128]{1,0:T(8,128)(2,1)S(1)} %get-tuple-element.97.z0_ref.refs_4_), channel_id=1, source_target_pairs={{0,8},{4,36},{8,16},{12,44},{16,24},{20,52},{24,0},{28,60},{32,40}... | collective-permute-start | bytes 786440 | tf_op jit(solution)/shard_map/ppermute | solution.py:495
  115.0 27.0 %copy-start.2 = (bf16[1024,128]{1,0:T(8,128)(2,1)S(1)}, bf16[1024,128]{1,0:T(8,128)(2,1)}, u32[]{:S(2)}) copy-start(bf16[1024,128]{1,0:T(8,128)(2,1)} %left_3_ref.1) | copy-start | bytes 786436
  115.0 27.0 %copy-start.3 = (bf16[1024,128]{1,0:T(8,128)(2,1)S(1)}, bf16[1024,128]{1,0:T(8,128)(2,1)}, u32[]{:S(2)}) copy-start(bf16[1024,128]{1,0:T(8,128)(2,1)} %get-tuple-element.80.left_1_ref) | copy-start | bytes 786436
  115.0 27.0 %copy-start.4 = (bf16[1024,128]{1,0:T(8,128)(2,1)S(1)}, bf16[1024,128]{1,0:T(8,128)(2,1)}, u32[]{:S(2)}) copy-start(bf16[1024,128]{1,0:T(8,128)(2,1)} %get-tuple-element.81.left_2_ref) | copy-start | bytes 786436
  122.8 27.0 %copy-start.6 = (bf16[4096,128]{1,0:T(8,128)(2,1)}, bf16[4096,128]{1,0:T(8,128)(2,1)S(1)}, u32[]{:S(2)}) copy-start(bf16[4096,128]{1,0:T(8,128)(2,1)S(1)} %pad_maximum_fusion.1) | copy-start | bytes 3145732
  122.8 21.0 %collective-permute-start.27 = (bf16[4096,128]{1,0:T(8,128)(2,1)S(1)}, bf16[4096,128]{1,0:T(8,128)(2,1)S(1)}, u32[]{:S(2)}, u32[]{:S(2)}) collective-permute-start(bf16[4096,128]{1,0:T(8,128)(2,1)S(1)} %pad_maximum_fusion.1), channel_id=1, source_target_pairs={{0,96},{4,28},{8,104},{12,4},{16,112},{20,12},{24,120},{28,20},{32... | collective-permute-start | bytes 3145736 | tf_op jit(solution)/shard_map/ppermute | solution.py:495
  128.0 16.1 %collective-permute-start.26 = (bf16[4096,128]{1,0:T(8,128)(2,1)S(1)}, bf16[4096,128]{1,0:T(8,128)(2,1)}, u32[]{:S(2)}, u32[]{:S(2)}) collective-permute-start(bf16[4096,128]{1,0:T(8,128)(2,1)S(1)} %pad_maximum_fusion.1), channel_id=1, source_target_pairs={{0,32},{4,12},{8,40},{12,20},{16,48},{20,28},{24,56},{28,4},{32,64... | collective-permute-start | bytes 3145736 | tf_op jit(solution)/shard_map/ppermute | solution.py:495
  128.0 10.4 %collective-permute-start.30 = (bf16[1024,128]{1,0:T(8,128)(2,1)S(1)}, bf16[1024,128]{1,0:T(8,128)(2,1)S(1)}, u32[]{:S(2)}, u32[]{:S(2)}) collective-permute-start(bf16[1024,128]{1,0:T(8,128)(2,1)S(1)} %get-tuple-element.97.z0_ref.refs_4_), channel_id=1, source_target_pairs={{0,3},{1,0},{2,1},{3,2},{4,7},{5,4},{6,5},{7,6},{8,11},{9,8},{10,9... | collective-permute-start | bytes 786440 | tf_op jit(solution)/shard_map/ppermute | solution.py:522
  131.7 8.0 %collective-permute-start.29 = (bf16[1024,128]{1,0:T(8,128)(2,1)S(1)}, bf16[1024,128]{1,0:T(8,128)(2,1)S(1)}, u32[]{:S(2)}, u32[]{:S(2)}) collective-permute-start(bf16[1024,128]{1,0:T(8,128)(2,1)S(1)} %get-tuple-element.97.z0_ref.refs_4_), channel_id=1, source_target_pairs={{0,2},{1,3},{2,0},{3,1},{4,6},{5,7},{6,4},{7,5},{8,10},{9,11},{10,... | collective-permute-start | bytes 786440 | tf_op jit(solution)/shard_map/ppermute | solution.py:522
  131.7 10.4 %collective-permute-start.28 = (bf16[1024,128]{1,0:T(8,128)(2,1)S(1)}, bf16[1024,128]{1,0:T(8,128)(2,1)S(1)}, u32[]{:S(2)}, u32[]{:S(2)}) collective-permute-start(bf16[1024,128]{1,0:T(8,128)(2,1)S(1)} %get-tuple-element.97.z0_ref.refs_4_), channel_id=1, source_target_pairs={{0,1},{1,2},{2,3},{3,0},{4,5},{5,6},{6,7},{7,4},{8,9},{9,10},{10,1... | collective-permute-start | bytes 786440 | tf_op jit(solution)/shard_map/ppermute | solution.py:522
  138.4 22.2 %collective-permute-start.33 = (bf16[4096,128]{1,0:T(8,128)(2,1)S(1)}, bf16[4096,128]{1,0:T(8,128)(2,1)}, u32[]{:S(2)}, u32[]{:S(2)}) collective-permute-start(bf16[4096,128]{1,0:T(8,128)(2,1)S(1)} %pad_maximum_fusion.1), channel_id=1, source_target_pairs={{0,4},{4,0},{8,12},{12,8},{16,20},{20,16},{24,28},{28,24},{32,36},... | collective-permute-start | bytes 3145736 | tf_op jit(solution)/shard_map/ppermute | solution.py:490
  143.8 16.7 %copy-start.8 = (bf16[4096,128]{1,0:T(8,128)(2,1)}, bf16[4096,128]{1,0:T(8,128)(2,1)S(1)}, u32[]{:S(2)}) copy-start(bf16[4096,128]{1,0:T(8,128)(2,1)S(1)} %collective-permute-done.27) | copy-start | bytes 3145732
  145.1 12.9 %collective-permute-start.32 = (bf16[2048,128]{1,0:T(8,128)(2,1)}, bf16[2048,128]{1,0:T(8,128)(2,1)}, u32[]{:S(2)}, u32[]{:S(2)}) collective-permute-start(bf16[2048,128]{1,0:T(8,128)(2,1)} %slice.49), channel_id=1, source_target_pairs={{0,96},{4,28},{8,104},{12,4},{16,112},{20,12},{24,120},{28,20},{32... | collective-permute-start | bytes 1572872 | tf_op jit(solution)/shard_map/ppermute | solution.py:495
  149.8 10.7 %collective-permute-start.31 = (bf16[2048,128]{1,0:T(8,128)(2,1)}, bf16[2048,128]{1,0:T(8,128)(2,1)}, u32[]{:S(2)}, u32[]{:S(2)}) collective-permute-start(bf16[2048,128]{1,0:T(8,128)(2,1)} %slice.48), channel_id=1, source_target_pairs={{0,32},{4,12},{8,40},{12,20},{16,48},{20,28},{24,56},{28,4},{32,64... | collective-permute-start | bytes 1572872 | tf_op jit(solution)/shard_map/ppermute | solution.py:495
  149.8 12.8 %collective-permute-start.34 = (bf16[4096,128]{1,0:T(8,128)(2,1)}, bf16[4096,128]{1,0:T(8,128)(2,1)}, u32[]{:S(2)}, u32[]{:S(2)}) collective-permute-start(bf16[4096,128]{1,0:T(8,128)(2,1)} %collective-permute-done.26), channel_id=1, source_target_pairs={{0,4},{4,0},{8,12},{12,8},{16,20},{20,16},{24,28},{28,24},{32,36},... | collective-permute-start | bytes 3145736 | tf_op jit(solution)/shard_map/ppermute | solution.py:490
  149.8 12.8 %collective-permute-start.37 = (bf16[4096,128]{1,0:T(8,128)(2,1)S(1)}, bf16[4096,128]{1,0:T(8,128)(2,1)}, u32[]{:S(2)}, u32[]{:S(2)}) collective-permute-start(bf16[4096,128]{1,0:T(8,128)(2,1)S(1)} %collective-permute-done.27), channel_id=1, source_target_pairs={{0,4},{4,0},{8,12},{12,8},{16,20},{20,16},{24,28},{28,24},{32,36},... | collective-permute-start | bytes 3145736 | tf_op jit(solution)/shard_map/ppermute | solution.py:490
  150.3 25.4 %all-to-all-start.1 = ((f32[32,48,128]{2,1,0:T(8,128)}), f32[32,48,128]{2,1,0:T(8,128)S(1)}, u32[]{:S(2)}, u32[]{:S(2)}) async-start(f32[32,48,128]{2,1,0:T(8,128)} %slopes.1), calls=%async_computation.1 | async-start | bytes 1572864 | tf_op jit(solution)/shard_map/all_to_all | solution.py:571
  157.9 2.6 %collective-permute-start.36 = (bf16[2048,128]{1,0:T(8,128)(2,1)}, bf16[2048,128]{1,0:T(8,128)(2,1)S(1)}, u32[]{:S(2)}, u32[]{:S(2)}) collective-permute-start(bf16[2048,128]{1,0:T(8,128)(2,1)} %collective-permute-done.32), channel_id=1, source_target_pairs={{0,4},{4,0},{8,12},{12,8},{16,20},{20,16},{24,28},{28,24},{32,36},... | collective-permute-start | bytes 1572872 | tf_op jit(solution)/shard_map/ppermute | solution.py:490
  160.5 2.1 %collective-permute-start.35 = (bf16[2048,128]{1,0:T(8,128)(2,1)}, bf16[2048,128]{1,0:T(8,128)(2,1)S(1)}, u32[]{:S(2)}, u32[]{:S(2)}) collective-permute-start(bf16[2048,128]{1,0:T(8,128)(2,1)} %collective-permute-done.31), channel_id=1, source_target_pairs={{0,4},{4,0},{8,12},{12,8},{16,20},{20,16},{24,28},{28,24},{32,36},... | collective-permute-start | bytes 1572872 | tf_op jit(solution)/shard_map/ppermute | solution.py:490
  175.6 18.5 %copy-start.18 = (f32[1024,128]{1,0:T(8,128)S(1)}, f32[1024,128]{1,0:T(8,128)}, u32[]{:S(2)}) copy-start(f32[1024,128]{1,0:T(8,128)} %get-tuple-element.84) | copy-start | bytes 1572868
  175.6 7.4 %collective-permute-start.38 = (bf16[512,128]{1,0:T(8,128)(2,1)}, bf16[512,128]{1,0:T(8,128)(2,1)S(1)}, u32[]{:S(2)}, u32[]{:S(2)}) collective-permute-start(bf16[512,128]{1,0:T(8,128)(2,1)} %get-tuple-element.86), channel_id=1, source_target_pairs={{0,1},{1,2},{2,3},{3,0},{4,5},{5,6},{6,7},{7,4},{8,9},{9,10},{10,1... | collective-permute-start | bytes 393224 | tf_op jit(solution)/shard_map/ppermute | solution.py:522
  175.8 8.3 %collective-permute-start.40 = (bf16[512,128]{1,0:T(8,128)(2,1)}, bf16[512,128]{1,0:T(8,128)(2,1)S(1)}, u32[]{:S(2)}, u32[]{:S(2)}) collective-permute-start(bf16[512,128]{1,0:T(8,128)(2,1)} %get-tuple-element.87), channel_id=1, source_target_pairs={{0,3},{1,0},{2,1},{3,2},{4,7},{5,4},{6,5},{7,6},{8,11},{9,8},{10,9... | collective-permute-start | bytes 393224 | tf_op jit(solution)/shard_map/ppermute | solution.py:522
  179.0 6.7 %collective-permute-start.41 = (bf16[512,128]{1,0:T(8,128)(2,1)}, bf16[512,128]{1,0:T(8,128)(2,1)S(1)}, u32[]{:S(2)}, u32[]{:S(2)}) collective-permute-start(bf16[512,128]{1,0:T(8,128)(2,1)} %get-tuple-element.88), channel_id=1, source_target_pairs={{0,1},{1,2},{2,3},{3,0},{4,5},{5,6},{6,7},{7,4},{8,9},{9,10},{10,1... | collective-permute-start | bytes 393224 | tf_op jit(solution)/shard_map/ppermute | solution.py:522
  179.0 7.4 %collective-permute-start.42 = (bf16[512,128]{1,0:T(8,128)(2,1)}, bf16[512,128]{1,0:T(8,128)(2,1)S(1)}, u32[]{:S(2)}, u32[]{:S(2)}) collective-permute-start(bf16[512,128]{1,0:T(8,128)(2,1)} %get-tuple-element.90), channel_id=1, source_target_pairs={{0,3},{1,0},{2,1},{3,2},{4,7},{5,4},{6,5},{7,6},{8,11},{9,8},{10,9... | collective-permute-start | bytes 393224 | tf_op jit(solution)/shard_map/ppermute | solution.py:522
  183.9 8.2 %collective-permute-start.39 = (bf16[512,128]{1,0:T(8,128)(2,1)S(1)}, bf16[512,128]{1,0:T(8,128)(2,1)S(1)}, u32[]{:S(2)}, u32[]{:S(2)}) collective-permute-start(bf16[512,128]{1,0:T(8,128)(2,1)S(1)} %add_convert_fusion.3), channel_id=1, source_target_pairs={{0,1},{1,2},{2,3},{3,0},{4,5},{5,6},{6,7},{7,4},{8,9},{9,10},{10,1... | collective-permute-start | bytes 393224 | tf_op jit(solution)/shard_map/ppermute | solution.py:522
  185.8 5.8 %collective-permute-start.44 = (f32[48,128]{1,0:T(8,128)S(1)}, f32[48,128]{1,0:T(8,128)S(1)}, u32[]{:S(2)}, u32[]{:S(2)}) collective-permute-start(f32[48,128]{1,0:T(8,128)S(1)} %reduce_sum.9), channel_id=1, source_target_pairs={{0,0},{1,33},{2,66},{3,99},{4,4},{5,37},{6,70},{7,103},{8,8},{9,41... | collective-permute-start | bytes 73736 | tf_op jit(solution)/shard_map/ppermute | solution.py:584
  187.4 6.6 %collective-permute-start.43 = (bf16[512,128]{1,0:T(8,128)(2,1)S(1)}, bf16[512,128]{1,0:T(8,128)(2,1)S(1)}, u32[]{:S(2)}, u32[]{:S(2)}) collective-permute-start(bf16[512,128]{1,0:T(8,128)(2,1)S(1)} %add_convert_fusion.1), channel_id=1, source_target_pairs={{0,3},{1,0},{2,1},{3,2},{4,7},{5,4},{6,5},{7,6},{8,11},{9,8},{10,9... | collective-permute-start | bytes 393224 | tf_op jit(solution)/shard_map/ppermute | solution.py:522
  (6 other events, 17.7 us)

commit v3 on v2

--- a/solution.py
+++ b/solution.py
@@ -565,9 +565,8 @@
     base_out = jnp.dot(local, grad_z, preferred_element_type=F32)
     base_in = jnp.einsum("ij,ik->jk", local, grad_z, preferred_element_type=F32)
     slivers = width * planes // devices
-    pieces_z, (base_out, base_in), terms = gather(
-        grad_z, devices, (base_out, base_in), lambda held: slopes([prop_out, prop_in, node_features], rights, devices)
-    )
+    pieces_z, (base_out, base_in), _ = gather(grad_z, devices, (base_out, base_in), lambda held: ())
+    terms = slopes([prop_out, prop_in, node_features], rights, devices)
     terms = lax.all_to_all(terms, "nodes", 0, 0, tiled=True)
     parts = spread(info, listed, base_out, base_in, [grad_z, w_in, w_out, w_self], arrived, others, away, pieces_z, True)
     grad_sum, middle_sum = collect(*parts, True)

time: 196 us -> 194 us (0.990)
    ppermute x18, waiting for transfers between devices: 18.2 us -> 9.05 us  [shift(): lax.ppermute(values, 'hid', [(here, (here + step) % planes) for here in r...]
    ppermute x14, waiting for transfers between devices: 26.8 us -> 34.4 us  [move(): return lax.ppermute(part, 'nodes', around(devices, stage, step))]
    ppermute x14, starting transfers between devices: 22.9 us -> 19.7 us  [move(): return lax.ppermute(part, 'nodes', around(devices, stage, step))]
    ppermute x18, starting transfers between devices: 34.5 us -> 36.7 us  [shift(): lax.ppermute(values, 'hid', [(here, (here + step) % planes) for here in r...]
  transfers between devices with their start and end apart: 47 -> 47, of which waited for: 21 -> 19; matrix products, arithmetic and copies ran while one was open for 8% -> 8% of each run, Pallas kernels for 15% -> 15%
where the time goes in v3:
time: 194 us; the launch traced here: 193 us
  starting transfers between devices  73.2 us (38%)
  waiting for transfers between devices  53.6 us (28%)
  Pallas kernels  42.8 us (22%)
  local copies, waits for them, and re-layouts  10 us (5%)
  other arithmetic  8.75 us (5%)
  matrix products  3.05 us (2%)
    ppermute x18, starting transfers between devices, shift(): lax.ppermute(values, 'hid', [(here, (here + step) % planes) for here in r...  36.7 us
    ppermute x14, waiting for transfers between devices, move(): return lax.ppermute(part, 'nodes', around(devices, stage, step))  34.4 us
    pallas_call x2, Pallas kernels, spread(): pl.pallas_call(lambda *refs: spread_kernel(turned, len(pieces), *refs), i...  25.9 us
    ppermute x14, starting transfers between devices, move(): return lax.ppermute(part, 'nodes', around(devices, stage, step))  19.7 us
    ppermute x18, waiting for transfers between devices, shift(): lax.ppermute(values, 'hid', [(here, (here + step) % planes) for here in r...  9.05 us
    pallas_call x1, Pallas kernels, pile(): pl.pallas_call(pile_kernel, in_specs=[smem, smem, smem, pl.BlockSpec(memo...  8.43 us
    all_to_all x1, starting transfers between devices, shards(): arrived = lax.all_to_all(send, 'nodes', 0, 0, tiled=True)  6.9 us
    pallas_call x1, Pallas kernels, pick(): pl.pallas_call(lambda *refs: pick_kernel(blocks, *refs), in_specs=[smem,...  6.77 us
  transfers between devices with their start and end apart: 47, of which 19 were waited for; matrix products, arithmetic and copies ran while one was open for 8% of the time, Pallas kernels for 15%

profile of v3, /device:TPU:0, one launch (start us, length us, event | category | flops | bytes accessed | tf_op | source)
XLA Modules:
  0.0 193.1 jit_solution(1189835653697550908)
XLA Ops:
  0.6 2.9 %collective-permute-start.2 = (bf16[1024,128]{1,0:T(8,128)(2,1)}, bf16[1024,128]{1,0:T(8,128)(2,1)S(1)}, u32[]{:S(2)}, u32[]{:S(2)}) collective-permute-start(bf16[1024,128]{1,0:T(8,128)(2,1)} %left_3_ref.1), channel_id=1, source_target_pairs={{0,24},{4,100},{8,0},{12,108},{16,8},{20,116},{24,16},{28,124},{32... | collective-permute-start | bytes 786440 | tf_op jit(solution)/shard_map/ppermute | solution.py:495
  3.5 0.8 collective-permute-start.1
  4.3 0.9 collective-permute-start
  6.6 6.8 %pick.1 = (bf16[64,128,128]{2,1,0:T(8,128)(2,1)}, bf16[32,144,128]{2,1,0:T(8,128)(2,1)}, s32[64]{0:T(128)}) custom-call(s32[256]{0:T(256)} %src_ref.1, s32[256]{0:T(256)} %dst_ref.1, s32[6]{0:T(128)} %stack.35.refs_2_.info_ref.refs_0_, s32[256,128,128]{2,1,0:T(8,128)} %pattern_ref.1), custom_call_target="tpu_custom_call" | custom-call | flops 1048576 | bytes 8388608 | tf_op jit(solution)/shard_map/pick/pallas_call | solution.py:105
  13.4 6.9 %all-to-all-start = ((bf16[32,144,128]{2,1,0:T(8,128)(2,1)}), bf16[32,144,128]{2,1,0:T(8,128)(2,1)}, u32[]{:S(2)}, u32[]{:S(2)}) async-start(bf16[32,144,128]{2,1,0:T(8,128)(2,1)} %get-tuple-element.49), calls=%async_computation | async-start | bytes 2359296 | tf_op jit(solution)/shard_map/all_to_all | solution.py:538
  20.3 1.1 pad_maximum_fusion
  21.5 3.0 %collective-permute-start.4 = (bf16[4096,128]{1,0:T(8,128)(2,1)}, bf16[4096,128]{1,0:T(8,128)(2,1)}, u32[]{:S(2)}, u32[]{:S(2)}) collective-permute-start(bf16[4096,128]{1,0:T(8,128)(2,1)} %pad_maximum_fusion), channel_id=1, source_target_pairs={{0,96},{4,28},{8,104},{12,4},{16,112},{20,12},{24,120},{28,20},{32... | collective-permute-start | bytes 3145736 | tf_op jit(solution)/shard_map/ppermute | solution.py:495
  25.2 3.9 %collective-permute-start.6 = (bf16[384,128]{1,0:T(8,128)(2,1)S(1)}, bf16[384,128]{1,0:T(8,128)(2,1)S(1)}, u32[]{:S(2)}, u32[]{:S(2)}) collective-permute-start(bf16[384,128]{1,0:T(8,128)(2,1)S(1)} %bitcast.55), channel_id=1, source_target_pairs={{0,2},{1,3},{2,0},{3,1},{4,6},{5,7},{6,4},{7,5},{8,10},{9,11},{10,... | collective-permute-start | bytes 294920 | tf_op jit(solution)/shard_map/ppermute | solution.py:522
  29.1 1.0 collective-permute-start.7
  30.1 8.4 %pile.1 = (bf16[1024,1024]{1,0:T(8,128)(2,1)}, f32[1024,128]{1,0:T(8,128)}, f32[1024,128]{1,0:T(8,128)}) custom-call(s32[256]{0:T(256)} %src_ref.1, s32[256]{0:T(256)} %dst_ref.1, s32[6]{0:T(128)} %stack.35.refs_2_.info_ref.refs_0_, s32[256,128,128]{2,1,0:T(8,128)} %pattern_ref.1, bf16[1024,128]{1,0:T(8,128)(2,1)} %left_3_ref.1), custom_call_target="tpu_custom_call" | custom-call | flops 4194304 | bytes 16777216 | tf_op jit(solution)/shard_map/pile/pallas_call | solution.py:192
  38.6 8.5 %collective-permute-done.4 = bf16[4096,128]{1,0:T(8,128)(2,1)} collective-permute-done((bf16[4096,128]{1,0:T(8,128)(2,1)}, bf16[4096,128]{1,0:T(8,128)(2,1)}, u32[]{:S(2)}, u32[]{:S(2)}) %collective-permute-start.4) | collective-permute-done | bytes 1048608 | tf_op jit(solution)/shard_map/ppermute | solution.py:495
  47.1 4.0 %collective-permute-start.5 = (bf16[384,128]{1,0:T(8,128)(2,1)S(1)}, bf16[384,128]{1,0:T(8,128)(2,1)S(1)}, u32[]{:S(2)}, u32[]{:S(2)}) collective-permute-start(bf16[384,128]{1,0:T(8,128)(2,1)S(1)} %bitcast.54), channel_id=1, source_target_pairs={{0,3},{1,0},{2,1},{3,2},{4,7},{5,4},{6,5},{7,6},{8,11},{9,8},{10,9... | collective-permute-start | bytes 294920 | tf_op jit(solution)/shard_map/ppermute | solution.py:522
  51.1 1.1 slice.45
  52.2 2.3 %collective-permute-start.11 = (bf16[2048,128]{1,0:T(8,128)(2,1)S(1)}, bf16[2048,128]{1,0:T(8,128)(2,1)S(1)}, u32[]{:S(2)}, u32[]{:S(2)}) collective-permute-start(bf16[2048,128]{1,0:T(8,128)(2,1)S(1)} %slice.45), channel_id=1, source_target_pairs={{0,96},{4,28},{8,104},{12,4},{16,112},{20,12},{24,120},{28,20},{32... | collective-permute-start | bytes 1572872 | tf_op jit(solution)/shard_map/ppermute | solution.py:495
  54.5 1.3 fusion
  56.4 1.1 slice.44
  58.3 0.8 collective-permute-start.16
  59.1 2.4 %collective-permute-done.11 = bf16[2048,128]{1,0:T(8,128)(2,1)S(1)} collective-permute-done((bf16[2048,128]{1,0:T(8,128)(2,1)S(1)}, bf16[2048,128]{1,0:T(8,128)(2,1)S(1)}, u32[]{:S(2)}, u32[]{:S(2)}) %collective-permute-start.11) | collective-permute-done | bytes 524320 | tf_op jit(solution)/shard_map/ppermute | solution.py:495
  61.4 6.6 %collective-permute-done.10 = bf16[2048,128]{1,0:T(8,128)(2,1)S(1)} collective-permute-done((bf16[2048,128]{1,0:T(8,128)(2,1)S(1)}, bf16[2048,128]{1,0:T(8,128)(2,1)S(1)}, u32[]{:S(2)}, u32[]{:S(2)}) %collective-permute-start.10) | collective-permute-done | bytes 524320 | tf_op jit(solution)/shard_map/ppermute | solution.py:495
  68.0 3.2 %collective-permute-done.9.refs_11_.refs_10_ = bf16[16,144,128]{2,1,0:T(8,128)(2,1)S(1)} collective-permute-done((bf16[16,144,128]{2,1,0:T(8,128)(2,1)S(1)}, bf16[16,144,128]{2,1,0:T(8,128)(2,1)S(1)}, u32[]{:S(2)}, u32[]{:S(2)}) %collective-permute-start.9) | collective-permute-done | bytes 589856 | tf_op jit(solution)/shard_map/ppermute | solution.py:543
  71.2 4.5 %collective-permute-done.8.refs_10_.refs_9_ = bf16[16,144,128]{2,1,0:T(8,128)(2,1)} collective-permute-done((bf16[16,144,128]{2,1,0:T(8,128)(2,1)S(1)}, bf16[16,144,128]{2,1,0:T(8,128)(2,1)}, u32[]{:S(2)}, u32[]{:S(2)}) %collective-permute-start.8) | collective-permute-done | bytes 589856 | tf_op jit(solution)/shard_map/ppermute | solution.py:542
  75.8 0.8 copy-done.11
  76.6 0.8 copy-done.12
  77.4 13.4 %spread.2 = (f32[1024,128]{1,0:T(8,128)}, f32[512,128]{1,0:T(8,128)}, bf16[512,128]{1,0:T(8,128)(2,1)}, bf16[512,128]{1,0:T(8,128)(2,1)}, bf16[512,128]{1,0:T(8,...) custom-call(s32[6]{0:T(128)} %stack.35.refs_2_.info_ref.refs_0_, ...), custom_call_target="tpu_custom_call" | custom-call | flops 671088640 | bytes 16777216 | tf_op jit(solution)/shard_map/spread/pallas_call | solution.py:433
  91.2 2.9 %collective-permute-start.19 = (bf16[512,128]{1,0:T(8,128)(2,1)}, bf16[512,128]{1,0:T(8,128)(2,1)S(1)}, u32[]{:S(2)}, u32[]{:S(2)}) collective-permute-start(bf16[512,128]{1,0:T(8,128)(2,1)} %get-tuple-element.70), channel_id=1, source_target_pairs={{0,3},{1,0},{2,1},{3,2},{4,7},{5,4},{6,5},{7,6},{8,11},{9,8},{10,9... | collective-permute-start | bytes 393224 | tf_op jit(solution)/shard_map/ppermute | solution.py:522
  94.1 3.2 %collective-permute-start.21 = (bf16[512,128]{1,0:T(8,128)(2,1)}, bf16[512,128]{1,0:T(8,128)(2,1)S(1)}, u32[]{:S(2)}, u32[]{:S(2)}) collective-permute-start(bf16[512,128]{1,0:T(8,128)(2,1)} %get-tuple-element.73), channel_id=1, source_target_pairs={{0,3},{1,0},{2,1},{3,2},{4,7},{5,4},{6,5},{7,6},{8,11},{9,8},{10,9... | collective-permute-start | bytes 393224 | tf_op jit(solution)/shard_map/ppermute | solution.py:522
  97.4 1.3 collective-permute-done.17
  98.6 1.0 add_convert_fusion.5
  100.2 1.0 add_convert_fusion.4
  101.2 3.6 %collective-permute-start.22 = (bf16[512,128]{1,0:T(8,128)(2,1)S(1)}, bf16[512,128]{1,0:T(8,128)(2,1)S(1)}, u32[]{:S(2)}, u32[]{:S(2)}) collective-permute-start(bf16[512,128]{1,0:T(8,128)(2,1)S(1)} %add_convert_fusion.4), channel_id=1, source_target_pairs={{0,3},{1,0},{2,1},{3,2},{4,7},{5,4},{6,5},{7,6},{8,11},{9,8},{10,9... | collective-permute-start | bytes 393224 | tf_op jit(solution)/shard_map/ppermute | solution.py:522
  104.8 1.0 collective-permute-done.18
  105.9 1.5 collective-permute-done.22
  107.3 1.1 convert_add_fusion.1
  108.5 1.0 multiply_convert_fusion
  109.4 2.2 %collective-permute-start.25 = (bf16[1024,128]{1,0:T(8,128)(2,1)S(1)}, bf16[1024,128]{1,0:T(8,128)(2,1)S(1)}, u32[]{:S(2)}, u32[]{:S(2)}) collective-permute-start(bf16[1024,128]{1,0:T(8,128)(2,1)S(1)} %get-tuple-element.95.refs_4_.z0_ref), channel_id=1, source_target_pairs={{0,24},{4,100},{8,0},{12,108},{16,8},{20,116},{24,16},{28,124},{32... | collective-permute-start | bytes 786440 | tf_op jit(solution)/shard_map/ppermute | solution.py:495
  111.6 1.4 collective-permute-start.24
  113.5 1.6 fusion.3.refs_3_
  115.1 1.5 fusion.2.refs_2_
  116.6 1.7 collective-permute-done.25
  118.3 1.2 collective-permute-done.24
  119.6 2.7 %collective-permute-done.23 = bf16[1024,128]{1,0:T(8,128)(2,1)S(1)} collective-permute-done((bf16[1024,128]{1,0:T(8,128)(2,1)S(1)}, bf16[1024,128]{1,0:T(8,128)(2,1)S(1)}, u32[]{:S(2)}, u32[]{:S(2)}) %collective-permute-start.23) | collective-permute-done | bytes 262176 | tf_op jit(solution)/shard_map/ppermute | solution.py:495
  122.4 3.0 %collective-permute-start.27 = (bf16[4096,128]{1,0:T(8,128)(2,1)S(1)}, bf16[4096,128]{1,0:T(8,128)(2,1)S(1)}, u32[]{:S(2)}, u32[]{:S(2)}) collective-permute-start(bf16[4096,128]{1,0:T(8,128)(2,1)S(1)} %pad_maximum_fusion.1), channel_id=1, source_target_pairs={{0,96},{4,28},{8,104},{12,4},{16,112},{20,12},{24,120},{28,20},{32... | collective-permute-start | bytes 3145736 | tf_op jit(solution)/shard_map/ppermute | solution.py:495
  125.3 3.9 %collective-permute-start.43 = (bf16[1024,128]{1,0:T(8,128)(2,1)S(1)}, bf16[1024,128]{1,0:T(8,128)(2,1)S(1)}, u32[]{:S(2)}, u32[]{:S(2)}) collective-permute-start(bf16[1024,128]{1,0:T(8,128)(2,1)S(1)} %get-tuple-element.95.refs_4_.z0_ref), channel_id=1, source_target_pairs={{0,3},{1,0},{2,1},{3,2},{4,7},{5,4},{6,5},{7,6},{8,11},{9,8},{10,9... | collective-permute-start | bytes 786440 | tf_op jit(solution)/shard_map/ppermute | solution.py:522
  129.2 0.9 collective-permute-start.41
  130.1 7.7 %collective-permute-done.27 = bf16[4096,128]{1,0:T(8,128)(2,1)S(1)} collective-permute-done((bf16[4096,128]{1,0:T(8,128)(2,1)S(1)}, bf16[4096,128]{1,0:T(8,128)(2,1)S(1)}, u32[]{:S(2)}, u32[]{:S(2)}) %collective-permute-start.27) | collective-permute-done | bytes 1048608 | tf_op jit(solution)/shard_map/ppermute | solution.py:495
  137.8 3.6 %collective-permute-done.26 = bf16[4096,128]{1,0:T(8,128)(2,1)} collective-permute-done((bf16[4096,128]{1,0:T(8,128)(2,1)S(1)}, bf16[4096,128]{1,0:T(8,128)(2,1)}, u32[]{:S(2)}, u32[]{:S(2)}) %collective-permute-start.26) | collective-permute-done | bytes 1048608 | tf_op jit(solution)/shard_map/ppermute | solution.py:495
  141.4 1.9 slice.48
  143.3 0.8 slice.49
  144.8 1.4 collective-permute-start.28
  146.7 1.7 slopes.1
  148.4 6.7 %all-to-all-start.1 = ((f32[32,48,128]{2,1,0:T(8,128)}), f32[32,48,128]{2,1,0:T(8,128)S(1)}, u32[]{:S(2)}, u32[]{:S(2)}) async-start(f32[32,48,128]{2,1,0:T(8,128)} %slopes.1), calls=%async_computation.1 | async-start | bytes 1572864 | tf_op jit(solution)/shard_map/all_to_all | solution.py:570
  155.8 1.6 collective-permute-done.33
  157.4 0.7 collective-permute-done.32
  158.2 0.7 copy-done.17
  158.9 12.5 %spread.3 = (f32[1024,128]{1,0:T(8,128)}, f32[512,128]{1,0:T(8,128)}, bf16[512,128]{1,0:T(8,128)(2,1)}, bf16[512,128]{1,0:T(8,128)(2,1)}, bf16[512,128]{1,0:T(8,...) custom-call(s32[6]{0:T(128)} %stack.35.refs_2_.info_ref.refs_0_, s32[146]{0:T(256)} %get-tuple-element.74.refs_1_, ...), custom_call_target="tpu_custom_call" | custom-call | flops 671088640 | bytes 16777216 | tf_op jit(solution)/shard_map/spread/pallas_call | solution.py:433
  171.6 3.7 %collective-permute-start.37 = (bf16[512,128]{1,0:T(8,128)(2,1)}, bf16[512,128]{1,0:T(8,128)(2,1)S(1)}, u32[]{:S(2)}, u32[]{:S(2)}) collective-permute-start(bf16[512,128]{1,0:T(8,128)(2,1)} %get-tuple-element.84), channel_id=1, source_target_pairs={{0,3},{1,0},{2,1},{3,2},{4,7},{5,4},{6,5},{7,6},{8,11},{9,8},{10,9... | collective-permute-start | bytes 393224 | tf_op jit(solution)/shard_map/ppermute | solution.py:522
  175.3 3.2 %collective-permute-start.39 = (bf16[512,128]{1,0:T(8,128)(2,1)}, bf16[512,128]{1,0:T(8,128)(2,1)S(1)}, u32[]{:S(2)}, u32[]{:S(2)}) collective-permute-start(bf16[512,128]{1,0:T(8,128)(2,1)} %get-tuple-element.87), channel_id=1, source_target_pairs={{0,3},{1,0},{2,1},{3,2},{4,7},{5,4},{6,5},{7,6},{8,11},{9,8},{10,9... | collective-permute-start | bytes 393224 | tf_op jit(solution)/shard_map/ppermute | solution.py:522
  178.6 1.1 collective-permute-done.35
  179.7 1.0 add_convert_fusion.3
  180.7 1.8 collective-permute-done.38
  183.1 1.0 add_convert_fusion.1
  184.1 5.6 %collective-permute-start.40 = (bf16[512,128]{1,0:T(8,128)(2,1)S(1)}, bf16[512,128]{1,0:T(8,128)(2,1)S(1)}, u32[]{:S(2)}, u32[]{:S(2)}) collective-permute-start(bf16[512,128]{1,0:T(8,128)(2,1)S(1)} %add_convert_fusion.1), channel_id=1, source_target_pairs={{0,3},{1,0},{2,1},{3,2},{4,7},{5,4},{6,5},{7,6},{8,11},{9,8},{10,9... | collective-permute-start | bytes 393224 | tf_op jit(solution)/shard_map/ppermute | solution.py:522
  190.4 1.9 collective-permute-done.40
  192.4 0.7 pad_maximum_fusion.4
  (103 shorter events, 7.9 us)
Async XLA Ops:
  0.6 19.7 %collective-permute-start.2 = (bf16[1024,128]{1,0:T(8,128)(2,1)}, bf16[1024,128]{1,0:T(8,128)(2,1)S(1)}, u32[]{:S(2)}, u32[]{:S(2)}) collective-permute-start(bf16[1024,128]{1,0:T(8,128)(2,1)} %left_3_ref.1), channel_id=1, source_target_pairs={{0,24},{4,100},{8,0},{12,108},{16,8},{20,116},{24,16},{28,124},{32... | collective-permute-start | bytes 786440 | tf_op jit(solution)/shard_map/ppermute | solution.py:495
  3.5 16.8 %collective-permute-start.1 = (bf16[1024,128]{1,0:T(8,128)(2,1)}, bf16[1024,128]{1,0:T(8,128)(2,1)S(1)}, u32[]{:S(2)}, u32[]{:S(2)}) collective-permute-start(bf16[1024,128]{1,0:T(8,128)(2,1)} %left_3_ref.1), channel_id=1, source_target_pairs={{0,16},{4,68},{8,24},{12,76},{16,0},{20,84},{24,8},{28,92},{32,48}... | collective-permute-start | bytes 786440 | tf_op jit(solution)/shard_map/ppermute | solution.py:495
  4.3 16.0 %collective-permute-start = (bf16[1024,128]{1,0:T(8,128)(2,1)}, bf16[1024,128]{1,0:T(8,128)(2,1)S(1)}, u32[]{:S(2)}, u32[]{:S(2)}) collective-permute-start(bf16[1024,128]{1,0:T(8,128)(2,1)} %left_3_ref.1), channel_id=1, source_target_pairs={{0,8},{4,36},{8,16},{12,44},{16,24},{20,52},{24,0},{28,60},{32,40}... | collective-permute-start | bytes 786440 | tf_op jit(solution)/shard_map/ppermute | solution.py:495
  13.4 11.1 %copy-start.13 = (bf16[512,128]{1,0:T(8,128)(2,1)S(1)}, bf16[512,128]{1,0:T(8,128)(2,1)}, u32[]{:S(2)}) copy-start(bf16[512,128]{1,0:T(8,128)(2,1)} %refs_7_.1) | copy-start | bytes 393220
  13.4 11.1 %copy-start.14 = (bf16[512,128]{1,0:T(8,128)(2,1)S(1)}, bf16[512,128]{1,0:T(8,128)(2,1)}, u32[]{:S(2)}) copy-start(bf16[512,128]{1,0:T(8,128)(2,1)} %refs_5_.1) | copy-start | bytes 393220
  13.4 11.1 %copy-start.15 = (bf16[512,128]{1,0:T(8,128)(2,1)S(1)}, bf16[512,128]{1,0:T(8,128)(2,1)}, u32[]{:S(2)}) copy-start(bf16[512,128]{1,0:T(8,128)(2,1)} %refs_6_.1) | copy-start | bytes 393220
  13.4 37.7 %all-to-all-start = ((bf16[32,144,128]{2,1,0:T(8,128)(2,1)}), bf16[32,144,128]{2,1,0:T(8,128)(2,1)}, u32[]{:S(2)}, u32[]{:S(2)}) async-start(bf16[32,144,128]{2,1,0:T(8,128)(2,1)} %get-tuple-element.49), calls=%async_computation | async-start | bytes 2359296 | tf_op jit(solution)/shard_map/all_to_all | solution.py:538
  21.5 25.6 %collective-permute-start.4 = (bf16[4096,128]{1,0:T(8,128)(2,1)}, bf16[4096,128]{1,0:T(8,128)(2,1)}, u32[]{:S(2)}, u32[]{:S(2)}) collective-permute-start(bf16[4096,128]{1,0:T(8,128)(2,1)} %pad_maximum_fusion), channel_id=1, source_target_pairs={{0,96},{4,28},{8,104},{12,4},{16,112},{20,12},{24,120},{28,20},{32... | collective-permute-start | bytes 3145736 | tf_op jit(solution)/shard_map/ppermute | solution.py:495
  24.5 26.6 %collective-permute-start.3 = (bf16[4096,128]{1,0:T(8,128)(2,1)}, bf16[4096,128]{1,0:T(8,128)(2,1)}, u32[]{:S(2)}, u32[]{:S(2)}) collective-permute-start(bf16[4096,128]{1,0:T(8,128)(2,1)} %pad_maximum_fusion), channel_id=1, source_target_pairs={{0,32},{4,12},{8,40},{12,20},{16,48},{20,28},{24,56},{28,4},{32,64... | collective-permute-start | bytes 3145736 | tf_op jit(solution)/shard_map/ppermute | solution.py:495
  24.5 33.8 %collective-permute-start.12 = (bf16[4096,128]{1,0:T(8,128)(2,1)}, bf16[4096,128]{1,0:T(8,128)(2,1)}, u32[]{:S(2)}, u32[]{:S(2)}) collective-permute-start(bf16[4096,128]{1,0:T(8,128)(2,1)} %pad_maximum_fusion), channel_id=1, source_target_pairs={{0,4},{4,0},{8,12},{12,8},{16,20},{20,16},{24,28},{28,24},{32,36},... | collective-permute-start | bytes 3145736 | tf_op jit(solution)/shard_map/ppermute | solution.py:490
  25.2 30.6 %collective-permute-start.6 = (bf16[384,128]{1,0:T(8,128)(2,1)S(1)}, bf16[384,128]{1,0:T(8,128)(2,1)S(1)}, u32[]{:S(2)}, u32[]{:S(2)}) collective-permute-start(bf16[384,128]{1,0:T(8,128)(2,1)S(1)} %bitcast.55), channel_id=1, source_target_pairs={{0,2},{1,3},{2,0},{3,1},{4,6},{5,7},{6,4},{7,5},{8,10},{9,11},{10,... | collective-permute-start | bytes 294920 | tf_op jit(solution)/shard_map/ppermute | solution.py:522
  29.1 28.3 %collective-permute-start.7 = (bf16[384,128]{1,0:T(8,128)(2,1)}, bf16[384,128]{1,0:T(8,128)(2,1)S(1)}, u32[]{:S(2)}, u32[]{:S(2)}) collective-permute-start(bf16[384,128]{1,0:T(8,128)(2,1)} %bitcast.14), channel_id=1, source_target_pairs={{0,1},{1,2},{2,3},{3,0},{4,5},{5,6},{6,7},{7,4},{8,9},{9,10},{10,1... | collective-permute-start | bytes 294920 | tf_op jit(solution)/shard_map/ppermute | solution.py:522
  47.1 10.5 %collective-permute-start.5 = (bf16[384,128]{1,0:T(8,128)(2,1)S(1)}, bf16[384,128]{1,0:T(8,128)(2,1)S(1)}, u32[]{:S(2)}, u32[]{:S(2)}) collective-permute-start(bf16[384,128]{1,0:T(8,128)(2,1)S(1)} %bitcast.54), channel_id=1, source_target_pairs={{0,3},{1,0},{2,1},{3,2},{4,7},{5,4},{6,5},{7,6},{8,11},{9,8},{10,9... | collective-permute-start | bytes 294920 | tf_op jit(solution)/shard_map/ppermute | solution.py:522
  52.2 9.2 %collective-permute-start.11 = (bf16[2048,128]{1,0:T(8,128)(2,1)S(1)}, bf16[2048,128]{1,0:T(8,128)(2,1)S(1)}, u32[]{:S(2)}, u32[]{:S(2)}) collective-permute-start(bf16[2048,128]{1,0:T(8,128)(2,1)S(1)} %slice.45), channel_id=1, source_target_pairs={{0,96},{4,28},{8,104},{12,4},{16,112},{20,12},{24,120},{28,20},{32... | collective-permute-start | bytes 1572872 | tf_op jit(solution)/shard_map/ppermute | solution.py:495
  55.9 21.5 %copy-start.20 = (bf16[384,128]{1,0:T(8,128)(2,1)}, bf16[384,128]{1,0:T(8,128)(2,1)S(1)}, u32[]{:S(2)}) copy-start(bf16[384,128]{1,0:T(8,128)(2,1)S(1)} %collective-permute-done.6.refs_7_) | copy-start | bytes 294916
  55.9 15.4 %collective-permute-start.9 = (bf16[16,144,128]{2,1,0:T(8,128)(2,1)S(1)}, bf16[16,144,128]{2,1,0:T(8,128)(2,1)S(1)}, u32[]{:S(2)}, u32[]{:S(2)}) collective-permute-start(bf16[16,144,128]{2,1,0:T(8,128)(2,1)S(1)} %get-tuple-element.91), channel_id=1, source_target_pairs={{0,3},{1,2},{2,1},{3,0},{4,7},{5,6},{6,5},{7,4},{8,11},{9,10},{10,... | collective-permute-start | bytes 1769480 | tf_op jit(solution)/shard_map/ppermute | solution.py:543
  57.4 20.0 %copy-start.21 = (bf16[384,128]{1,0:T(8,128)(2,1)}, bf16[384,128]{1,0:T(8,128)(2,1)S(1)}, u32[]{:S(2)}) copy-start(bf16[384,128]{1,0:T(8,128)(2,1)S(1)} %collective-permute-done.7.refs_8_) | copy-start | bytes 294916
  57.5 18.3 %collective-permute-start.13 = (bf16[4096,128]{1,0:T(8,128)(2,1)}, bf16[4096,128]{1,0:T(8,128)(2,1)}, u32[]{:S(2)}, u32[]{:S(2)}) collective-permute-start(bf16[4096,128]{1,0:T(8,128)(2,1)} %collective-permute-done.3), channel_id=1, source_target_pairs={{0,4},{4,0},{8,12},{12,8},{16,20},{20,16},{24,28},{28,24},{32,36},... | collective-permute-start | bytes 3145736 | tf_op jit(solution)/shard_map/ppermute | solution.py:490
  57.6 19.8 %copy-start.22 = (bf16[384,128]{1,0:T(8,128)(2,1)}, bf16[384,128]{1,0:T(8,128)(2,1)S(1)}, u32[]{:S(2)}) copy-start(bf16[384,128]{1,0:T(8,128)(2,1)S(1)} %collective-permute-done.5.refs_6_) | copy-start | bytes 294916
  57.6 10.5 %collective-permute-start.10 = (bf16[2048,128]{1,0:T(8,128)(2,1)S(1)}, bf16[2048,128]{1,0:T(8,128)(2,1)S(1)}, u32[]{:S(2)}, u32[]{:S(2)}) collective-permute-start(bf16[2048,128]{1,0:T(8,128)(2,1)S(1)} %slice.44), channel_id=1, source_target_pairs={{0,32},{4,12},{8,40},{12,20},{16,48},{20,28},{24,56},{28,4},{32,64... | collective-permute-start | bytes 1572872 | tf_op jit(solution)/shard_map/ppermute | solution.py:495
  58.3 17.5 %collective-permute-start.16 = (bf16[4096,128]{1,0:T(8,128)(2,1)}, bf16[4096,128]{1,0:T(8,128)(2,1)}, u32[]{:S(2)}, u32[]{:S(2)}) collective-permute-start(bf16[4096,128]{1,0:T(8,128)(2,1)} %collective-permute-done.4), channel_id=1, source_target_pairs={{0,4},{4,0},{8,12},{12,8},{16,20},{20,16},{24,28},{28,24},{32,36},... | collective-permute-start | bytes 3145736 | tf_op jit(solution)/shard_map/ppermute | solution.py:490
  61.4 14.3 %copy-start.9 = (bf16[2048,128]{1,0:T(8,128)(2,1)}, bf16[2048,128]{1,0:T(8,128)(2,1)S(1)}, u32[]{:S(2)}) copy-start(bf16[2048,128]{1,0:T(8,128)(2,1)S(1)} %collective-permute-done.11) | copy-start | bytes 1572868
  61.4 14.3 %collective-permute-start.8 = (bf16[16,144,128]{2,1,0:T(8,128)(2,1)S(1)}, bf16[16,144,128]{2,1,0:T(8,128)(2,1)}, u32[]{:S(2)}, u32[]{:S(2)}) collective-permute-start(bf16[16,144,128]{2,1,0:T(8,128)(2,1)S(1)} %get-tuple-element.92), channel_id=1, source_target_pairs={{0,1},{1,0},{2,3},{3,2},{4,5},{5,4},{6,7},{7,6},{8,9},{9,8},{10,11... | collective-permute-start | bytes 1769480 | tf_op jit(solution)/shard_map/ppermute | solution.py:542
  68.0 7.7 %copy-start.10 = (bf16[2048,128]{1,0:T(8,128)(2,1)}, bf16[2048,128]{1,0:T(8,128)(2,1)S(1)}, u32[]{:S(2)}) copy-start(bf16[2048,128]{1,0:T(8,128)(2,1)S(1)} %collective-permute-done.10) | copy-start | bytes 1572868
  68.0 7.7 %collective-permute-start.15 = (bf16[2048,128]{1,0:T(8,128)(2,1)S(1)}, bf16[2048,128]{1,0:T(8,128)(2,1)S(1)}, u32[]{:S(2)}, u32[]{:S(2)}) collective-permute-start(bf16[2048,128]{1,0:T(8,128)(2,1)S(1)} %collective-permute-done.11), channel_id=1, source_target_pairs={{0,4},{4,0},{8,12},{12,8},{16,20},{20,16},{24,28},{28,24},{32,36},... | collective-permute-start | bytes 1572872 | tf_op jit(solution)/shard_map/ppermute | solution.py:490
  71.2 4.6 %collective-permute-start.14 = (bf16[2048,128]{1,0:T(8,128)(2,1)S(1)}, bf16[2048,128]{1,0:T(8,128)(2,1)S(1)}, u32[]{:S(2)}, u32[]{:S(2)}) collective-permute-start(bf16[2048,128]{1,0:T(8,128)(2,1)S(1)} %collective-permute-done.10), channel_id=1, source_target_pairs={{0,4},{4,0},{8,12},{12,8},{16,20},{20,16},{24,28},{28,24},{32,36},... | collective-permute-start | bytes 1572872 | tf_op jit(solution)/shard_map/ppermute | solution.py:490
  90.8 17.7 %copy-start.19 = (bf16[1024,128]{1,0:T(8,128)(2,1)S(1)}, bf16[1024,128]{1,0:T(8,128)(2,1)}, u32[]{:S(2)}) copy-start(bf16[1024,128]{1,0:T(8,128)(2,1)} %param.13) | copy-start | bytes 786436
  90.8 22.7 %copy-start.5 = (bf16[1024,1024]{1,0:T(8,128)(2,1)S(1)}, bf16[1024,1024]{1,0:T(8,128)(2,1)}, u32[]{:S(2)}) copy-start(bf16[1024,1024]{1,0:T(8,128)(2,1)} %get-tuple-element.75) | copy-start | bytes 6291460
  90.8 7.8 %collective-permute-start.17 = (bf16[512,128]{1,0:T(8,128)(2,1)}, bf16[512,128]{1,0:T(8,128)(2,1)S(1)}, u32[]{:S(2)}, u32[]{:S(2)}) collective-permute-start(bf16[512,128]{1,0:T(8,128)(2,1)} %get-tuple-element.69), channel_id=1, source_target_pairs={{0,1},{1,2},{2,3},{3,0},{4,5},{5,6},{6,7},{7,4},{8,9},{9,10},{10,1... | collective-permute-start | bytes 393224 | tf_op jit(solution)/shard_map/ppermute | solution.py:522
  91.2 13.6 %collective-permute-start.19 = (bf16[512,128]{1,0:T(8,128)(2,1)}, bf16[512,128]{1,0:T(8,128)(2,1)S(1)}, u32[]{:S(2)}, u32[]{:S(2)}) collective-permute-start(bf16[512,128]{1,0:T(8,128)(2,1)} %get-tuple-element.70), channel_id=1, source_target_pairs={{0,3},{1,0},{2,1},{3,2},{4,7},{5,4},{6,5},{7,6},{8,11},{9,8},{10,9... | collective-permute-start | bytes 393224 | tf_op jit(solution)/shard_map/ppermute | solution.py:522
  94.1 10.7 %collective-permute-start.20 = (bf16[512,128]{1,0:T(8,128)(2,1)}, bf16[512,128]{1,0:T(8,128)(2,1)S(1)}, u32[]{:S(2)}, u32[]{:S(2)}) collective-permute-start(bf16[512,128]{1,0:T(8,128)(2,1)} %get-tuple-element.71), channel_id=1, source_target_pairs={{0,1},{1,2},{2,3},{3,0},{4,5},{5,6},{6,7},{7,4},{8,9},{9,10},{10,1... | collective-permute-start | bytes 393224 | tf_op jit(solution)/shard_map/ppermute | solution.py:522
  94.1 6.1 %collective-permute-start.21 = (bf16[512,128]{1,0:T(8,128)(2,1)}, bf16[512,128]{1,0:T(8,128)(2,1)S(1)}, u32[]{:S(2)}, u32[]{:S(2)}) collective-permute-start(bf16[512,128]{1,0:T(8,128)(2,1)} %get-tuple-element.73), channel_id=1, source_target_pairs={{0,3},{1,0},{2,1},{3,2},{4,7},{5,4},{6,5},{7,6},{8,11},{9,8},{10,9... | collective-permute-start | bytes 393224 | tf_op jit(solution)/shard_map/ppermute | solution.py:522
  99.6 6.2 %collective-permute-start.18 = (bf16[512,128]{1,0:T(8,128)(2,1)S(1)}, bf16[512,128]{1,0:T(8,128)(2,1)S(1)}, u32[]{:S(2)}, u32[]{:S(2)}) collective-permute-start(bf16[512,128]{1,0:T(8,128)(2,1)S(1)} %add_convert_fusion.5), channel_id=1, source_target_pairs={{0,1},{1,2},{2,3},{3,0},{4,5},{5,6},{6,7},{7,4},{8,9},{9,10},{10,1... | collective-permute-start | bytes 393224 | tf_op jit(solution)/shard_map/ppermute | solution.py:522
  101.2 6.1 %collective-permute-start.22 = (bf16[512,128]{1,0:T(8,128)(2,1)S(1)}, bf16[512,128]{1,0:T(8,128)(2,1)S(1)}, u32[]{:S(2)}, u32[]{:S(2)}) collective-permute-start(bf16[512,128]{1,0:T(8,128)(2,1)S(1)} %add_convert_fusion.4), channel_id=1, source_target_pairs={{0,3},{1,0},{2,1},{3,2},{4,7},{5,4},{6,5},{7,6},{8,11},{9,8},{10,9... | collective-permute-start | bytes 393224 | tf_op jit(solution)/shard_map/ppermute | solution.py:522
  109.4 37.3 %copy-start = (bf16[1024,128]{1,0:T(8,128)(2,1)}, bf16[1024,128]{1,0:T(8,128)(2,1)S(1)}, u32[]{:S(2)}) copy-start(bf16[1024,128]{1,0:T(8,128)(2,1)S(1)} %get-tuple-element.95.refs_4_.z0_ref) | copy-start | bytes 786436
  109.4 8.9 %collective-permute-start.25 = (bf16[1024,128]{1,0:T(8,128)(2,1)S(1)}, bf16[1024,128]{1,0:T(8,128)(2,1)S(1)}, u32[]{:S(2)}, u32[]{:S(2)}) collective-permute-start(bf16[1024,128]{1,0:T(8,128)(2,1)S(1)} %get-tuple-element.95.refs_4_.z0_ref), channel_id=1, source_target_pairs={{0,24},{4,100},{8,0},{12,108},{16,8},{20,116},{24,16},{28,124},{32... | collective-permute-start | bytes 786440 | tf_op jit(solution)/shard_map/ppermute | solution.py:495
  111.6 8.0 %collective-permute-start.24 = (bf16[1024,128]{1,0:T(8,128)(2,1)S(1)}, bf16[1024,128]{1,0:T(8,128)(2,1)S(1)}, u32[]{:S(2)}, u32[]{:S(2)}) collective-permute-start(bf16[1024,128]{1,0:T(8,128)(2,1)S(1)} %get-tuple-element.95.refs_4_.z0_ref), channel_id=1, source_target_pairs={{0,16},{4,68},{8,24},{12,76},{16,0},{20,84},{24,8},{28,92},{32,48}... | collective-permute-start | bytes 786440 | tf_op jit(solution)/shard_map/ppermute | solution.py:495
  112.9 9.3 %collective-permute-start.23 = (bf16[1024,128]{1,0:T(8,128)(2,1)S(1)}, bf16[1024,128]{1,0:T(8,128)(2,1)S(1)}, u32[]{:S(2)}, u32[]{:S(2)}) collective-permute-start(bf16[1024,128]{1,0:T(8,128)(2,1)S(1)} %get-tuple-element.95.refs_4_.z0_ref), channel_id=1, source_target_pairs={{0,8},{4,36},{8,16},{12,44},{16,24},{20,52},{24,0},{28,60},{32,40}... | collective-permute-start | bytes 786440 | tf_op jit(solution)/shard_map/ppermute | solution.py:495
  116.6 30.1 %copy-start.2 = (bf16[1024,128]{1,0:T(8,128)(2,1)S(1)}, bf16[1024,128]{1,0:T(8,128)(2,1)}, u32[]{:S(2)}) copy-start(bf16[1024,128]{1,0:T(8,128)(2,1)} %left_3_ref.1) | copy-start | bytes 786436
  116.6 30.1 %copy-start.3 = (bf16[1024,128]{1,0:T(8,128)(2,1)S(1)}, bf16[1024,128]{1,0:T(8,128)(2,1)}, u32[]{:S(2)}) copy-start(bf16[1024,128]{1,0:T(8,128)(2,1)} %get-tuple-element.88.left_1_ref) | copy-start | bytes 786436
  116.6 30.1 %copy-start.4 = (bf16[1024,128]{1,0:T(8,128)(2,1)S(1)}, bf16[1024,128]{1,0:T(8,128)(2,1)}, u32[]{:S(2)}) copy-start(bf16[1024,128]{1,0:T(8,128)(2,1)} %get-tuple-element.89.left_2_ref) | copy-start | bytes 786436
  122.3 26.1 %copy-start.6 = (bf16[4096,128]{1,0:T(8,128)(2,1)}, bf16[4096,128]{1,0:T(8,128)(2,1)S(1)}, u32[]{:S(2)}) copy-start(bf16[4096,128]{1,0:T(8,128)(2,1)S(1)} %pad_maximum_fusion.1) | copy-start | bytes 3145732
  122.4 15.4 %collective-permute-start.27 = (bf16[4096,128]{1,0:T(8,128)(2,1)S(1)}, bf16[4096,128]{1,0:T(8,128)(2,1)S(1)}, u32[]{:S(2)}, u32[]{:S(2)}) collective-permute-start(bf16[4096,128]{1,0:T(8,128)(2,1)S(1)} %pad_maximum_fusion.1), channel_id=1, source_target_pairs={{0,96},{4,28},{8,104},{12,4},{16,112},{20,12},{24,120},{28,20},{32... | collective-permute-start | bytes 3145736 | tf_op jit(solution)/shard_map/ppermute | solution.py:495
  125.3 16.1 %collective-permute-start.26 = (bf16[4096,128]{1,0:T(8,128)(2,1)S(1)}, bf16[4096,128]{1,0:T(8,128)(2,1)}, u32[]{:S(2)}, u32[]{:S(2)}) collective-permute-start(bf16[4096,128]{1,0:T(8,128)(2,1)S(1)} %pad_maximum_fusion.1), channel_id=1, source_target_pairs={{0,32},{4,12},{8,40},{12,20},{16,48},{20,28},{24,56},{28,4},{32,64... | collective-permute-start | bytes 3145736 | tf_op jit(solution)/shard_map/ppermute | solution.py:495
  125.3 19.5 %collective-permute-start.43 = (bf16[1024,128]{1,0:T(8,128)(2,1)S(1)}, bf16[1024,128]{1,0:T(8,128)(2,1)S(1)}, u32[]{:S(2)}, u32[]{:S(2)}) collective-permute-start(bf16[1024,128]{1,0:T(8,128)(2,1)S(1)} %get-tuple-element.95.refs_4_.z0_ref), channel_id=1, source_target_pairs={{0,3},{1,0},{2,1},{3,2},{4,7},{5,4},{6,5},{7,6},{8,11},{9,8},{10,9... | collective-permute-start | bytes 786440 | tf_op jit(solution)/shard_map/ppermute | solution.py:522
  129.2 16.9 %collective-permute-start.42 = (bf16[1024,128]{1,0:T(8,128)(2,1)S(1)}, bf16[1024,128]{1,0:T(8,128)(2,1)S(1)}, u32[]{:S(2)}, u32[]{:S(2)}) collective-permute-start(bf16[1024,128]{1,0:T(8,128)(2,1)S(1)} %get-tuple-element.95.refs_4_.z0_ref), channel_id=1, source_target_pairs={{0,2},{1,3},{2,0},{3,1},{4,6},{5,7},{6,4},{7,5},{8,10},{9,11},{10,... | collective-permute-start | bytes 786440 | tf_op jit(solution)/shard_map/ppermute | solution.py:522
  129.2 16.9 %collective-permute-start.41 = (bf16[1024,128]{1,0:T(8,128)(2,1)S(1)}, bf16[1024,128]{1,0:T(8,128)(2,1)S(1)}, u32[]{:S(2)}, u32[]{:S(2)}) collective-permute-start(bf16[1024,128]{1,0:T(8,128)(2,1)S(1)} %get-tuple-element.95.refs_4_.z0_ref), channel_id=1, source_target_pairs={{0,1},{1,2},{2,3},{3,0},{4,5},{5,6},{6,7},{7,4},{8,9},{9,10},{10,1... | collective-permute-start | bytes 786440 | tf_op jit(solution)/shard_map/ppermute | solution.py:522
  137.8 10.6 %copy-start.8 = (bf16[4096,128]{1,0:T(8,128)(2,1)}, bf16[4096,128]{1,0:T(8,128)(2,1)S(1)}, u32[]{:S(2)}) copy-start(bf16[4096,128]{1,0:T(8,128)(2,1)S(1)} %collective-permute-done.27) | copy-start | bytes 3145732
  137.8 18.0 %collective-permute-start.30 = (bf16[4096,128]{1,0:T(8,128)(2,1)S(1)}, bf16[4096,128]{1,0:T(8,128)(2,1)}, u32[]{:S(2)}, u32[]{:S(2)}) collective-permute-start(bf16[4096,128]{1,0:T(8,128)(2,1)S(1)} %pad_maximum_fusion.1), channel_id=1, source_target_pairs={{0,4},{4,0},{8,12},{12,8},{16,20},{20,16},{24,28},{28,24},{32,36},... | collective-permute-start | bytes 3145736 | tf_op jit(solution)/shard_map/ppermute | solution.py:490
  144.1 11.1 %collective-permute-start.29 = (bf16[2048,128]{1,0:T(8,128)(2,1)}, bf16[2048,128]{1,0:T(8,128)(2,1)}, u32[]{:S(2)}, u32[]{:S(2)}) collective-permute-start(bf16[2048,128]{1,0:T(8,128)(2,1)} %slice.49), channel_id=1, source_target_pairs={{0,96},{4,28},{8,104},{12,4},{16,112},{20,12},{24,120},{28,20},{32... | collective-permute-start | bytes 1572872 | tf_op jit(solution)/shard_map/ppermute | solution.py:495
  144.8 10.8 %collective-permute-start.28 = (bf16[2048,128]{1,0:T(8,128)(2,1)}, bf16[2048,128]{1,0:T(8,128)(2,1)}, u32[]{:S(2)}, u32[]{:S(2)}) collective-permute-start(bf16[2048,128]{1,0:T(8,128)(2,1)} %slice.48), channel_id=1, source_target_pairs={{0,32},{4,12},{8,40},{12,20},{16,48},{20,28},{24,56},{28,4},{32,64... | collective-permute-start | bytes 1572872 | tf_op jit(solution)/shard_map/ppermute | solution.py:495
  146.2 12.0 %collective-permute-start.31 = (bf16[4096,128]{1,0:T(8,128)(2,1)}, bf16[4096,128]{1,0:T(8,128)(2,1)}, u32[]{:S(2)}, u32[]{:S(2)}) collective-permute-start(bf16[4096,128]{1,0:T(8,128)(2,1)} %collective-permute-done.26), channel_id=1, source_target_pairs={{0,4},{4,0},{8,12},{12,8},{16,20},{20,16},{24,28},{28,24},{32,36},... | collective-permute-start | bytes 3145736 | tf_op jit(solution)/shard_map/ppermute | solution.py:490
  146.2 12.0 %collective-permute-start.34 = (bf16[4096,128]{1,0:T(8,128)(2,1)S(1)}, bf16[4096,128]{1,0:T(8,128)(2,1)}, u32[]{:S(2)}, u32[]{:S(2)}) collective-permute-start(bf16[4096,128]{1,0:T(8,128)(2,1)S(1)} %collective-permute-done.27), channel_id=1, source_target_pairs={{0,4},{4,0},{8,12},{12,8},{16,20},{20,16},{24,28},{28,24},{32,36},... | collective-permute-start | bytes 3145736 | tf_op jit(solution)/shard_map/ppermute | solution.py:490
  148.4 23.1 %all-to-all-start.1 = ((f32[32,48,128]{2,1,0:T(8,128)}), f32[32,48,128]{2,1,0:T(8,128)S(1)}, u32[]{:S(2)}, u32[]{:S(2)}) async-start(f32[32,48,128]{2,1,0:T(8,128)} %slopes.1), calls=%async_computation.1 | async-start | bytes 1572864 | tf_op jit(solution)/shard_map/all_to_all | solution.py:570
  155.2 2.2 %collective-permute-start.33 = (bf16[2048,128]{1,0:T(8,128)(2,1)}, bf16[2048,128]{1,0:T(8,128)(2,1)S(1)}, u32[]{:S(2)}, u32[]{:S(2)}) collective-permute-start(bf16[2048,128]{1,0:T(8,128)(2,1)} %collective-permute-done.29), channel_id=1, source_target_pairs={{0,4},{4,0},{8,12},{12,8},{16,20},{20,16},{24,28},{28,24},{32,36},... | collective-permute-start | bytes 1572872 | tf_op jit(solution)/shard_map/ppermute | solution.py:490
  155.5 2.6 %collective-permute-start.32 = (bf16[2048,128]{1,0:T(8,128)(2,1)}, bf16[2048,128]{1,0:T(8,128)(2,1)S(1)}, u32[]{:S(2)}, u32[]{:S(2)}) collective-permute-start(bf16[2048,128]{1,0:T(8,128)(2,1)} %collective-permute-done.28), channel_id=1, source_target_pairs={{0,4},{4,0},{8,12},{12,8},{16,20},{20,16},{24,28},{28,24},{32,36},... | collective-permute-start | bytes 1572872 | tf_op jit(solution)/shard_map/ppermute | solution.py:490
  171.4 20.9 %copy-start.18 = (f32[1024,128]{1,0:T(8,128)S(1)}, f32[1024,128]{1,0:T(8,128)}, u32[]{:S(2)}) copy-start(f32[1024,128]{1,0:T(8,128)} %get-tuple-element.81) | copy-start | bytes 1572868
  171.4 8.2 %collective-permute-start.35 = (bf16[512,128]{1,0:T(8,128)(2,1)}, bf16[512,128]{1,0:T(8,128)(2,1)S(1)}, u32[]{:S(2)}, u32[]{:S(2)}) collective-permute-start(bf16[512,128]{1,0:T(8,128)(2,1)} %get-tuple-element.83), channel_id=1, source_target_pairs={{0,1},{1,2},{2,3},{3,0},{4,5},{5,6},{6,7},{7,4},{8,9},{9,10},{10,1... | collective-permute-start | bytes 393224 | tf_op jit(solution)/shard_map/ppermute | solution.py:522
  171.6 9.1 %collective-permute-start.37 = (bf16[512,128]{1,0:T(8,128)(2,1)}, bf16[512,128]{1,0:T(8,128)(2,1)S(1)}, u32[]{:S(2)}, u32[]{:S(2)}) collective-permute-start(bf16[512,128]{1,0:T(8,128)(2,1)} %get-tuple-element.84), channel_id=1, source_target_pairs={{0,3},{1,0},{2,1},{3,2},{4,7},{5,4},{6,5},{7,6},{8,11},{9,8},{10,9... | collective-permute-start | bytes 393224 | tf_op jit(solution)/shard_map/ppermute | solution.py:522
  175.3 7.1 %collective-permute-start.38 = (bf16[512,128]{1,0:T(8,128)(2,1)}, bf16[512,128]{1,0:T(8,128)(2,1)S(1)}, u32[]{:S(2)}, u32[]{:S(2)}) collective-permute-start(bf16[512,128]{1,0:T(8,128)(2,1)} %get-tuple-element.85), channel_id=1, source_target_pairs={{0,1},{1,2},{2,3},{3,0},{4,5},{5,6},{6,7},{7,4},{8,9},{9,10},{10,1... | collective-permute-start | bytes 393224 | tf_op jit(solution)/shard_map/ppermute | solution.py:522
  175.3 7.8 %collective-permute-start.39 = (bf16[512,128]{1,0:T(8,128)(2,1)}, bf16[512,128]{1,0:T(8,128)(2,1)S(1)}, u32[]{:S(2)}, u32[]{:S(2)}) collective-permute-start(bf16[512,128]{1,0:T(8,128)(2,1)} %get-tuple-element.87), channel_id=1, source_target_pairs={{0,3},{1,0},{2,1},{3,2},{4,7},{5,4},{6,5},{7,6},{8,11},{9,8},{10,9... | collective-permute-start | bytes 393224 | tf_op jit(solution)/shard_map/ppermute | solution.py:522
  180.6 9.7 %collective-permute-start.36 = (bf16[512,128]{1,0:T(8,128)(2,1)S(1)}, bf16[512,128]{1,0:T(8,128)(2,1)S(1)}, u32[]{:S(2)}, u32[]{:S(2)}) collective-permute-start(bf16[512,128]{1,0:T(8,128)(2,1)S(1)} %add_convert_fusion.3), channel_id=1, source_target_pairs={{0,1},{1,2},{2,3},{3,0},{4,5},{5,6},{6,7},{7,4},{8,9},{9,10},{10,1... | collective-permute-start | bytes 393224 | tf_op jit(solution)/shard_map/ppermute | solution.py:522
  182.5 7.3 %collective-permute-start.44 = (f32[48,128]{1,0:T(8,128)S(1)}, f32[48,128]{1,0:T(8,128)S(1)}, u32[]{:S(2)}, u32[]{:S(2)}) collective-permute-start(f32[48,128]{1,0:T(8,128)S(1)} %reduce_sum.9), channel_id=1, source_target_pairs={{0,0},{1,33},{2,66},{3,99},{4,4},{5,37},{6,70},{7,103},{8,8},{9,41... | collective-permute-start | bytes 73736 | tf_op jit(solution)/shard_map/ppermute | solution.py:583
  184.1 8.1 %collective-permute-start.40 = (bf16[512,128]{1,0:T(8,128)(2,1)S(1)}, bf16[512,128]{1,0:T(8,128)(2,1)S(1)}, u32[]{:S(2)}, u32[]{:S(2)}) collective-permute-start(bf16[512,128]{1,0:T(8,128)(2,1)S(1)} %add_convert_fusion.1), channel_id=1, source_target_pairs={{0,3},{1,0},{2,1},{3,2},{4,7},{5,4},{6,5},{7,6},{8,11},{9,8},{10,9... | collective-permute-start | bytes 393224 | tf_op jit(solution)/shard_map/ppermute | solution.py:522
  (6 other events, 16.4 us)

commit v4 on v3

--- a/solution.py
+++ b/solution.py
@@ -9,7 +9,7 @@
 GROUP = 16
 BATCH = 8
 CODES = 16
-PICKS = 4
+PICKS = 8
 MIB = 1024 * 1024
 ROOM = 63 * MIB
 LESS = 16 * MIB
@@ -44,7 +44,7 @@
         listed[found] = slot
         return found + ((owner != myself) & (slot < total)).astype(jnp.int32)
 
-    found = lax.fori_loop(0, dst_ref.shape[0], scan, 0, unroll=8)
+    found = lax.fori_loop(0, dst_ref.shape[0], scan, 0, unroll=32)
     found = jnp.minimum(found, devices * CAP)
 
     def keep(entry, carry):

time: 194 us -> 194 us (level)
    ppermute x14, starting transfers between devices: 19.7 us -> 22.1 us  [move(): return lax.ppermute(part, 'nodes', around(devices, stage, step))]
  transfers between devices with their start and end apart: 47 -> 47, of which waited for: 19 -> 20; matrix products, arithmetic and copies ran while one was open for 8% -> 8% of each run, Pallas kernels for 15% -> 15%
where the time goes in v4:
time: 194 us
  starting transfers between devices  73.4 us (38%)
  waiting for transfers between devices  55.4 us (29%)
  Pallas kernels  41.2 us (21%)
  local copies, waits for them, and re-layouts  10 us (5%)
  other arithmetic  8.75 us (5%)
  matrix products  3.05 us (2%)
    ppermute x18, starting transfers between devices, shift(): lax.ppermute(values, 'hid', [(here, (here + step) % planes) for here in r...  36.5 us
    ppermute x14, waiting for transfers between devices, move(): return lax.ppermute(part, 'nodes', around(devices, stage, step))  36.3 us
    pallas_call x2, Pallas kernels, spread(): pl.pallas_call(lambda *refs: spread_kernel(turned, len(pieces), *refs), i...  25.2 us
    ppermute x14, starting transfers between devices, move(): return lax.ppermute(part, 'nodes', around(devices, stage, step))  22.1 us
    ppermute x18, waiting for transfers between devices, shift(): lax.ppermute(values, 'hid', [(here, (here + step) % planes) for here in r...  9.25 us
    pallas_call x1, Pallas kernels, pile(): pl.pallas_call(pile_kernel, in_specs=[smem, smem, smem, pl.BlockSpec(memo...  7.83 us
    all_to_all x1, starting transfers between devices, shards(): arrived = lax.all_to_all(send, 'nodes', 0, 0, tiled=True)  6.73 us
    pallas_call x1, Pallas kernels, pick(): pl.pallas_call(lambda *refs: pick_kernel(blocks, *refs), in_specs=[smem,...  6.45 us
  transfers between devices with their start and end apart: 47, of which 20 were waited for; matrix products, arithmetic and copies ran while one was open for 8% of the time, Pallas kernels for 15%

profile of v4, /device:TPU:0, one launch (start us, length us, event | category | flops | bytes accessed | tf_op | source)
XLA Modules:
  0.0 193.5 jit_solution(7284545947729457148)
XLA Ops:
  0.6 2.9 %collective-permute-start.2 = (bf16[1024,128]{1,0:T(8,128)(2,1)}, bf16[1024,128]{1,0:T(8,128)(2,1)S(1)}, u32[]{:S(2)}, u32[]{:S(2)}) collective-permute-start(bf16[1024,128]{1,0:T(8,128)(2,1)} %left_3_ref.1), channel_id=1, source_target_pairs={{0,24},{4,100},{8,0},{12,108},{16,8},{20,116},{24,16},{28,124},{32... | collective-permute-start | bytes 786440 | tf_op jit(solution)/shard_map/ppermute | solution.py:495
  3.5 0.8 collective-permute-start.1
  4.3 0.9 collective-permute-start
  6.6 6.4 %pick.1 = (bf16[64,128,128]{2,1,0:T(8,128)(2,1)}, bf16[32,144,128]{2,1,0:T(8,128)(2,1)}, s32[64]{0:T(128)}) custom-call(s32[256]{0:T(256)} %src_ref.1, s32[256]{0:T(256)} %dst_ref.1, s32[6]{0:T(128)} %stack.35.refs_2_.info_ref.refs_0_, s32[256,128,128]{2,1,0:T(8,128)} %pattern_ref.1), custom_call_target="tpu_custom_call" | custom-call | flops 1048576 | bytes 8388608 | tf_op jit(solution)/shard_map/pick/pallas_call | solution.py:105
  13.1 6.7 %all-to-all-start = ((bf16[32,144,128]{2,1,0:T(8,128)(2,1)}), bf16[32,144,128]{2,1,0:T(8,128)(2,1)}, u32[]{:S(2)}, u32[]{:S(2)}) async-start(bf16[32,144,128]{2,1,0:T(8,128)(2,1)} %get-tuple-element.49), calls=%async_computation | async-start | bytes 2359296 | tf_op jit(solution)/shard_map/all_to_all | solution.py:538
  19.8 1.1 pad_maximum_fusion
  21.0 3.0 %collective-permute-start.4 = (bf16[4096,128]{1,0:T(8,128)(2,1)}, bf16[4096,128]{1,0:T(8,128)(2,1)}, u32[]{:S(2)}, u32[]{:S(2)}) collective-permute-start(bf16[4096,128]{1,0:T(8,128)(2,1)} %pad_maximum_fusion), channel_id=1, source_target_pairs={{0,96},{4,28},{8,104},{12,4},{16,112},{20,12},{24,120},{28,20},{32... | collective-permute-start | bytes 3145736 | tf_op jit(solution)/shard_map/ppermute | solution.py:495
  24.7 3.9 %collective-permute-start.6 = (bf16[384,128]{1,0:T(8,128)(2,1)S(1)}, bf16[384,128]{1,0:T(8,128)(2,1)S(1)}, u32[]{:S(2)}, u32[]{:S(2)}) collective-permute-start(bf16[384,128]{1,0:T(8,128)(2,1)S(1)} %bitcast.55), channel_id=1, source_target_pairs={{0,2},{1,3},{2,0},{3,1},{4,6},{5,7},{6,4},{7,5},{8,10},{9,11},{10,... | collective-permute-start | bytes 294920 | tf_op jit(solution)/shard_map/ppermute | solution.py:522
  28.6 1.0 collective-permute-start.7
  29.6 7.8 %pile.1 = (bf16[1024,1024]{1,0:T(8,128)(2,1)}, f32[1024,128]{1,0:T(8,128)}, f32[1024,128]{1,0:T(8,128)}) custom-call(s32[256]{0:T(256)} %src_ref.1, s32[256]{0:T(256)} %dst_ref.1, s32[6]{0:T(128)} %stack.35.refs_2_.info_ref.refs_0_, s32[256,128,128]{2,1,0:T(8,128)} %pattern_ref.1, bf16[1024,128]{1,0:T(8,128)(2,1)} %left_3_ref.1), custom_call_target="tpu_custom_call" | custom-call | flops 4194304 | bytes 16777216 | tf_op jit(solution)/shard_map/pile/pallas_call | solution.py:192
  37.5 9.1 %collective-permute-done.4 = bf16[4096,128]{1,0:T(8,128)(2,1)} collective-permute-done((bf16[4096,128]{1,0:T(8,128)(2,1)}, bf16[4096,128]{1,0:T(8,128)(2,1)}, u32[]{:S(2)}, u32[]{:S(2)}) %collective-permute-start.4) | collective-permute-done | bytes 1048608 | tf_op jit(solution)/shard_map/ppermute | solution.py:495
  46.6 4.0 %collective-permute-start.5 = (bf16[384,128]{1,0:T(8,128)(2,1)S(1)}, bf16[384,128]{1,0:T(8,128)(2,1)S(1)}, u32[]{:S(2)}, u32[]{:S(2)}) collective-permute-start(bf16[384,128]{1,0:T(8,128)(2,1)S(1)} %bitcast.54), channel_id=1, source_target_pairs={{0,3},{1,0},{2,1},{3,2},{4,7},{5,4},{6,5},{7,6},{8,11},{9,8},{10,9... | collective-permute-start | bytes 294920 | tf_op jit(solution)/shard_map/ppermute | solution.py:522
  50.6 1.1 slice.45
  51.7 2.3 %collective-permute-start.11 = (bf16[2048,128]{1,0:T(8,128)(2,1)S(1)}, bf16[2048,128]{1,0:T(8,128)(2,1)S(1)}, u32[]{:S(2)}, u32[]{:S(2)}) collective-permute-start(bf16[2048,128]{1,0:T(8,128)(2,1)S(1)} %slice.45), channel_id=1, source_target_pairs={{0,96},{4,28},{8,104},{12,4},{16,112},{20,12},{24,120},{28,20},{32... | collective-permute-start | bytes 1572872 | tf_op jit(solution)/shard_map/ppermute | solution.py:495
  54.0 1.3 fusion
  55.9 1.1 slice.44
  57.8 0.8 collective-permute-start.16
  58.6 2.4 %collective-permute-done.11 = bf16[2048,128]{1,0:T(8,128)(2,1)S(1)} collective-permute-done((bf16[2048,128]{1,0:T(8,128)(2,1)S(1)}, bf16[2048,128]{1,0:T(8,128)(2,1)S(1)}, u32[]{:S(2)}, u32[]{:S(2)}) %collective-permute-start.11) | collective-permute-done | bytes 524320 | tf_op jit(solution)/shard_map/ppermute | solution.py:495
  60.9 6.6 %collective-permute-done.10 = bf16[2048,128]{1,0:T(8,128)(2,1)S(1)} collective-permute-done((bf16[2048,128]{1,0:T(8,128)(2,1)S(1)}, bf16[2048,128]{1,0:T(8,128)(2,1)S(1)}, u32[]{:S(2)}, u32[]{:S(2)}) %collective-permute-start.10) | collective-permute-done | bytes 524320 | tf_op jit(solution)/shard_map/ppermute | solution.py:495
  67.5 3.2 %collective-permute-done.9.refs_11_.refs_10_ = bf16[16,144,128]{2,1,0:T(8,128)(2,1)S(1)} collective-permute-done((bf16[16,144,128]{2,1,0:T(8,128)(2,1)S(1)}, bf16[16,144,128]{2,1,0:T(8,128)(2,1)S(1)}, u32[]{:S(2)}, u32[]{:S(2)}) %collective-permute-start.9) | collective-permute-done | bytes 589856 | tf_op jit(solution)/shard_map/ppermute | solution.py:543
  70.7 4.5 %collective-permute-done.8.refs_10_.refs_9_ = bf16[16,144,128]{2,1,0:T(8,128)(2,1)} collective-permute-done((bf16[16,144,128]{2,1,0:T(8,128)(2,1)S(1)}, bf16[16,144,128]{2,1,0:T(8,128)(2,1)}, u32[]{:S(2)}, u32[]{:S(2)}) %collective-permute-start.8) | collective-permute-done | bytes 589856 | tf_op jit(solution)/shard_map/ppermute | solution.py:542
  75.3 0.8 copy-done.11
  76.1 0.8 copy-done.12
  76.9 13.0 %spread.2 = (f32[1024,128]{1,0:T(8,128)}, f32[512,128]{1,0:T(8,128)}, bf16[512,128]{1,0:T(8,128)(2,1)}, bf16[512,128]{1,0:T(8,128)(2,1)}, bf16[512,128]{1,0:T(8,...) custom-call(s32[6]{0:T(128)} %stack.35.refs_2_.info_ref.refs_0_, ...), custom_call_target="tpu_custom_call" | custom-call | flops 671088640 | bytes 16777216 | tf_op jit(solution)/shard_map/spread/pallas_call | solution.py:433
  90.3 2.9 %collective-permute-start.19 = (bf16[512,128]{1,0:T(8,128)(2,1)}, bf16[512,128]{1,0:T(8,128)(2,1)S(1)}, u32[]{:S(2)}, u32[]{:S(2)}) collective-permute-start(bf16[512,128]{1,0:T(8,128)(2,1)} %get-tuple-element.70), channel_id=1, source_target_pairs={{0,3},{1,0},{2,1},{3,2},{4,7},{5,4},{6,5},{7,6},{8,11},{9,8},{10,9... | collective-permute-start | bytes 393224 | tf_op jit(solution)/shard_map/ppermute | solution.py:522
  93.2 3.2 %collective-permute-start.21 = (bf16[512,128]{1,0:T(8,128)(2,1)}, bf16[512,128]{1,0:T(8,128)(2,1)S(1)}, u32[]{:S(2)}, u32[]{:S(2)}) collective-permute-start(bf16[512,128]{1,0:T(8,128)(2,1)} %get-tuple-element.73), channel_id=1, source_target_pairs={{0,3},{1,0},{2,1},{3,2},{4,7},{5,4},{6,5},{7,6},{8,11},{9,8},{10,9... | collective-permute-start | bytes 393224 | tf_op jit(solution)/shard_map/ppermute | solution.py:522
  96.5 0.9 collective-permute-done.17
  97.4 1.0 add_convert_fusion.5
  98.4 0.9 collective-permute-done.21
  99.3 1.0 add_convert_fusion.4
  100.3 3.8 %collective-permute-start.22 = (bf16[512,128]{1,0:T(8,128)(2,1)S(1)}, bf16[512,128]{1,0:T(8,128)(2,1)S(1)}, u32[]{:S(2)}, u32[]{:S(2)}) collective-permute-start(bf16[512,128]{1,0:T(8,128)(2,1)S(1)} %add_convert_fusion.4), channel_id=1, source_target_pairs={{0,3},{1,0},{2,1},{3,2},{4,7},{5,4},{6,5},{7,6},{8,11},{9,8},{10,9... | collective-permute-start | bytes 393224 | tf_op jit(solution)/shard_map/ppermute | solution.py:522
  104.6 2.0 %collective-permute-done.22 = bf16[512,128]{1,0:T(8,128)(2,1)S(1)} collective-permute-done((bf16[512,128]{1,0:T(8,128)(2,1)S(1)}, bf16[512,128]{1,0:T(8,128)(2,1)S(1)}, u32[]{:S(2)}, u32[]{:S(2)}) %collective-permute-start.22) | collective-permute-done | bytes 131104 | tf_op jit(solution)/shard_map/ppermute | solution.py:522
  106.6 1.1 convert_add_fusion.1
  107.8 1.0 multiply_convert_fusion
  108.7 2.6 %collective-permute-start.25 = (bf16[1024,128]{1,0:T(8,128)(2,1)S(1)}, bf16[1024,128]{1,0:T(8,128)(2,1)S(1)}, u32[]{:S(2)}, u32[]{:S(2)}) collective-permute-start(bf16[1024,128]{1,0:T(8,128)(2,1)S(1)} %get-tuple-element.95.refs_4_.z0_ref), channel_id=1, source_target_pairs={{0,24},{4,100},{8,0},{12,108},{16,8},{20,116},{24,16},{28,124},{32... | collective-permute-start | bytes 786440 | tf_op jit(solution)/shard_map/ppermute | solution.py:495
  111.3 1.0 collective-permute-start.24
  112.2 1.0 collective-permute-start.23
  113.2 1.6 fusion.3.refs_3_
  114.8 1.5 fusion.2.refs_2_
  116.3 1.7 collective-permute-done.25
  118.0 1.2 collective-permute-done.24
  119.2 2.7 %collective-permute-done.23 = bf16[1024,128]{1,0:T(8,128)(2,1)S(1)} collective-permute-done((bf16[1024,128]{1,0:T(8,128)(2,1)S(1)}, bf16[1024,128]{1,0:T(8,128)(2,1)S(1)}, u32[]{:S(2)}, u32[]{:S(2)}) %collective-permute-start.23) | collective-permute-done | bytes 262176 | tf_op jit(solution)/shard_map/ppermute | solution.py:495
  122.0 4.9 %collective-permute-start.27 = (bf16[4096,128]{1,0:T(8,128)(2,1)S(1)}, bf16[4096,128]{1,0:T(8,128)(2,1)S(1)}, u32[]{:S(2)}, u32[]{:S(2)}) collective-permute-start(bf16[4096,128]{1,0:T(8,128)(2,1)S(1)} %pad_maximum_fusion.1), channel_id=1, source_target_pairs={{0,96},{4,28},{8,104},{12,4},{16,112},{20,12},{24,120},{28,20},{32... | collective-permute-start | bytes 3145736 | tf_op jit(solution)/shard_map/ppermute | solution.py:495
  127.0 3.8 %collective-permute-start.43 = (bf16[1024,128]{1,0:T(8,128)(2,1)S(1)}, bf16[1024,128]{1,0:T(8,128)(2,1)S(1)}, u32[]{:S(2)}, u32[]{:S(2)}) collective-permute-start(bf16[1024,128]{1,0:T(8,128)(2,1)S(1)} %get-tuple-element.95.refs_4_.z0_ref), channel_id=1, source_target_pairs={{0,3},{1,0},{2,1},{3,2},{4,7},{5,4},{6,5},{7,6},{8,11},{9,8},{10,9... | collective-permute-start | bytes 786440 | tf_op jit(solution)/shard_map/ppermute | solution.py:522
  130.7 0.9 collective-permute-start.41
  131.6 7.7 %collective-permute-done.27 = bf16[4096,128]{1,0:T(8,128)(2,1)S(1)} collective-permute-done((bf16[4096,128]{1,0:T(8,128)(2,1)S(1)}, bf16[4096,128]{1,0:T(8,128)(2,1)S(1)}, u32[]{:S(2)}, u32[]{:S(2)}) %collective-permute-start.27) | collective-permute-done | bytes 1048608 | tf_op jit(solution)/shard_map/ppermute | solution.py:495
  139.3 3.8 %collective-permute-done.26 = bf16[4096,128]{1,0:T(8,128)(2,1)} collective-permute-done((bf16[4096,128]{1,0:T(8,128)(2,1)S(1)}, bf16[4096,128]{1,0:T(8,128)(2,1)}, u32[]{:S(2)}, u32[]{:S(2)}) %collective-permute-start.26) | collective-permute-done | bytes 1048608 | tf_op jit(solution)/shard_map/ppermute | solution.py:495
  143.1 1.9 slice.48
  145.0 0.8 slice.49
  146.1 1.7 collective-permute-start.28
  148.4 1.7 slopes.1
  150.1 5.2 %all-to-all-start.1 = ((f32[32,48,128]{2,1,0:T(8,128)}), f32[32,48,128]{2,1,0:T(8,128)S(1)}, u32[]{:S(2)}, u32[]{:S(2)}) async-start(f32[32,48,128]{2,1,0:T(8,128)} %slopes.1), calls=%async_computation.1 | async-start | bytes 1572864 | tf_op jit(solution)/shard_map/all_to_all | solution.py:570
  155.7 1.1 collective-permute-done.28
  157.6 1.4 collective-permute-done.32
  158.9 0.8 copy-done.17
  159.7 12.1 %spread.3 = (f32[1024,128]{1,0:T(8,128)}, f32[512,128]{1,0:T(8,128)}, bf16[512,128]{1,0:T(8,128)(2,1)}, bf16[512,128]{1,0:T(8,128)(2,1)}, bf16[512,128]{1,0:T(8,...) custom-call(s32[6]{0:T(128)} %stack.35.refs_2_.info_ref.refs_0_, s32[146]{0:T(256)} %get-tuple-element.74.refs_1_, ...), custom_call_target="tpu_custom_call" | custom-call | flops 671088640 | bytes 16777216 | tf_op jit(solution)/shard_map/spread/pallas_call | solution.py:433
  172.0 3.8 %collective-permute-start.37 = (bf16[512,128]{1,0:T(8,128)(2,1)}, bf16[512,128]{1,0:T(8,128)(2,1)S(1)}, u32[]{:S(2)}, u32[]{:S(2)}) collective-permute-start(bf16[512,128]{1,0:T(8,128)(2,1)} %get-tuple-element.84), channel_id=1, source_target_pairs={{0,3},{1,0},{2,1},{3,2},{4,7},{5,4},{6,5},{7,6},{8,11},{9,8},{10,9... | collective-permute-start | bytes 393224 | tf_op jit(solution)/shard_map/ppermute | solution.py:522
  175.9 3.2 %collective-permute-start.39 = (bf16[512,128]{1,0:T(8,128)(2,1)}, bf16[512,128]{1,0:T(8,128)(2,1)S(1)}, u32[]{:S(2)}, u32[]{:S(2)}) collective-permute-start(bf16[512,128]{1,0:T(8,128)(2,1)} %get-tuple-element.87), channel_id=1, source_target_pairs={{0,3},{1,0},{2,1},{3,2},{4,7},{5,4},{6,5},{7,6},{8,11},{9,8},{10,9... | collective-permute-start | bytes 393224 | tf_op jit(solution)/shard_map/ppermute | solution.py:522
  179.1 1.1 collective-permute-done.35
  180.1 1.0 add_convert_fusion.3
  181.2 2.0 %collective-permute-done.38 = bf16[512,128]{1,0:T(8,128)(2,1)S(1)} collective-permute-done((bf16[512,128]{1,0:T(8,128)(2,1)}, bf16[512,128]{1,0:T(8,128)(2,1)S(1)}, u32[]{:S(2)}, u32[]{:S(2)}) %collective-permute-start.38) | collective-permute-done | bytes 131104 | tf_op jit(solution)/shard_map/ppermute | solution.py:522
  183.9 1.0 add_convert_fusion.1
  184.9 5.3 %collective-permute-start.40 = (bf16[512,128]{1,0:T(8,128)(2,1)S(1)}, bf16[512,128]{1,0:T(8,128)(2,1)S(1)}, u32[]{:S(2)}, u32[]{:S(2)}) collective-permute-start(bf16[512,128]{1,0:T(8,128)(2,1)S(1)} %add_convert_fusion.1), channel_id=1, source_target_pairs={{0,3},{1,0},{2,1},{3,2},{4,7},{5,4},{6,5},{7,6},{8,11},{9,8},{10,9... | collective-permute-start | bytes 393224 | tf_op jit(solution)/shard_map/ppermute | solution.py:522
  190.8 1.9 collective-permute-done.40
  (103 shorter events, 8.1 us)
Async XLA Ops:
  0.6 19.2 %collective-permute-start.2 = (bf16[1024,128]{1,0:T(8,128)(2,1)}, bf16[1024,128]{1,0:T(8,128)(2,1)S(1)}, u32[]{:S(2)}, u32[]{:S(2)}) collective-permute-start(bf16[1024,128]{1,0:T(8,128)(2,1)} %left_3_ref.1), channel_id=1, source_target_pairs={{0,24},{4,100},{8,0},{12,108},{16,8},{20,116},{24,16},{28,124},{32... | collective-permute-start | bytes 786440 | tf_op jit(solution)/shard_map/ppermute | solution.py:495
  3.5 16.3 %collective-permute-start.1 = (bf16[1024,128]{1,0:T(8,128)(2,1)}, bf16[1024,128]{1,0:T(8,128)(2,1)S(1)}, u32[]{:S(2)}, u32[]{:S(2)}) collective-permute-start(bf16[1024,128]{1,0:T(8,128)(2,1)} %left_3_ref.1), channel_id=1, source_target_pairs={{0,16},{4,68},{8,24},{12,76},{16,0},{20,84},{24,8},{28,92},{32,48}... | collective-permute-start | bytes 786440 | tf_op jit(solution)/shard_map/ppermute | solution.py:495
  4.3 15.5 %collective-permute-start = (bf16[1024,128]{1,0:T(8,128)(2,1)}, bf16[1024,128]{1,0:T(8,128)(2,1)S(1)}, u32[]{:S(2)}, u32[]{:S(2)}) collective-permute-start(bf16[1024,128]{1,0:T(8,128)(2,1)} %left_3_ref.1), channel_id=1, source_target_pairs={{0,8},{4,36},{8,16},{12,44},{16,24},{20,52},{24,0},{28,60},{32,40}... | collective-permute-start | bytes 786440 | tf_op jit(solution)/shard_map/ppermute | solution.py:495
  13.0 10.9 %copy-start.13 = (bf16[512,128]{1,0:T(8,128)(2,1)S(1)}, bf16[512,128]{1,0:T(8,128)(2,1)}, u32[]{:S(2)}) copy-start(bf16[512,128]{1,0:T(8,128)(2,1)} %refs_7_.1) | copy-start | bytes 393220
  13.0 10.9 %copy-start.14 = (bf16[512,128]{1,0:T(8,128)(2,1)S(1)}, bf16[512,128]{1,0:T(8,128)(2,1)}, u32[]{:S(2)}) copy-start(bf16[512,128]{1,0:T(8,128)(2,1)} %refs_5_.1) | copy-start | bytes 393220
  13.1 10.9 %copy-start.15 = (bf16[512,128]{1,0:T(8,128)(2,1)S(1)}, bf16[512,128]{1,0:T(8,128)(2,1)}, u32[]{:S(2)}) copy-start(bf16[512,128]{1,0:T(8,128)(2,1)} %refs_6_.1) | copy-start | bytes 393220
  13.1 37.5 %all-to-all-start = ((bf16[32,144,128]{2,1,0:T(8,128)(2,1)}), bf16[32,144,128]{2,1,0:T(8,128)(2,1)}, u32[]{:S(2)}, u32[]{:S(2)}) async-start(bf16[32,144,128]{2,1,0:T(8,128)(2,1)} %get-tuple-element.49), calls=%async_computation | async-start | bytes 2359296 | tf_op jit(solution)/shard_map/all_to_all | solution.py:538
  21.0 25.6 %collective-permute-start.4 = (bf16[4096,128]{1,0:T(8,128)(2,1)}, bf16[4096,128]{1,0:T(8,128)(2,1)}, u32[]{:S(2)}, u32[]{:S(2)}) collective-permute-start(bf16[4096,128]{1,0:T(8,128)(2,1)} %pad_maximum_fusion), channel_id=1, source_target_pairs={{0,96},{4,28},{8,104},{12,4},{16,112},{20,12},{24,120},{28,20},{32... | collective-permute-start | bytes 3145736 | tf_op jit(solution)/shard_map/ppermute | solution.py:495
  24.0 26.6 %collective-permute-start.3 = (bf16[4096,128]{1,0:T(8,128)(2,1)}, bf16[4096,128]{1,0:T(8,128)(2,1)}, u32[]{:S(2)}, u32[]{:S(2)}) collective-permute-start(bf16[4096,128]{1,0:T(8,128)(2,1)} %pad_maximum_fusion), channel_id=1, source_target_pairs={{0,32},{4,12},{8,40},{12,20},{16,48},{20,28},{24,56},{28,4},{32,64... | collective-permute-start | bytes 3145736 | tf_op jit(solution)/shard_map/ppermute | solution.py:495
  24.0 33.8 %collective-permute-start.12 = (bf16[4096,128]{1,0:T(8,128)(2,1)}, bf16[4096,128]{1,0:T(8,128)(2,1)}, u32[]{:S(2)}, u32[]{:S(2)}) collective-permute-start(bf16[4096,128]{1,0:T(8,128)(2,1)} %pad_maximum_fusion), channel_id=1, source_target_pairs={{0,4},{4,0},{8,12},{12,8},{16,20},{20,16},{24,28},{28,24},{32,36},... | collective-permute-start | bytes 3145736 | tf_op jit(solution)/shard_map/ppermute | solution.py:490
  24.7 30.6 %collective-permute-start.6 = (bf16[384,128]{1,0:T(8,128)(2,1)S(1)}, bf16[384,128]{1,0:T(8,128)(2,1)S(1)}, u32[]{:S(2)}, u32[]{:S(2)}) collective-permute-start(bf16[384,128]{1,0:T(8,128)(2,1)S(1)} %bitcast.55), channel_id=1, source_target_pairs={{0,2},{1,3},{2,0},{3,1},{4,6},{5,7},{6,4},{7,5},{8,10},{9,11},{10,... | collective-permute-start | bytes 294920 | tf_op jit(solution)/shard_map/ppermute | solution.py:522
  28.6 28.3 %collective-permute-start.7 = (bf16[384,128]{1,0:T(8,128)(2,1)}, bf16[384,128]{1,0:T(8,128)(2,1)S(1)}, u32[]{:S(2)}, u32[]{:S(2)}) collective-permute-start(bf16[384,128]{1,0:T(8,128)(2,1)} %bitcast.14), channel_id=1, source_target_pairs={{0,1},{1,2},{2,3},{3,0},{4,5},{5,6},{6,7},{7,4},{8,9},{9,10},{10,1... | collective-permute-start | bytes 294920 | tf_op jit(solution)/shard_map/ppermute | solution.py:522
  46.6 10.5 %collective-permute-start.5 = (bf16[384,128]{1,0:T(8,128)(2,1)S(1)}, bf16[384,128]{1,0:T(8,128)(2,1)S(1)}, u32[]{:S(2)}, u32[]{:S(2)}) collective-permute-start(bf16[384,128]{1,0:T(8,128)(2,1)S(1)} %bitcast.54), channel_id=1, source_target_pairs={{0,3},{1,0},{2,1},{3,2},{4,7},{5,4},{6,5},{7,6},{8,11},{9,8},{10,9... | collective-permute-start | bytes 294920 | tf_op jit(solution)/shard_map/ppermute | solution.py:522
  51.7 9.2 %collective-permute-start.11 = (bf16[2048,128]{1,0:T(8,128)(2,1)S(1)}, bf16[2048,128]{1,0:T(8,128)(2,1)S(1)}, u32[]{:S(2)}, u32[]{:S(2)}) collective-permute-start(bf16[2048,128]{1,0:T(8,128)(2,1)S(1)} %slice.45), channel_id=1, source_target_pairs={{0,96},{4,28},{8,104},{12,4},{16,112},{20,12},{24,120},{28,20},{32... | collective-permute-start | bytes 1572872 | tf_op jit(solution)/shard_map/ppermute | solution.py:495
  55.4 21.5 %copy-start.20 = (bf16[384,128]{1,0:T(8,128)(2,1)}, bf16[384,128]{1,0:T(8,128)(2,1)S(1)}, u32[]{:S(2)}) copy-start(bf16[384,128]{1,0:T(8,128)(2,1)S(1)} %collective-permute-done.6.refs_7_) | copy-start | bytes 294916
  55.4 15.4 %collective-permute-start.9 = (bf16[16,144,128]{2,1,0:T(8,128)(2,1)S(1)}, bf16[16,144,128]{2,1,0:T(8,128)(2,1)S(1)}, u32[]{:S(2)}, u32[]{:S(2)}) collective-permute-start(bf16[16,144,128]{2,1,0:T(8,128)(2,1)S(1)} %get-tuple-element.91), channel_id=1, source_target_pairs={{0,3},{1,2},{2,1},{3,0},{4,7},{5,6},{6,5},{7,4},{8,11},{9,10},{10,... | collective-permute-start | bytes 1769480 | tf_op jit(solution)/shard_map/ppermute | solution.py:543
  56.9 19.9 %copy-start.21 = (bf16[384,128]{1,0:T(8,128)(2,1)}, bf16[384,128]{1,0:T(8,128)(2,1)S(1)}, u32[]{:S(2)}) copy-start(bf16[384,128]{1,0:T(8,128)(2,1)S(1)} %collective-permute-done.7.refs_8_) | copy-start | bytes 294916
  57.0 18.3 %collective-permute-start.13 = (bf16[4096,128]{1,0:T(8,128)(2,1)}, bf16[4096,128]{1,0:T(8,128)(2,1)}, u32[]{:S(2)}, u32[]{:S(2)}) collective-permute-start(bf16[4096,128]{1,0:T(8,128)(2,1)} %collective-permute-done.3), channel_id=1, source_target_pairs={{0,4},{4,0},{8,12},{12,8},{16,20},{20,16},{24,28},{28,24},{32,36},... | collective-permute-start | bytes 3145736 | tf_op jit(solution)/shard_map/ppermute | solution.py:490
  57.1 19.8 %copy-start.22 = (bf16[384,128]{1,0:T(8,128)(2,1)}, bf16[384,128]{1,0:T(8,128)(2,1)S(1)}, u32[]{:S(2)}) copy-start(bf16[384,128]{1,0:T(8,128)(2,1)S(1)} %collective-permute-done.5.refs_6_) | copy-start | bytes 294916
  57.1 10.5 %collective-permute-start.10 = (bf16[2048,128]{1,0:T(8,128)(2,1)S(1)}, bf16[2048,128]{1,0:T(8,128)(2,1)S(1)}, u32[]{:S(2)}, u32[]{:S(2)}) collective-permute-start(bf16[2048,128]{1,0:T(8,128)(2,1)S(1)} %slice.44), channel_id=1, source_target_pairs={{0,32},{4,12},{8,40},{12,20},{16,48},{20,28},{24,56},{28,4},{32,64... | collective-permute-start | bytes 1572872 | tf_op jit(solution)/shard_map/ppermute | solution.py:495
  57.8 17.5 %collective-permute-start.16 = (bf16[4096,128]{1,0:T(8,128)(2,1)}, bf16[4096,128]{1,0:T(8,128)(2,1)}, u32[]{:S(2)}, u32[]{:S(2)}) collective-permute-start(bf16[4096,128]{1,0:T(8,128)(2,1)} %collective-permute-done.4), channel_id=1, source_target_pairs={{0,4},{4,0},{8,12},{12,8},{16,20},{20,16},{24,28},{28,24},{32,36},... | collective-permute-start | bytes 3145736 | tf_op jit(solution)/shard_map/ppermute | solution.py:490
  60.9 14.3 %copy-start.9 = (bf16[2048,128]{1,0:T(8,128)(2,1)}, bf16[2048,128]{1,0:T(8,128)(2,1)S(1)}, u32[]{:S(2)}) copy-start(bf16[2048,128]{1,0:T(8,128)(2,1)S(1)} %collective-permute-done.11) | copy-start | bytes 1572868
  60.9 14.3 %collective-permute-start.8 = (bf16[16,144,128]{2,1,0:T(8,128)(2,1)S(1)}, bf16[16,144,128]{2,1,0:T(8,128)(2,1)}, u32[]{:S(2)}, u32[]{:S(2)}) collective-permute-start(bf16[16,144,128]{2,1,0:T(8,128)(2,1)S(1)} %get-tuple-element.92), channel_id=1, source_target_pairs={{0,1},{1,0},{2,3},{3,2},{4,5},{5,4},{6,7},{7,6},{8,9},{9,8},{10,11... | collective-permute-start | bytes 1769480 | tf_op jit(solution)/shard_map/ppermute | solution.py:542
  67.5 7.7 %copy-start.10 = (bf16[2048,128]{1,0:T(8,128)(2,1)}, bf16[2048,128]{1,0:T(8,128)(2,1)S(1)}, u32[]{:S(2)}) copy-start(bf16[2048,128]{1,0:T(8,128)(2,1)S(1)} %collective-permute-done.10) | copy-start | bytes 1572868
  67.5 7.7 %collective-permute-start.15 = (bf16[2048,128]{1,0:T(8,128)(2,1)S(1)}, bf16[2048,128]{1,0:T(8,128)(2,1)S(1)}, u32[]{:S(2)}, u32[]{:S(2)}) collective-permute-start(bf16[2048,128]{1,0:T(8,128)(2,1)S(1)} %collective-permute-done.11), channel_id=1, source_target_pairs={{0,4},{4,0},{8,12},{12,8},{16,20},{20,16},{24,28},{28,24},{32,36},... | collective-permute-start | bytes 1572872 | tf_op jit(solution)/shard_map/ppermute | solution.py:490
  70.7 4.6 %collective-permute-start.14 = (bf16[2048,128]{1,0:T(8,128)(2,1)S(1)}, bf16[2048,128]{1,0:T(8,128)(2,1)S(1)}, u32[]{:S(2)}, u32[]{:S(2)}) collective-permute-start(bf16[2048,128]{1,0:T(8,128)(2,1)S(1)} %collective-permute-done.10), channel_id=1, source_target_pairs={{0,4},{4,0},{8,12},{12,8},{16,20},{20,16},{24,28},{28,24},{32,36},... | collective-permute-start | bytes 1572872 | tf_op jit(solution)/shard_map/ppermute | solution.py:490
  89.9 17.8 %copy-start.19 = (bf16[1024,128]{1,0:T(8,128)(2,1)S(1)}, bf16[1024,128]{1,0:T(8,128)(2,1)}, u32[]{:S(2)}) copy-start(bf16[1024,128]{1,0:T(8,128)(2,1)} %param.13) | copy-start | bytes 786436
  89.9 23.3 %copy-start.5 = (bf16[1024,1024]{1,0:T(8,128)(2,1)S(1)}, bf16[1024,1024]{1,0:T(8,128)(2,1)}, u32[]{:S(2)}) copy-start(bf16[1024,1024]{1,0:T(8,128)(2,1)} %get-tuple-element.75) | copy-start | bytes 6291460
  89.9 7.4 %collective-permute-start.17 = (bf16[512,128]{1,0:T(8,128)(2,1)}, bf16[512,128]{1,0:T(8,128)(2,1)S(1)}, u32[]{:S(2)}, u32[]{:S(2)}) collective-permute-start(bf16[512,128]{1,0:T(8,128)(2,1)} %get-tuple-element.69), channel_id=1, source_target_pairs={{0,1},{1,2},{2,3},{3,0},{4,5},{5,6},{6,7},{7,4},{8,9},{9,10},{10,1... | collective-permute-start | bytes 393224 | tf_op jit(solution)/shard_map/ppermute | solution.py:522
  90.3 13.8 %collective-permute-start.19 = (bf16[512,128]{1,0:T(8,128)(2,1)}, bf16[512,128]{1,0:T(8,128)(2,1)S(1)}, u32[]{:S(2)}, u32[]{:S(2)}) collective-permute-start(bf16[512,128]{1,0:T(8,128)(2,1)} %get-tuple-element.70), channel_id=1, source_target_pairs={{0,3},{1,0},{2,1},{3,2},{4,7},{5,4},{6,5},{7,6},{8,11},{9,8},{10,9... | collective-permute-start | bytes 393224 | tf_op jit(solution)/shard_map/ppermute | solution.py:522
  93.2 10.9 %collective-permute-start.20 = (bf16[512,128]{1,0:T(8,128)(2,1)}, bf16[512,128]{1,0:T(8,128)(2,1)S(1)}, u32[]{:S(2)}, u32[]{:S(2)}) collective-permute-start(bf16[512,128]{1,0:T(8,128)(2,1)} %get-tuple-element.71), channel_id=1, source_target_pairs={{0,1},{1,2},{2,3},{3,0},{4,5},{5,6},{6,7},{7,4},{8,9},{9,10},{10,1... | collective-permute-start | bytes 393224 | tf_op jit(solution)/shard_map/ppermute | solution.py:522
  93.2 6.1 %collective-permute-start.21 = (bf16[512,128]{1,0:T(8,128)(2,1)}, bf16[512,128]{1,0:T(8,128)(2,1)S(1)}, u32[]{:S(2)}, u32[]{:S(2)}) collective-permute-start(bf16[512,128]{1,0:T(8,128)(2,1)} %get-tuple-element.73), channel_id=1, source_target_pairs={{0,3},{1,0},{2,1},{3,2},{4,7},{5,4},{6,5},{7,6},{8,11},{9,8},{10,9... | collective-permute-start | bytes 393224 | tf_op jit(solution)/shard_map/ppermute | solution.py:522
  98.3 6.2 %collective-permute-start.18 = (bf16[512,128]{1,0:T(8,128)(2,1)S(1)}, bf16[512,128]{1,0:T(8,128)(2,1)S(1)}, u32[]{:S(2)}, u32[]{:S(2)}) collective-permute-start(bf16[512,128]{1,0:T(8,128)(2,1)S(1)} %add_convert_fusion.5), channel_id=1, source_target_pairs={{0,1},{1,2},{2,3},{3,0},{4,5},{5,6},{6,7},{7,4},{8,9},{9,10},{10,1... | collective-permute-start | bytes 393224 | tf_op jit(solution)/shard_map/ppermute | solution.py:522
  100.3 6.3 %collective-permute-start.22 = (bf16[512,128]{1,0:T(8,128)(2,1)S(1)}, bf16[512,128]{1,0:T(8,128)(2,1)S(1)}, u32[]{:S(2)}, u32[]{:S(2)}) collective-permute-start(bf16[512,128]{1,0:T(8,128)(2,1)S(1)} %add_convert_fusion.4), channel_id=1, source_target_pairs={{0,3},{1,0},{2,1},{3,2},{4,7},{5,4},{6,5},{7,6},{8,11},{9,8},{10,9... | collective-permute-start | bytes 393224 | tf_op jit(solution)/shard_map/ppermute | solution.py:522
  108.7 39.6 %copy-start = (bf16[1024,128]{1,0:T(8,128)(2,1)}, bf16[1024,128]{1,0:T(8,128)(2,1)S(1)}, u32[]{:S(2)}) copy-start(bf16[1024,128]{1,0:T(8,128)(2,1)S(1)} %get-tuple-element.95.refs_4_.z0_ref) | copy-start | bytes 786436
  108.7 9.3 %collective-permute-start.25 = (bf16[1024,128]{1,0:T(8,128)(2,1)S(1)}, bf16[1024,128]{1,0:T(8,128)(2,1)S(1)}, u32[]{:S(2)}, u32[]{:S(2)}) collective-permute-start(bf16[1024,128]{1,0:T(8,128)(2,1)S(1)} %get-tuple-element.95.refs_4_.z0_ref), channel_id=1, source_target_pairs={{0,24},{4,100},{8,0},{12,108},{16,8},{20,116},{24,16},{28,124},{32... | collective-permute-start | bytes 786440 | tf_op jit(solution)/shard_map/ppermute | solution.py:495
  111.3 8.0 %collective-permute-start.24 = (bf16[1024,128]{1,0:T(8,128)(2,1)S(1)}, bf16[1024,128]{1,0:T(8,128)(2,1)S(1)}, u32[]{:S(2)}, u32[]{:S(2)}) collective-permute-start(bf16[1024,128]{1,0:T(8,128)(2,1)S(1)} %get-tuple-element.95.refs_4_.z0_ref), channel_id=1, source_target_pairs={{0,16},{4,68},{8,24},{12,76},{16,0},{20,84},{24,8},{28,92},{32,48}... | collective-permute-start | bytes 786440 | tf_op jit(solution)/shard_map/ppermute | solution.py:495
  112.2 9.7 %collective-permute-start.23 = (bf16[1024,128]{1,0:T(8,128)(2,1)S(1)}, bf16[1024,128]{1,0:T(8,128)(2,1)S(1)}, u32[]{:S(2)}, u32[]{:S(2)}) collective-permute-start(bf16[1024,128]{1,0:T(8,128)(2,1)S(1)} %get-tuple-element.95.refs_4_.z0_ref), channel_id=1, source_target_pairs={{0,8},{4,36},{8,16},{12,44},{16,24},{20,52},{24,0},{28,60},{32,40}... | collective-permute-start | bytes 786440 | tf_op jit(solution)/shard_map/ppermute | solution.py:495
  116.3 32.1 %copy-start.2 = (bf16[1024,128]{1,0:T(8,128)(2,1)S(1)}, bf16[1024,128]{1,0:T(8,128)(2,1)}, u32[]{:S(2)}) copy-start(bf16[1024,128]{1,0:T(8,128)(2,1)} %left_3_ref.1) | copy-start | bytes 786436
  116.3 32.1 %copy-start.3 = (bf16[1024,128]{1,0:T(8,128)(2,1)S(1)}, bf16[1024,128]{1,0:T(8,128)(2,1)}, u32[]{:S(2)}) copy-start(bf16[1024,128]{1,0:T(8,128)(2,1)} %get-tuple-element.88.left_1_ref) | copy-start | bytes 786436
  116.3 32.1 %copy-start.4 = (bf16[1024,128]{1,0:T(8,128)(2,1)S(1)}, bf16[1024,128]{1,0:T(8,128)(2,1)}, u32[]{:S(2)}) copy-start(bf16[1024,128]{1,0:T(8,128)(2,1)} %get-tuple-element.89.left_2_ref) | copy-start | bytes 786436
  122.0 28.1 %copy-start.6 = (bf16[4096,128]{1,0:T(8,128)(2,1)}, bf16[4096,128]{1,0:T(8,128)(2,1)S(1)}, u32[]{:S(2)}) copy-start(bf16[4096,128]{1,0:T(8,128)(2,1)S(1)} %pad_maximum_fusion.1) | copy-start | bytes 3145732
  122.0 17.3 %collective-permute-start.27 = (bf16[4096,128]{1,0:T(8,128)(2,1)S(1)}, bf16[4096,128]{1,0:T(8,128)(2,1)S(1)}, u32[]{:S(2)}, u32[]{:S(2)}) collective-permute-start(bf16[4096,128]{1,0:T(8,128)(2,1)S(1)} %pad_maximum_fusion.1), channel_id=1, source_target_pairs={{0,96},{4,28},{8,104},{12,4},{16,112},{20,12},{24,120},{28,20},{32... | collective-permute-start | bytes 3145736 | tf_op jit(solution)/shard_map/ppermute | solution.py:495
  127.0 16.1 %collective-permute-start.26 = (bf16[4096,128]{1,0:T(8,128)(2,1)S(1)}, bf16[4096,128]{1,0:T(8,128)(2,1)}, u32[]{:S(2)}, u32[]{:S(2)}) collective-permute-start(bf16[4096,128]{1,0:T(8,128)(2,1)S(1)} %pad_maximum_fusion.1), channel_id=1, source_target_pairs={{0,32},{4,12},{8,40},{12,20},{16,48},{20,28},{24,56},{28,4},{32,64... | collective-permute-start | bytes 3145736 | tf_op jit(solution)/shard_map/ppermute | solution.py:495
  127.0 19.1 %collective-permute-start.43 = (bf16[1024,128]{1,0:T(8,128)(2,1)S(1)}, bf16[1024,128]{1,0:T(8,128)(2,1)S(1)}, u32[]{:S(2)}, u32[]{:S(2)}) collective-permute-start(bf16[1024,128]{1,0:T(8,128)(2,1)S(1)} %get-tuple-element.95.refs_4_.z0_ref), channel_id=1, source_target_pairs={{0,3},{1,0},{2,1},{3,2},{4,7},{5,4},{6,5},{7,6},{8,11},{9,8},{10,9... | collective-permute-start | bytes 786440 | tf_op jit(solution)/shard_map/ppermute | solution.py:522
  130.7 17.1 %collective-permute-start.42 = (bf16[1024,128]{1,0:T(8,128)(2,1)S(1)}, bf16[1024,128]{1,0:T(8,128)(2,1)S(1)}, u32[]{:S(2)}, u32[]{:S(2)}) collective-permute-start(bf16[1024,128]{1,0:T(8,128)(2,1)S(1)} %get-tuple-element.95.refs_4_.z0_ref), channel_id=1, source_target_pairs={{0,2},{1,3},{2,0},{3,1},{4,6},{5,7},{6,4},{7,5},{8,10},{9,11},{10,... | collective-permute-start | bytes 786440 | tf_op jit(solution)/shard_map/ppermute | solution.py:522
  130.7 17.1 %collective-permute-start.41 = (bf16[1024,128]{1,0:T(8,128)(2,1)S(1)}, bf16[1024,128]{1,0:T(8,128)(2,1)S(1)}, u32[]{:S(2)}, u32[]{:S(2)}) collective-permute-start(bf16[1024,128]{1,0:T(8,128)(2,1)S(1)} %get-tuple-element.95.refs_4_.z0_ref), channel_id=1, source_target_pairs={{0,1},{1,2},{2,3},{3,0},{4,5},{5,6},{6,7},{7,4},{8,9},{9,10},{10,1... | collective-permute-start | bytes 786440 | tf_op jit(solution)/shard_map/ppermute | solution.py:522
  139.3 10.8 %copy-start.8 = (bf16[4096,128]{1,0:T(8,128)(2,1)}, bf16[4096,128]{1,0:T(8,128)(2,1)S(1)}, u32[]{:S(2)}) copy-start(bf16[4096,128]{1,0:T(8,128)(2,1)S(1)} %collective-permute-done.27) | copy-start | bytes 3145732
  139.3 17.5 %collective-permute-start.30 = (bf16[4096,128]{1,0:T(8,128)(2,1)S(1)}, bf16[4096,128]{1,0:T(8,128)(2,1)}, u32[]{:S(2)}, u32[]{:S(2)}) collective-permute-start(bf16[4096,128]{1,0:T(8,128)(2,1)S(1)} %pad_maximum_fusion.1), channel_id=1, source_target_pairs={{0,4},{4,0},{8,12},{12,8},{16,20},{20,16},{24,28},{28,24},{32,36},... | collective-permute-start | bytes 3145736 | tf_op jit(solution)/shard_map/ppermute | solution.py:490
  145.8 9.6 %collective-permute-start.29 = (bf16[2048,128]{1,0:T(8,128)(2,1)}, bf16[2048,128]{1,0:T(8,128)(2,1)}, u32[]{:S(2)}, u32[]{:S(2)}) collective-permute-start(bf16[2048,128]{1,0:T(8,128)(2,1)} %slice.49), channel_id=1, source_target_pairs={{0,96},{4,28},{8,104},{12,4},{16,112},{20,12},{24,120},{28,20},{32... | collective-permute-start | bytes 1572872 | tf_op jit(solution)/shard_map/ppermute | solution.py:495
  146.1 10.7 %collective-permute-start.28 = (bf16[2048,128]{1,0:T(8,128)(2,1)}, bf16[2048,128]{1,0:T(8,128)(2,1)}, u32[]{:S(2)}, u32[]{:S(2)}) collective-permute-start(bf16[2048,128]{1,0:T(8,128)(2,1)} %slice.48), channel_id=1, source_target_pairs={{0,32},{4,12},{8,40},{12,20},{16,48},{20,28},{24,56},{28,4},{32,64... | collective-permute-start | bytes 1572872 | tf_op jit(solution)/shard_map/ppermute | solution.py:495
  147.8 11.1 %collective-permute-start.31 = (bf16[4096,128]{1,0:T(8,128)(2,1)}, bf16[4096,128]{1,0:T(8,128)(2,1)}, u32[]{:S(2)}, u32[]{:S(2)}) collective-permute-start(bf16[4096,128]{1,0:T(8,128)(2,1)} %collective-permute-done.26), channel_id=1, source_target_pairs={{0,4},{4,0},{8,12},{12,8},{16,20},{20,16},{24,28},{28,24},{32,36},... | collective-permute-start | bytes 3145736 | tf_op jit(solution)/shard_map/ppermute | solution.py:490
  147.8 11.1 %collective-permute-start.34 = (bf16[4096,128]{1,0:T(8,128)(2,1)S(1)}, bf16[4096,128]{1,0:T(8,128)(2,1)}, u32[]{:S(2)}, u32[]{:S(2)}) collective-permute-start(bf16[4096,128]{1,0:T(8,128)(2,1)S(1)} %collective-permute-done.27), channel_id=1, source_target_pairs={{0,4},{4,0},{8,12},{12,8},{16,20},{20,16},{24,28},{28,24},{32,36},... | collective-permute-start | bytes 3145736 | tf_op jit(solution)/shard_map/ppermute | solution.py:490
  150.1 21.9 %all-to-all-start.1 = ((f32[32,48,128]{2,1,0:T(8,128)}), f32[32,48,128]{2,1,0:T(8,128)S(1)}, u32[]{:S(2)}, u32[]{:S(2)}) async-start(f32[32,48,128]{2,1,0:T(8,128)} %slopes.1), calls=%async_computation.1 | async-start | bytes 1572864 | tf_op jit(solution)/shard_map/all_to_all | solution.py:570
  155.4 2.2 %collective-permute-start.33 = (bf16[2048,128]{1,0:T(8,128)(2,1)}, bf16[2048,128]{1,0:T(8,128)(2,1)S(1)}, u32[]{:S(2)}, u32[]{:S(2)}) collective-permute-start(bf16[2048,128]{1,0:T(8,128)(2,1)} %collective-permute-done.29), channel_id=1, source_target_pairs={{0,4},{4,0},{8,12},{12,8},{16,20},{20,16},{24,28},{28,24},{32,36},... | collective-permute-start | bytes 1572872 | tf_op jit(solution)/shard_map/ppermute | solution.py:490
  156.8 2.1 %collective-permute-start.32 = (bf16[2048,128]{1,0:T(8,128)(2,1)}, bf16[2048,128]{1,0:T(8,128)(2,1)S(1)}, u32[]{:S(2)}, u32[]{:S(2)}) collective-permute-start(bf16[2048,128]{1,0:T(8,128)(2,1)} %collective-permute-done.28), channel_id=1, source_target_pairs={{0,4},{4,0},{8,12},{12,8},{16,20},{20,16},{24,28},{28,24},{32,36},... | collective-permute-start | bytes 1572872 | tf_op jit(solution)/shard_map/ppermute | solution.py:490
  171.9 20.8 %copy-start.18 = (f32[1024,128]{1,0:T(8,128)S(1)}, f32[1024,128]{1,0:T(8,128)}, u32[]{:S(2)}) copy-start(f32[1024,128]{1,0:T(8,128)} %get-tuple-element.81) | copy-start | bytes 1572868
  171.9 8.3 %collective-permute-start.35 = (bf16[512,128]{1,0:T(8,128)(2,1)}, bf16[512,128]{1,0:T(8,128)(2,1)S(1)}, u32[]{:S(2)}, u32[]{:S(2)}) collective-permute-start(bf16[512,128]{1,0:T(8,128)(2,1)} %get-tuple-element.83), channel_id=1, source_target_pairs={{0,1},{1,2},{2,3},{3,0},{4,5},{5,6},{6,7},{7,4},{8,9},{9,10},{10,1... | collective-permute-start | bytes 393224 | tf_op jit(solution)/shard_map/ppermute | solution.py:522
  172.0 9.2 %collective-permute-start.37 = (bf16[512,128]{1,0:T(8,128)(2,1)}, bf16[512,128]{1,0:T(8,128)(2,1)S(1)}, u32[]{:S(2)}, u32[]{:S(2)}) collective-permute-start(bf16[512,128]{1,0:T(8,128)(2,1)} %get-tuple-element.84), channel_id=1, source_target_pairs={{0,3},{1,0},{2,1},{3,2},{4,7},{5,4},{6,5},{7,6},{8,11},{9,8},{10,9... | collective-permute-start | bytes 393224 | tf_op jit(solution)/shard_map/ppermute | solution.py:522
  175.9 7.3 %collective-permute-start.38 = (bf16[512,128]{1,0:T(8,128)(2,1)}, bf16[512,128]{1,0:T(8,128)(2,1)S(1)}, u32[]{:S(2)}, u32[]{:S(2)}) collective-permute-start(bf16[512,128]{1,0:T(8,128)(2,1)} %get-tuple-element.85), channel_id=1, source_target_pairs={{0,1},{1,2},{2,3},{3,0},{4,5},{5,6},{6,7},{7,4},{8,9},{9,10},{10,1... | collective-permute-start | bytes 393224 | tf_op jit(solution)/shard_map/ppermute | solution.py:522
  175.9 8.0 %collective-permute-start.39 = (bf16[512,128]{1,0:T(8,128)(2,1)}, bf16[512,128]{1,0:T(8,128)(2,1)S(1)}, u32[]{:S(2)}, u32[]{:S(2)}) collective-permute-start(bf16[512,128]{1,0:T(8,128)(2,1)} %get-tuple-element.87), channel_id=1, source_target_pairs={{0,3},{1,0},{2,1},{3,2},{4,7},{5,4},{6,5},{7,6},{8,11},{9,8},{10,9... | collective-permute-start | bytes 393224 | tf_op jit(solution)/shard_map/ppermute | solution.py:522
  181.1 9.6 %collective-permute-start.36 = (bf16[512,128]{1,0:T(8,128)(2,1)S(1)}, bf16[512,128]{1,0:T(8,128)(2,1)S(1)}, u32[]{:S(2)}, u32[]{:S(2)}) collective-permute-start(bf16[512,128]{1,0:T(8,128)(2,1)S(1)} %add_convert_fusion.3), channel_id=1, source_target_pairs={{0,1},{1,2},{2,3},{3,0},{4,5},{5,6},{6,7},{7,4},{8,9},{9,10},{10,1... | collective-permute-start | bytes 393224 | tf_op jit(solution)/shard_map/ppermute | solution.py:522
  183.2 7.0 %collective-permute-start.44 = (f32[48,128]{1,0:T(8,128)S(1)}, f32[48,128]{1,0:T(8,128)S(1)}, u32[]{:S(2)}, u32[]{:S(2)}) collective-permute-start(f32[48,128]{1,0:T(8,128)S(1)} %reduce_sum.9), channel_id=1, source_target_pairs={{0,0},{1,33},{2,66},{3,99},{4,4},{5,37},{6,70},{7,103},{8,8},{9,41... | collective-permute-start | bytes 73736 | tf_op jit(solution)/shard_map/ppermute | solution.py:583
  184.9 7.8 %collective-permute-start.40 = (bf16[512,128]{1,0:T(8,128)(2,1)S(1)}, bf16[512,128]{1,0:T(8,128)(2,1)S(1)}, u32[]{:S(2)}, u32[]{:S(2)}) collective-permute-start(bf16[512,128]{1,0:T(8,128)(2,1)S(1)} %add_convert_fusion.1), channel_id=1, source_target_pairs={{0,3},{1,0},{2,1},{3,2},{4,7},{5,4},{6,5},{7,6},{8,11},{9,8},{10,9... | collective-permute-start | bytes 393224 | tf_op jit(solution)/shard_map/ppermute | solution.py:522
  (6 other events, 16.8 us)
